TPU v7x, 32 devices: a whole 2x2x4 slice. The times are simulated.
32 devices in a mesh: lat: 8 (over z, y), lon: 4 (over x, core).
Axes of the slice: x: 2, y: 2, z: 4, core: 2. Of those that a mesh axis runs over, the one named last changes fastest.
Arguments:
- spec: float32 [4, 2, 640, 1344], P(None, None, 'lat', 'lon'), may hold values from -6 to 6
- legendre: bfloat16 [640, 1344, 1280], P('lat', 'lon'), may hold values from -0.25 to 0.25
- wave_pairs: int32 [640], replicated, may hold values from 0 to 639, each once
- row_waves: int32 [2560], P('lat'), may hold values from 16 to 1280, as said below
- forcing: float32 [4, 2560, 5120], P(None, 'lat', 'lon'), may hold values from -6 to 6
- helm_coef: float32 [4], replicated, may hold values from 6.1035155e-07 to 4.8828124e-06
Outputs:
- grid_field: float32 [4, 2560, 5120], P(None, 'lat', 'lon')
- spec_new: float32 [4, 2, 640, 1344], P(None, None, 'lat', 'lon')
Inputs may be any that keep to these rules, and one draw needn't show every extreme that they name: Each value appears once; row s holds the wavenumbers wave_pairs[s] and 1279 - wave_pairs[s]. `row_waves`: rows near the equator resolve all 1280 wavenumbers.
All inputs are finite; a program needn't handle non-finite values.
Results may differ from a plain program's by a relative error of at most 0.028.
Values may be sent and summed in bfloat16 or wider, within the bound.
No kernel may reach another device: no remote copies, remote signals or barrier semaphores. Data moves between devices by JAX's collectives and lax.ppermute only.
A program may use at most 192 MiB of HBM per device.

v0:
```python
import math

import jax
import jax.numpy as jnp
from jax import lax
from jax.experimental import pallas as pl
from jax.experimental.pallas import tpu as pltpu
from jax.sharding import PartitionSpec as P

M = 1280
LANES = 128
HALF = LANES // 2
STEP = 16
VMEM_BYTES = 50 * 1024 * 1024
F32 = jnp.float32
BF16 = jnp.bfloat16


def column_info(pair_values, columns):
    boundary = M - pair_values[:, None]
    first_part = columns[None, :] < boundary
    valid_cols = columns[None, :] < M + 1
    second_part = jnp.logical_and(valid_cols, jnp.logical_not(first_part))
    offset = jnp.where(first_part, columns[None, :], columns[None, :] - boundary)
    parity = (1 - 2 * (offset % 2)).astype(jnp.float32)
    degree = jnp.where(first_part, pair_values[:, None] + columns[None, :], columns[None, :] - 1)
    return (
        first_part.astype(jnp.float32),
        second_part.astype(jnp.float32),
        parity,
        degree.astype(jnp.float32),
    )


def wave_numbers(pair_values):
    return jnp.stack([pair_values, M - 1 - pair_values], axis=-1)


def angles(wave_table, positions, length):
    winding = wave_table[..., None] * positions % length
    return winding.astype(jnp.float32) * (2.0 * math.pi / length)


def plain_body(spec, legendre, wave_pairs, row_waves, forcing, helm_coef):
    groups = lax.axis_size("lat")
    lat_id = lax.axis_index("lat")
    lon_id = lax.axis_index("lon")
    fields, _, slot_count, col_width = spec.shape
    half_lats = legendre.shape[2]
    lats_total = 2 * half_lats
    band_rows = row_waves.shape[0]
    seg_width = forcing.shape[2]
    lons_total = seg_width * lax.axis_size("lon")
    my_pairs = lax.dynamic_slice_in_dim(wave_pairs, lat_id * slot_count, slot_count)
    columns = lon_id * col_width + jnp.arange(col_width, dtype=jnp.int32)
    first_part, second_part, parity, degree = column_info(my_pairs, columns)
    selector = jnp.stack([first_part, second_part])
    flip_signs = jnp.stack([jnp.ones_like(parity), parity])
    factor = (selector[:, None] * flip_signs[None]).astype(jnp.bfloat16)
    mixed_terms = factor[:, :, None, None] * spec.astype(jnp.bfloat16)[None, None]
    upward = jnp.einsum(
        "qhfrsc,sck->hkfrsq", mixed_terms, legendre, preferred_element_type=jnp.float32
    ) * (0.5 / math.sqrt(M))
    lat_rows = jnp.concatenate([upward[0], jnp.flip(upward[1], axis=0)], axis=0)
    partial_value = lat_rows.reshape(lats_total, -1).astype(jnp.bfloat16)
    wave_table = wave_numbers(wave_pairs).reshape(groups, slot_count * 2)
    kept_mask = (wave_table[None, :, None, None, :] < row_waves[:, None, None, None, None]).astype(
        jnp.float32
    )
    shares = lax.psum_scatter(
        partial_value.astype(jnp.float32).astype(jnp.bfloat16),
        "lon",
        scatter_dimension=1,
        tiled=True,
    )
    banded = lax.all_to_all(shares, "lat", split_axis=0, concat_axis=1, tiled=True)
    whole = lax.all_gather(banded.reshape(band_rows, groups, -1), "lon", axis=2, tiled=True)
    fourier = whole.reshape(band_rows, groups, fields, 2, slot_count * 2) * kept_mask.astype(
        jnp.bfloat16
    )
    places = lon_id * seg_width + jnp.arange(seg_width, dtype=jnp.int32)
    phases = angles(wave_table, places, lons_total)
    weight = jnp.where(wave_table == 0, 1.0, 2.0).astype(jnp.float32)[..., None]
    forward_table = jnp.stack([weight * jnp.cos(phases), -weight * jnp.sin(phases)]).astype(
        jnp.bfloat16
    )
    grid_field = jnp.einsum(
        "lgfrn,rgnx->flx", fourier, forward_table, preferred_element_type=jnp.float32
    )
    tendency = (forcing - 0.5 * grid_field * grid_field).astype(jnp.bfloat16)
    back_table = (jnp.stack([jnp.cos(phases), -jnp.sin(phases)]) / lons_total).astype(jnp.bfloat16)
    pieces = jnp.einsum("flx,rgnx->lgfrn", tendency, back_table, preferred_element_type=jnp.float32)
    pieces = (pieces * kept_mask).astype(jnp.bfloat16)
    shares_back = lax.psum_scatter(
        pieces.reshape(band_rows, groups, -1).astype(jnp.float32).astype(jnp.bfloat16),
        "lon",
        scatter_dimension=2,
        tiled=True,
    )
    swapped = lax.all_to_all(shares_back, "lat", split_axis=1, concat_axis=0, tiled=True)
    fan_flat = lax.all_gather(swapped, "lon", axis=2, tiled=True).reshape(lats_total, -1)
    fan_rows = fan_flat.reshape(lats_total, fields, 2, slot_count, 2)
    mixed_back = jnp.stack([fan_rows[:half_lats], jnp.flip(fan_rows[half_lats:], axis=0)])
    downward = jnp.einsum(
        "hkfrsq,sck->frsqhc", mixed_back, legendre, preferred_element_type=jnp.float32
    )
    spectral_tendency = (
        first_part * (downward[:, :, :, 0, 0] + parity * downward[:, :, :, 0, 1])
        + second_part * (downward[:, :, :, 1, 0] + parity * downward[:, :, :, 1, 1])
    ) * math.sqrt(M)
    valid_cols = first_part + second_part
    divisor = 1.0 + helm_coef[:, None, None, None] * (degree * (degree + 1.0))[None, None]
    spec_new = valid_cols[None, None] * (spec + spectral_tendency) / divisor
    return (grid_field, spec_new)


def row_of(h, q, d, r):
    return ((h * 2 + q) * 4 + d) * 2 + r


def dot(a, b):
    return jnp.dot(a, b, preferred_element_type=F32)


def dot_nt(a, b):
    return lax.dot_general(a, b, (((1,), (1,)), ((), ())), preferred_element_type=F32)


def low_half():
    return lax.broadcasted_iota(jnp.int32, (STEP, LANES), 1) < HALF


def tile_groups(tiles, packed, groups):
    if packed:
        return [(n, 2 * n) for n in range(len(tiles))]
    return [(n, n) for n in range(len(tiles))]


def up_kernel(place, mix, *refs, tiles, packed, groups, scale):
    legs, (keep, send, scratch) = refs[: len(tiles)], refs[len(tiles) :]
    me = place[0]
    rows = mix.shape[1]
    for s in range(STEP):
        basis = jnp.concatenate([leg[s] for leg in legs], axis=1)
        found = dot(mix[s], basis) * scale
        for n in range(len(tiles)):
            scratch[n, s * rows : (s + 1) * rows, :] = found[:, n * LANES : (n + 1) * LANES]

    def fetch(h, q, d, r, n):
        return scratch[n, pl.ds(row_of(h, q, d, r), STEP, stride=rows), :]

    for h in range(2):
        for q in range(2):
            for d in range(4):
                target = (keep, send)[d % 2]
                for n, group in tile_groups(tiles, packed, groups):
                    slot = me ^ (groups - 1 - group if h else group)
                    if packed:
                        real, imag = fetch(h, q, d, 0, n), fetch(h, q, d, 1, n)
                        even = jnp.where(low_half(), real, pltpu.roll(imag, HALF, 1))
                        odd = jnp.where(low_half(), pltpu.roll(real, HALF, 1), imag)
                        target[d // 2, slot, q] = even.astype(BF16)
                        target[d // 2, slot ^ 1, q] = odd.astype(BF16)
                    else:
                        for r in range(2):
                            target[d // 2, slot, r, q] = fetch(h, q, d, r, n).astype(BF16)


def up_chunk(place, mix, legendre, tiles, packed, groups, scale):
    slots, rows, width = mix.shape
    lead = (2, groups, 2) if packed else (2, groups, 2, 2)
    out = jax.ShapeDtypeStruct(lead + (slots, LANES), BF16)
    out_spec = pl.BlockSpec(lead + (STEP, LANES), lambda i, p: (0,) * len(lead) + (i, 0))

    def leg_spec(tile):
        return pl.BlockSpec((STEP, width, LANES), lambda i, p: (i, 0, tile))

    return pl.pallas_call(
        lambda *refs: up_kernel(*refs, tiles=tiles, packed=packed, groups=groups, scale=scale),
        out_shape=(out, out),
        grid_spec=pltpu.PrefetchScalarGridSpec(
            num_scalar_prefetch=1,
            grid=(slots // STEP,),
            in_specs=[pl.BlockSpec((STEP, rows, width), lambda i, p: (i, 0, 0))]
            + [leg_spec(t) for t in tiles],
            out_specs=(out_spec, out_spec),
            scratch_shapes=[pltpu.VMEM((len(tiles), STEP * rows, LANES), F32)],
        ),
        compiler_params=pltpu.CompilerParams(vmem_limit_bytes=VMEM_BYTES),
        cost_estimate=pl.CostEstimate(
            flops=2 * slots * 256 * 2 * width * len(tiles) * LANES // 2,
            bytes_accessed=slots * width * len(tiles) * LANES * 2,
            transcendentals=0,
        ),
        name="legendre_up",
    )(place, mix, *[legendre] * len(tiles))


def down_kernel(place, *refs, tiles, packed, groups, first, last):
    fans, legs = refs[:4], refs[4 : 4 + len(tiles)]
    rest = list(refs[4 + len(tiles) :])
    factors = rest.pop(0)
    previous = None if first else rest.pop(0)
    spec, inverse = (rest.pop(0), rest.pop(0)) if last else (None, None)
    out, scratch, sums = rest
    me, mine = place[0], place[1]
    rows = 32

    def put(h, q, d, r, n, value):
        scratch[n, pl.ds(row_of(h, q, d, r), STEP, stride=rows), :] = value

    for h in range(2):
        for q in range(2):
            for d in range(4):
                for n, group in tile_groups(tiles, packed, groups):
                    slot = me ^ (groups - 1 - group if h else group)
                    if packed:
                        even = fans[d][slot, q].astype(F32)
                        odd = fans[d][slot ^ 1, q].astype(F32)
                        put(h, q, d, 0, n, jnp.where(low_half(), even, pltpu.roll(odd, HALF, 1)))
                        put(h, q, d, 1, n, jnp.where(low_half(), pltpu.roll(even, HALF, 1), odd))
                    else:
                        for r in range(2):
                            put(h, q, d, r, n, fans[d][slot, r, q].astype(F32))
    for s in range(STEP):
        basis = jnp.concatenate([leg[s] for leg in legs], axis=1)
        values = [scratch[n, s * rows : (s + 1) * rows, :] for n in range(len(tiles))]
        values = jnp.concatenate(values, axis=1).astype(BF16)
        found = dot_nt(values, basis)
        total = sum(found[8 * n : 8 * n + 8] * factors[s, n : n + 1, :] for n in range(4))
        for n in range(8):
            sums[n, s : s + 1, :] = total[n : n + 1]
    for d in range(4):
        field = mine ^ d
        for r in range(2):
            n = 2 * d + r
            total = sums[n]
            if not first:
                total = total + previous[field, r]
            if last:
                total = (spec[field, r] + total * math.sqrt(M)) * inverse[field]
            out[field, r] = total


def down_chunk(place, fans, legendre, factors, previous, spec, inverse, tiles, packed, groups):
    slots, _, width = factors.shape
    first, last = previous is None, spec is not None
    lead = (groups, 2) if packed else (groups, 2, 2)
    fan_spec = pl.BlockSpec(lead + (STEP, LANES), lambda i, p: (0,) * len(lead) + (i, 0))
    field_spec = pl.BlockSpec((4, 2, STEP, width), lambda i, p: (0, 0, i, 0))

    def leg_spec(tile):
        return pl.BlockSpec((STEP, width, LANES), lambda i, p: (i, 0, tile))

    operands = [*fans, *[legendre] * len(tiles), factors]
    specs = [fan_spec] * 4 + [leg_spec(t) for t in tiles]
    specs.append(pl.BlockSpec((STEP, 4, width), lambda i, p: (i, 0, 0)))
    if not first:
        operands.append(previous)
        specs.append(field_spec)
    if last:
        operands += [spec, inverse]
        specs += [field_spec, pl.BlockSpec((4, STEP, width), lambda i, p: (0, i, 0))]
    return pl.pallas_call(
        lambda *refs: down_kernel(
            *refs, tiles=tiles, packed=packed, groups=groups, first=first, last=last
        ),
        out_shape=jax.ShapeDtypeStruct((4, 2, slots, width), F32),
        grid_spec=pltpu.PrefetchScalarGridSpec(
            num_scalar_prefetch=1,
            grid=(slots // STEP,),
            in_specs=specs,
            out_specs=field_spec,
            scratch_shapes=[
                pltpu.VMEM((len(tiles), STEP * 32, LANES), F32),
                pltpu.VMEM((8, STEP, width), F32),
            ],
        ),
        compiler_params=pltpu.CompilerParams(vmem_limit_bytes=VMEM_BYTES),
        cost_estimate=pl.CostEstimate(
            flops=2 * slots * 256 * width * len(tiles) * LANES,
            bytes_accessed=slots * width * len(tiles) * LANES * 2,
            transcendentals=0,
        ),
        name="legendre_down",
    )(place, *operands)


def table_kernel(cos_far, sin_far, cos_near, sin_near, out):
    for n in range(cos_far.shape[1]):
        lanes = slice(n * LANES, (n + 1) * LANES)
        cos_a, sin_a = cos_far[:, n : n + 1], sin_far[:, n : n + 1]
        cos_b, sin_b = cos_near[...], sin_near[...]
        out[0, 0, :, lanes] = (cos_a * cos_b - sin_a * sin_b).astype(BF16)
        out[1, 0, :, lanes] = (-sin_a * cos_b - cos_a * sin_b).astype(BF16)


def make_table(waves, first_place, width, length, groups):
    far = angles(waves, first_place + LANES * jnp.arange(width // LANES, dtype=jnp.int32), length)
    near = angles(waves, jnp.arange(LANES, dtype=jnp.int32), length)
    count = waves.shape[0] // groups
    far_spec = pl.BlockSpec((count, width // LANES), lambda i: (i, 0))
    near_spec = pl.BlockSpec((count, LANES), lambda i: (i, 0))
    return pl.pallas_call(
        table_kernel,
        out_shape=jax.ShapeDtypeStruct((2, groups, count, width), BF16),
        grid=(groups,),
        in_specs=[far_spec, far_spec, near_spec, near_spec],
        out_specs=pl.BlockSpec((2, 1, count, width), lambda i: (0, i, 0, 0)),
        compiler_params=pltpu.CompilerParams(vmem_limit_bytes=VMEM_BYTES),
        name="zonal_table",
    )(jnp.cos(far), jnp.sin(far), jnp.cos(near), jnp.sin(near))


def zonal_kernel(place, *refs, packed, first, scale):
    coefs, rest = refs[:4], list(refs[4:])
    table, flip, spread, waves, row_waves, forcing = rest[:6]
    rest = rest[6:] if first else rest[7:]
    grid, keep, send, weight, lines, force, field, tend, read_sem, write_sem = rest
    mine, offset = place[1], pl.multiple_of(place[2], 8)
    parts, groups, per_group, width = table.shape
    count = groups * per_group
    rows = HALF if packed else LANES
    passes = ((1, 3, 0, 2),) if packed else ((1, 3), (0, 2))
    block = 256
    wave_block = groups // 2

    def force_copy(d):
        source = forcing.at[mine ^ d, pl.ds(offset, rows), :]
        return pltpu.make_async_copy(source, force.at[d], read_sem.at[d])

    def grid_copy(d):
        target = grid.at[mine ^ d, pl.ds(offset, rows), :]
        return pltpu.make_async_copy(field.at[d], target, write_sem.at[d])

    for d in range(4):
        force_copy(d).start()
    kept = waves[...] < row_waves[...]
    weight[...] = jnp.where(kept, jnp.where(waves[...] == 0, 1.0, 2.0), 0.0).astype(BF16)
    for fields in passes:
        for n, d in enumerate(fields):
            for r in range(2):
                if packed:
                    values = coefs[d][...].reshape(count, LANES) * weight[...]
                    turn = flip[r]
                else:
                    values = coefs[d][:, r].reshape(count, LANES) * weight[...]
                    turn = flip[...]
                lines[r, n * rows : (n + 1) * rows, :] = dot_nt(turn, values).astype(BF16)
        for d in fields:
            force_copy(d).wait()

        @pl.loop(0, width // block)
        def _(step):
            lanes = pl.ds(pl.multiple_of(step * block, block), block)
            total = dot(lines[0], table[0, :, :, lanes].reshape(count, block))
            total += dot(lines[1], table[1, :, :, lanes].reshape(count, block))
            for n, d in enumerate(fields):
                here = slice(n * rows, (n + 1) * rows)
                part = total[here]
                field[d, :, lanes] = part
                tend[here, lanes] = (force[d, :, lanes] - 0.5 * part * part).astype(BF16)

        for d in fields:
            grid_copy(d).start()

        @pl.loop(0, groups // wave_block)
        def _(step):
            several = pl.ds(step * wave_block, wave_block)
            some = wave_block * per_group
            mask = weight[pl.ds(pl.multiple_of(step * some, some), some), :].astype(F32) > 0
            found = []
            for r in range(2):
                sums = dot_nt(table[r, several].reshape(some, width), tend[...])
                found.append((sums * scale).astype(BF16))
            for n, d in enumerate(fields):
                target = (keep, send)[d % 2]
                if packed:
                    turned = dot(found[0], spread[n, 0]) + dot(found[1], spread[n, 1])
                    turned = jnp.where(mask, turned, 0.0).astype(BF16)
                    target[d // 2, several] = turned.reshape((wave_block,) + target.shape[2:])
                else:
                    for r in range(2):
                        turned = dot(found[r][:, n * rows : (n + 1) * rows], flip[...])
                        turned = jnp.where(mask, turned, 0.0).astype(BF16)
                        target[d // 2, several, r] = turned.reshape(
                            (wave_block,) + target.shape[3:]
                        )

    for d in range(4):
        grid_copy(d).wait()


def zonal_chunk(place, coefs, table, flip, spread, waves, row_waves, forcing, grid, packed, scale):
    parts, groups, per_group, width = table.shape
    count = groups * per_group
    rows = HALF if packed else LANES
    batch = 4 * rows if packed else 2 * rows
    first = grid is None
    sent = jax.ShapeDtypeStruct((2,) + coefs[0].shape, BF16)
    vmem, anywhere = pl.BlockSpec(memory_space=pltpu.VMEM), pl.BlockSpec(memory_space=pl.ANY)
    operands = [place, *coefs, table, flip, spread, waves, row_waves, forcing]
    specs = [pl.BlockSpec(memory_space=pltpu.SMEM)] + [vmem] * 9 + [anywhere]
    aliases = {}
    if not first:
        aliases = {len(operands): 0}
        operands.append(grid)
        specs.append(anywhere)
    return pl.pallas_call(
        lambda *refs: zonal_kernel(*refs, packed=packed, first=first, scale=scale),
        out_shape=(jax.ShapeDtypeStruct(forcing.shape, F32), sent, sent),
        in_specs=specs,
        out_specs=(anywhere, vmem, vmem),
        scratch_shapes=[
            pltpu.VMEM((count, LANES), BF16),
            pltpu.VMEM((2, batch, count), BF16),
            pltpu.VMEM((4, rows, width), F32),
            pltpu.VMEM((4, rows, width), F32),
            pltpu.VMEM((batch, width), BF16),
            pltpu.SemaphoreType.DMA((4,)),
            pltpu.SemaphoreType.DMA((4,)),
        ],
        input_output_aliases=aliases,
        compiler_params=pltpu.CompilerParams(vmem_limit_bytes=VMEM_BYTES),
        cost_estimate=pl.CostEstimate(
            flops=2 * 2 * 2 * 4 * rows * count * width,
            bytes_accessed=2 * 2 * count * width + 2 * 4 * 4 * rows * width,
            transcendentals=0,
        ),
        name="zonal",
    )(*operands)


def swap(value, axis, bit):
    pairs = [(n, n ^ bit) for n in range(lax.axis_size(axis))]
    return lax.ppermute(value, axis, pairs)


def add(*values):
    return sum(v.astype(F32) for v in values).astype(BF16)


def reduce_lon(keep, send):
    other = swap(send, "lon", 1)
    away = swap(add(keep[1], other[1]), "lon", 2)
    return add(keep[0], other[0], away)


def gather_lon(own):
    across = swap(own, "lon", 2)
    return own, swap(own, "lon", 1), across, swap(across, "lon", 1)


def exchange_lat(value, bits):
    value = value[:, None]
    for bit in bits:
        size = value.shape[0] // 2
        arrived = swap(value[size:], "lat", bit)
        value = jnp.stack([value[:size], arrived], axis=1)
        value = value.reshape((size, 2 * value.shape[2]) + value.shape[3:])
    return value[0]


def fast_plan(spec, legendre, row_waves, forcing):
    groups, lon_size = lax.axis_size("lat"), lax.axis_size("lon")
    fields, _, slots, _ = spec.shape
    half_lats, band, width = legendre.shape[2], row_waves.shape[0], forcing.shape[2]
    per_pair, odd = divmod(2 * band, LANES)
    if (groups, lon_size, fields) != (8, 4, 4) or odd or per_pair % 2 == 0:
        return None
    if slots % STEP or half_lats != 4 * band or width % 256 or 2 * slots % STEP:
        return None
    pairs = range(half_lats // (2 * band))
    full = [
        [t for p in pairs for t in (per_pair * p + n, per_pair * (p + 1) - 1 - n)]
        for n in range(per_pair // 2)
    ]
    return [per_pair * p + per_pair // 2 for p in pairs], full


def body(spec, legendre, wave_pairs, row_waves, forcing, helm_coef):
    plan = fast_plan(spec, legendre, row_waves, forcing)
    if plan is None:
        return plain_body(spec, legendre, wave_pairs, row_waves, forcing, helm_coef)
    shared_tiles, full_tiles = plan
    groups = lax.axis_size("lat")
    lat_id, lon_id = lax.axis_index("lat"), lax.axis_index("lon")
    fields, _, slots, col_width = spec.shape
    band, seg_width = row_waves.shape[0], forcing.shape[2]
    length = seg_width * lax.axis_size("lon")
    top = groups // 2
    bits = [1 << n for n in range(groups.bit_length() - 1)]

    my_pairs = lax.dynamic_slice_in_dim(wave_pairs, lat_id * slots, slots)
    columns = lon_id * col_width + jnp.arange(col_width, dtype=jnp.int32)
    first_part, second_part, parity, degree = column_info(my_pairs, columns)
    factors = jnp.stack(
        [first_part, second_part, parity * first_part, parity * second_part], axis=1
    )
    near = jnp.stack([lax.dynamic_index_in_dim(spec, lon_id ^ d, 0, False) for d in range(4)])
    near = jnp.transpose(near.astype(BF16), (2, 0, 1, 3)).reshape(slots, 1, 2 * fields, col_width)
    mix = (factors[:, :, None].astype(BF16) * near).reshape(slots, 8 * fields, col_width)
    divisor = 1.0 + helm_coef[:, None, None] * (degree * (degree + 1.0))[None]
    inverse = (first_part + second_part)[None] / divisor

    positions = [sum(((p >> n) & 1) << (len(bits) - 1 - n) for n in range(len(bits))) for p in range(groups)]
    grouped = wave_pairs.reshape(groups, slots)
    near_pairs = jnp.stack(
        [lax.dynamic_index_in_dim(grouped, lat_id ^ e, 0, False) for e in positions]
    )
    waves = jnp.stack([near_pairs, M - 1 - near_pairs], axis=1).reshape(-1)
    table = make_table(waves, lon_id * seg_width, seg_width, length, groups)

    south = lat_id >= top
    north = jnp.where(south, groups - 1 - lat_id, lat_id)
    row = jnp.arange(LANES, dtype=jnp.int32)
    place = jnp.stack([lat_id, lon_id])
    chunks = [(shared_tiles, True, 0)] + [(t, False, n) for n, t in enumerate(full_tiles)]
    setups = []
    for tiles, packed, n in chunks:
        rows = HALF if packed else LANES
        start = band - rows if packed else n * LANES
        start = jnp.where(north % 2 == 0, start, band - rows - start)
        start = jnp.where(south, band - rows - start, start)
        mirrored = jnp.where(south, rows - 1 - row[:rows], row[:rows])
        if packed:
            target = HALF * jnp.arange(2)[:, None] + mirrored[None]
            flip = target[..., None] == row
            spread = [
                jnp.concatenate([flip[r] if m == k else jnp.zeros_like(flip[r]) for m in range(4)])
                for k in range(4)
                for r in range(2)
            ]
            spread = jnp.stack(spread).reshape(4, 2, 4 * rows, LANES).astype(BF16)
        else:
            flip = mirrored[:, None] == row
            spread = jnp.zeros((8, LANES), BF16)
        kept = lax.dynamic_slice_in_dim(row_waves, start, rows)
        kept = jnp.sum(jnp.where(flip, kept[:, None], 0), axis=tuple(range(flip.ndim - 1)))
        spot = jnp.stack([lat_id, lon_id, start]).astype(jnp.int32)
        setups.append((spot, flip.astype(BF16), spread, kept[None].astype(jnp.int32)))

    scale = 0.5 / math.sqrt(M)
    grid_field, total = None, None
    sums = [up_chunk(place, mix, legendre, t, packed, groups, scale) for t, packed, _ in chunks]
    owns = [exchange_lat(reduce_lon(*s), bits[::-1]) for s in sums]
    fans = []
    for (tiles, packed, _), own, (spot, flip, spread, kept) in zip(chunks, owns, setups):
        coefs = gather_lon(own)
        grid_field, keep, send = zonal_chunk(
            spot, coefs, table, flip, spread, waves[:, None], kept, forcing, grid_field, packed, 1.0 / length
        )
        fans.append(gather_lon(exchange_lat(reduce_lon(keep, send), bits)))
    for n, (tiles, packed, _) in enumerate(chunks):
        last = n == len(chunks) - 1
        total = down_chunk(
            place, fans[n], legendre, factors, total, spec if last else None,
            inverse if last else None, tiles, packed, groups,
        )
    return grid_field, total


def solution(mesh):
    return jax.shard_map(
        body,
        mesh=mesh,
        in_specs=(
            P(None, None, "lat", "lon"),
            P("lat", "lon", None),
            P(),
            P("lat"),
            P(None, "lat", "lon"),
            P(),
        ),
        out_specs=(P(None, "lat", "lon"), P(None, None, "lat", "lon")),
        check_vma=False,
    )
```

profile of v0, /device:TPU:1, one launch (start us, length us, event | category | flops | bytes accessed | tf_op | source)
XLA Modules:
  0.0 343.1 jit_solution(3089818238283311269)
XLA Ops:
  1.3 1.3 broadcast_subtract_fusion.1
  3.7 1.4 dynamic-slice_convert_fusion.3
  6.4 9.6 %legendre_up.5 = (bf16[2,8,2,80,128]{4,3,2,1,0:T(8,128)(2,1)S(1)}, bf16[2,8,2,80,128]{4,3,2,1,0:T(8,128)(2,1)}) custom-call(s32[2]{0:T(128)S(1)} %pad_add_fusion.16.refs_0_, bf16[80,32,336]{2,1,0:T(8,128)(2,1)S(1)} %multiply_bitcast_fusion.refs_1_, bf16[80,336,1280]{2,1,0:T(8,128)(2,1)} %refs_8_.3, bf16[80,336,1280]{2,1,0:T(8,128)(2,1)} %refs_8_.3), custom_call_target="tpu_custom_call" | custom-call | flops 3523215360 | bytes 13762560 | tf_op jit(solution)/shard_map/legendre_up/pallas_call | solution.py:178
  16.0 15.2 %legendre_up.4 = (bf16[2,8,2,2,80,128]{5,4,3,2,1,0:T(8,128)(2,1)S(1)}, bf16[2,8,2,2,80,128]{5,4,3,2,1,0:T(8,128)(2,1)}) custom-call(s32[2]{0:T(128)S(1)} %pad_add_fusion.16.refs_0_, bf16[80,32,336]{2,1,0:T(8,128)(2,1)} %copy-done, bf16[80,336,1280]{2,1,0:T(8,128)(2,1)} %refs_8_.3, bf16[80,336,1280]{2,1,0:T(8,128)(2,1)} %refs_8_.3, ...), custom_call_target="tpu_custom_call" | custom-call | flops 7046430720 | bytes 27525120 | tf_op jit(solution)/shard_map/legendre_up/pallas_call | solution.py:178
  31.2 1.1 copy-done.8
  32.7 15.1 %legendre_up.3 = (bf16[2,8,2,2,80,128]{5,4,3,2,1,0:T(8,128)(2,1)S(1)}, bf16[2,8,2,2,80,128]{5,4,3,2,1,0:T(8,128)(2,1)}) custom-call(s32[2]{0:T(128)S(1)} %pad_add_fusion.16.refs_0_, bf16[80,32,336]{2,1,0:T(8,128)(2,1)} %copy-done, bf16[80,336,1280]{2,1,0:T(8,128)(2,1)} %refs_8_.3, bf16[80,336,1280]{2,1,0:T(8,128)(2,1)} %refs_8_.3, ...), custom_call_target="tpu_custom_call" | custom-call | flops 7046430720 | bytes 27525120 | tf_op jit(solution)/shard_map/legendre_up/pallas_call | solution.py:178
  47.8 1.1 copy-done.5
  50.1 3.1 multiply_sine_fusion
  53.2 1.1 fusion.24
  54.2 2.7 collective-permute-start.17
  57.0 2.7 fusion.18
  59.7 5.4 %collective-permute-done.17 = bf16[8,2,80,128]{3,2,1,0:T(8,128)(2,1)S(1)} collective-permute-done((bf16[8,2,80,128]{3,2,1,0:T(8,128)(2,1)S(1)}, bf16[8,2,80,128]{3,2,1,0:T(8,128)(2,1)S(1)}, u32[]{:S(2)}, u32[]{:S(2)}) %collective-permute-start.17) | collective-permute-done | bytes 327712 | tf_op jit(solution)/shard_map/ppermute | solution.py:436
  65.0 1.1 fusion.15
  66.2 2.4 collective-permute-start.18
  68.9 7.0 %collective-permute-done.18 = bf16[4,1,2,80,128]{4,3,2,0,1:T(8,128)(2,1)S(1)} collective-permute-done((bf16[4,1,2,80,128]{4,3,2,0,1:T(8,128)(2,1)S(1)}, bf16[4,1,2,80,128]{4,3,2,0,1:T(8,128)(2,1)S(1)}, u32[]{:S(2)}, u32[]{:S(2)}) %collective-permute-start.18) | collective-permute-done | bytes 163872 | tf_op jit(solution)/shard_map/ppermute | solution.py:436
  75.9 1.5 collective-permute-start.19
  77.4 2.4 fusion.11
  79.8 1.2 collective-permute-start.9
  81.1 1.3 collective-permute-start.20
  82.4 2.1 fusion.10
  85.4 1.9 convert_element_type.317
  87.3 1.1 copy-done.3
  88.3 7.3 %zonal_table.1.refs_5_ = bf16[2,8,160,1280]{3,2,1,0:T(8,128)(2,1)} custom-call(f32[1280,10]{1,0:T(8,128)S(1)} %copy-done.3, f32[1280,10]{1,0:T(8,128)S(1)} %get-tuple-element.70.sin_far, f32[1280,128]{1,0:T(8,128)S(1)} %get-tuple-element.87.cos_near, f32[1280,128]{1,0:T(8,128)S(1)} %get-tuple-element.86.sin_near), custom_call_target="tpu_custom_call" | custom-call | tf_op jit(solution)/shard_map/zonal_table/pallas_call | solution.py:304
  95.7 0.9 pad_maximum_fusion.16
  96.6 0.9 collective-permute-start.22
  97.6 1.6 fusion.2
  99.3 3.6 %collective-permute-start.10 = (bf16[4,1,2,2,80,128]{5,4,3,2,0,1:T(8,128)(2,1)S(1)}, bf16[4,1,2,2,80,128]{5,4,3,2,0,1:T(8,128)(2,1)S(1)}, u32[]{:S(2)}, u32[]{:S(2)}) collective-permute-start(bf16[4,1,2,2,80,128]{5,4,3,2,0,1:T(8,128)(2,1)S(1)} %get-tuple-element.68), channel_id=1, source_target_pairs={{0,16},{4,20},{8,24},{12,28},{16,0},{20,4},{24,8},{28,12},{1,17},{... | collective-permute-start | bytes 983048 | tf_op jit(solution)/shard_map/ppermute | solution.py:436
  102.9 6.8 %collective-permute-done.1 = bf16[8,2,2,80,128]{4,3,2,1,0:T(8,128)(2,1)} collective-permute-done((bf16[8,2,2,80,128]{4,3,2,1,0:T(8,128)(2,1)}, bf16[8,2,2,80,128]{4,3,2,1,0:T(8,128)(2,1)}, u32[]{:S(2)}, u32[]{:S(2)}) %collective-permute-start.1) | collective-permute-done | bytes 655392 | tf_op jit(solution)/shard_map/ppermute | solution.py:436
  109.6 1.5 fusion.3
  111.2 3.2 collective-permute-start.2
  114.5 3.2 collective-permute-start.21
  118.2 5.9 %collective-permute-done.10 = bf16[4,1,2,2,80,128]{5,4,3,2,0,1:T(8,128)(2,1)S(1)} collective-permute-done((bf16[4,1,2,2,80,128]{5,4,3,2,0,1:T(8,128)(2,1)S(1)}, bf16[4,1,2,2,80,128]{5,4,3,2,0,1:T(8,128)(2,1)S(1)}, u32[]{:S(2)}, u32[]{:S(2)}) %collective-permute-start.10) | collective-permute-done | bytes 327712 | tf_op jit(solution)/shard_map/ppermute | solution.py:436
  124.2 1.4 collective-permute-start.11
  125.6 5.6 %collective-permute-done.2 = bf16[4,1,2,2,80,128]{5,4,3,2,0,1:T(8,128)(2,1)S(1)} collective-permute-done((bf16[4,1,2,2,80,128]{5,4,3,2,0,1:T(8,128)(2,1)S(1)}, bf16[4,1,2,2,80,128]{5,4,3,2,0,1:T(8,128)(2,1)S(1)}, u32[]{:S(2)}, u32[]{:S(2)}) %collective-permute-start.2) | collective-permute-done | bytes 327712 | tf_op jit(solution)/shard_map/ppermute | solution.py:436
  131.3 1.4 collective-permute-start.3
  132.7 6.4 %collective-permute-done.11 = bf16[2,2,2,2,80,128]{5,4,3,2,0,1:T(8,128)(2,1)S(1)} collective-permute-done((bf16[2,2,2,2,80,128]{5,4,3,2,0,1:T(8,128)(2,1)S(1)}, bf16[2,2,2,2,80,128]{5,4,3,2,0,1:T(8,128)(2,1)S(1)}, u32[]{:S(2)}, u32[]{:S(2)}) %collective-permute-start.11) | collective-permute-done | bytes 327712 | tf_op jit(solution)/shard_map/ppermute | solution.py:436
  139.5 6.6 %collective-permute-done.3 = bf16[2,2,2,2,80,128]{5,4,3,2,0,1:T(8,128)(2,1)S(1)} collective-permute-done((bf16[2,2,2,2,80,128]{5,4,3,2,0,1:T(8,128)(2,1)S(1)}, bf16[2,2,2,2,80,128]{5,4,3,2,0,1:T(8,128)(2,1)S(1)}, u32[]{:S(2)}, u32[]{:S(2)}) %collective-permute-start.3) | collective-permute-done | bytes 327712 | tf_op jit(solution)/shard_map/ppermute | solution.py:436
  146.5 1.4 collective-permute-done.12
  148.0 1.3 collective-permute-start.14
  149.3 11.3 %zonal.3 = (f32[4,320,1280]{2,1,0:T(8,128)}, bf16[2,8,2,80,128]{4,3,2,1,0:T(8,128)(2,1)S(1)}, bf16[2,8,2,80,128]{4,3,2,1,0:T(8,128)(2,1)S(1)}) custom-call(s32[3]{0:T(128)S(1)} %pad_add_fusion.18.refs_0_, bf16[8,2,80,128]{3,2,1,0:T(8,128)(2,1)S(1)} %bitcast.211, bf16[8,2,80,128]{3,2,1,0:T(8,128)(2,1)S(1)} %collective-permute-done.21.refs_2_, ...), custom_call_target="tpu_custom_call" | custom-call | flops 3355443200 | bytes 9175040 | tf_op jit(solution)/shard_map/zonal/pallas_call | solution.py:409
  160.6 1.8 collective-permute-start.40
  163.3 2.0 collective-permute-start.15
  165.6 13.3 %collective-permute-done.6.refs_3_ = bf16[8,2,2,80,128]{4,3,2,1,0:T(8,128)(2,1)S(1)} collective-permute-done((bf16[8,2,2,80,128]{4,3,2,1,0:T(8,128)(2,1)S(1)}, bf16[8,2,2,80,128]{4,3,2,1,0:T(8,128)(2,1)S(1)}, u32[]{:S(2)}, u32[]{:S(2)}) %collective-permute-start.6) | collective-permute-done | bytes 655392 | tf_op jit(solution)/shard_map/ppermute | solution.py:436
  179.8 0.9 collective-permute-start.41
  180.6 17.7 %zonal.4 = (f32[4,320,1280]{2,1,0:T(8,128)}, bf16[2,8,2,2,80,128]{5,4,3,2,1,0:T(8,128)(2,1)}, bf16[2,8,2,2,80,128]{5,4,3,2,1,0:T(8,128)(2,1)}) custom-call(s32[3]{0:T(128)S(1)} %pad_add_fusion.17.refs_0_, bf16[8,2,2,80,128]{4,3,2,1,0:T(8,128)(2,1)S(1)} %bitcast.214, ...), custom_call_target="tpu_custom_call", output_to_operand_aliasing={{0}: (11, {})} | custom-call | flops 6710886400 | bytes 11796480 | tf_op jit(solution)/shard_map/zonal/pallas_call | solution.py:409
  198.7 17.9 %zonal.5 = (f32[4,320,1280]{2,1,0:T(8,128)}, bf16[2,8,2,2,80,128]{5,4,3,2,1,0:T(8,128)(2,1)}, bf16[2,8,2,2,80,128]{5,4,3,2,1,0:T(8,128)(2,1)}) custom-call(s32[3]{0:T(128)S(1)} %pad_add_fusion.14.refs_0_, bf16[8,2,2,80,128]{4,3,2,1,0:T(8,128)(2,1)S(1)} %bitcast.217, ...), custom_call_target="tpu_custom_call", output_to_operand_aliasing={{0}: (11, {})} | custom-call | flops 6710886400 | bytes 11796480 | tf_op jit(solution)/shard_map/zonal/pallas_call | solution.py:409
  217.4 5.3 %collective-permute-done.42 = bf16[4,1,2,80,128]{4,3,2,0,1:T(8,128)(2,1)S(1)} collective-permute-done((bf16[4,1,2,80,128]{4,3,2,0,1:T(8,128)(2,1)S(1)}, bf16[4,1,2,80,128]{4,3,2,0,1:T(8,128)(2,1)S(1)}, u32[]{:S(2)}, u32[]{:S(2)}) %collective-permute-start.42) | collective-permute-done | bytes 163872 | tf_op jit(solution)/shard_map/ppermute | solution.py:436
  224.9 3.3 collective-permute-done.43
  228.2 2.3 collective-permute-start.44
  230.5 7.6 %collective-permute-done.33 = bf16[8,2,2,80,128]{4,3,2,1,0:T(8,128)(2,1)S(1)} collective-permute-done((bf16[8,2,2,80,128]{4,3,2,1,0:T(8,128)(2,1)S(1)}, bf16[8,2,2,80,128]{4,3,2,1,0:T(8,128)(2,1)S(1)}, u32[]{:S(2)}, u32[]{:S(2)}) %collective-permute-start.33) | collective-permute-done | bytes 655392 | tf_op jit(solution)/shard_map/ppermute | solution.py:436
  238.7 13.4 %collective-permute-done.25 = bf16[8,2,2,80,128]{4,3,2,1,0:T(8,128)(2,1)S(1)} collective-permute-done((bf16[8,2,2,80,128]{4,3,2,1,0:T(8,128)(2,1)S(1)}, bf16[8,2,2,80,128]{4,3,2,1,0:T(8,128)(2,1)S(1)}, u32[]{:S(2)}, u32[]{:S(2)}) %collective-permute-start.25) | collective-permute-done | bytes 655392 | tf_op jit(solution)/shard_map/ppermute | solution.py:436
  253.0 6.8 %collective-permute-done.35 = bf16[2,2,2,2,80,128]{5,4,3,2,0,1:T(8,128)(2,1)S(1)} collective-permute-done((bf16[2,2,2,2,80,128]{5,4,3,2,0,1:T(8,128)(2,1)S(1)}, bf16[2,2,2,2,80,128]{5,4,3,2,0,1:T(8,128)(2,1)S(1)}, u32[]{:S(2)}, u32[]{:S(2)}) %collective-permute-start.35) | collective-permute-done | bytes 327712 | tf_op jit(solution)/shard_map/ppermute | solution.py:436
  259.9 2.4 collective-permute-start.36
  263.0 1.2 collective-permute-start.27
  264.3 12.3 %collective-permute-done.36 = bf16[1,4,2,2,80,128]{5,4,3,2,1,0:T(8,128)(2,1)S(1)} collective-permute-done((bf16[1,4,2,2,80,128]{5,4,3,2,1,0:T(8,128)(2,1)S(1)}, bf16[1,4,2,2,80,128]{5,4,3,2,1,0:T(8,128)(2,1)S(1)}, u32[]{:S(2)}, u32[]{:S(2)}) %collective-permute-start.36) | collective-permute-done | bytes 327712 | tf_op jit(solution)/shard_map/ppermute | solution.py:436
  277.7 1.9 collective-permute-start.45
  280.1 13.3 %collective-permute-done.28 = bf16[1,4,2,2,80,128]{5,4,3,2,1,0:T(8,128)(2,1)S(1)} collective-permute-done((bf16[1,4,2,2,80,128]{5,4,3,2,1,0:T(8,128)(2,1)S(1)}, bf16[1,4,2,2,80,128]{5,4,3,2,1,0:T(8,128)(2,1)S(1)}, u32[]{:S(2)}, u32[]{:S(2)}) %collective-permute-start.28) | collective-permute-done | bytes 327712 | tf_op jit(solution)/shard_map/ppermute | solution.py:436
  294.3 2.6 collective-permute-start.39
  297.2 9.7 %legendre_down.3.refs_10_ = f32[4,2,80,336]{3,2,1,0:T(8,128)S(1)} custom-call(s32[2]{0:T(128)S(1)} %pad_add_fusion.16.refs_0_, bf16[8,2,80,128]{3,2,1,0:T(8,128)(2,1)S(1)} %bitcast.208, bf16[8,2,80,128]{3,2,1,0:T(8,128)(2,1)S(1)} %collective-permute-done.45.refs_2_, bf16[8,2,80,128]{3,2,1,0:T(8,128)(2,1)S(1)} %collective-permute-done.46.refs_3_, ...), custom_call_target="tpu_custom_call" | custom-call | flops 3523215360 | bytes 13762560 | tf_op jit(solution)/shard_map/legendre_down/pallas_call | solution.py:264
  306.9 0.9 copy-done.2
  307.9 2.8 collective-permute-start.31
  310.7 15.3 %legendre_down.4.refs_10_ = f32[4,2,80,336]{3,2,1,0:T(8,128)S(1)} custom-call(s32[2]{0:T(128)S(1)} %pad_add_fusion.16.refs_0_, bf16[8,2,2,80,128]{4,3,2,1,0:T(8,128)(2,1)S(1)} %bitcast.204, bf16[8,2,2,80,128]{4,3,2,1,0:T(8,128)(2,1)S(1)} %collective-permute-done.37.refs_2_, bf16[8,2,2,80,128]{4,3,2,1,0:T(8,128)(2,1)S(1)} %collective-permute-done.38.refs_3_, ...), custom_call_target="tpu_custom_call" | custom-call | flops 7046430720 | bytes 27525120 | tf_op jit(solution)/shard_map/legendre_down/pallas_call | solution.py:264
  326.0 0.9 copy-done.1
  326.9 16.1 %legendre_down.5 = f32[4,2,80,336]{3,2,1,0:T(8,128)} custom-call(s32[2]{0:T(128)S(1)} %pad_add_fusion.16.refs_0_, bf16[8,2,2,80,128]{4,3,2,1,0:T(8,128)(2,1)S(1)} %bitcast.201, bf16[8,2,2,80,128]{4,3,2,1,0:T(8,128)(2,1)S(1)} %collective-permute-done.29.refs_2_, bf16[8,2,2,80,128]{4,3,2,1,0:T(8,128)(2,1)S(1)} %collective-permute-done.30.refs_3_, ...), custom_call_target="tpu_custom_call" | custom-call | flops 7046430720 | bytes 27525120 | tf_op jit(solution)/shard_map/legendre_down/pallas_call | solution.py:264
  (197 shorter events, 17.8 us)
Async XLA Ops:
  1.3 2.4 copy-start.19
  6.3 9.7 %copy-start = (bf16[80,32,336]{2,1,0:T(8,128)(2,1)}, bf16[80,32,336]{2,1,0:T(8,128)(2,1)S(1)}, u32[]{:S(2)}) copy-start(bf16[80,32,336]{2,1,0:T(8,128)(2,1)S(1)} %multiply_bitcast_fusion.refs_1_) | copy-start | bytes 5160964
  15.9 37.2 %collective-permute-start.16 = (bf16[2,8,2,80,128]{4,3,2,1,0:T(8,128)(2,1)}, bf16[2,8,2,80,128]{4,3,2,1,0:T(8,128)(2,1)}, u32[]{:S(2)}, u32[]{:S(2)}) collective-permute-start(bf16[2,8,2,80,128]{4,3,2,1,0:T(8,128)(2,1)} %get-tuple-element.22), channel_id=1, source_target_pairs={{0,1},{1,0},{2,3},{3,2},{4,5},{5,4},{6,7},{7,6},{8,9},{9,8},{10,11... | collective-permute-start | bytes 1966088 | tf_op jit(solution)/shard_map/ppermute | solution.py:436
  32.2 16.7 %copy-start.18 = (s32[640]{0:T(1024)S(1)}, s32[640]{0:T(1024)}, u32[]{:S(2)}) copy-start(s32[640]{0:T(1024)} %param.8) | copy-start | bytes 7684
  32.2 45.1 %collective-permute-start.8 = (bf16[2,8,2,2,80,128]{5,4,3,2,1,0:T(8,128)(2,1)}, bf16[2,8,2,2,80,128]{5,4,3,2,1,0:T(8,128)(2,1)}, u32[]{:S(2)}, u32[]{:S(2)}) collective-permute-start(bf16[2,8,2,2,80,128]{5,4,3,2,1,0:T(8,128)(2,1)} %get-tuple-element.20), channel_id=1, source_target_pairs={{0,1},{1,0},{2,3},{3,2},{4,5},{5,4},{6,7},{7,6},{8,9},{9,8},{10,11... | collective-permute-start | bytes 3932168 | tf_op jit(solution)/shard_map/ppermute | solution.py:436
  48.9 33.5 %collective-permute-start = (bf16[2,8,2,2,80,128]{5,4,3,2,1,0:T(8,128)(2,1)}, bf16[2,8,2,2,80,128]{5,4,3,2,1,0:T(8,128)(2,1)}, u32[]{:S(2)}, u32[]{:S(2)}) collective-permute-start(bf16[2,8,2,2,80,128]{5,4,3,2,1,0:T(8,128)(2,1)} %get-tuple-element.18), channel_id=1, source_target_pairs={{0,1},{1,0},{2,3},{3,2},{4,5},{5,4},{6,7},{7,6},{8,9},{9,8},{10,11... | collective-permute-start | bytes 3932168 | tf_op jit(solution)/shard_map/ppermute | solution.py:436
  54.2 10.8 %collective-permute-start.17 = (bf16[8,2,80,128]{3,2,1,0:T(8,128)(2,1)S(1)}, bf16[8,2,80,128]{3,2,1,0:T(8,128)(2,1)S(1)}, u32[]{:S(2)}, u32[]{:S(2)}) collective-permute-start(bf16[8,2,80,128]{3,2,1,0:T(8,128)(2,1)S(1)} %fusion.24), channel_id=1, source_target_pairs={{0,2},{1,3},{2,0},{3,1},{4,6},{5,7},{6,4},{7,5},{8,10},{9,11},{10,... | collective-permute-start | bytes 983048 | tf_op jit(solution)/shard_map/ppermute | solution.py:436
  59.7 9.0 %copy-start.23 = (s32[320]{0:T(512)S(1)}, s32[320]{0:T(512)}, u32[]{:S(2)}) copy-start(s32[320]{0:T(512)} %param.9) | copy-start | bytes 3844
  66.2 9.6 %collective-permute-start.18 = (bf16[4,1,2,80,128]{4,3,2,0,1:T(8,128)(2,1)S(1)}, bf16[4,1,2,80,128]{4,3,2,0,1:T(8,128)(2,1)S(1)}, u32[]{:S(2)}, u32[]{:S(2)}) collective-permute-start(bf16[4,1,2,80,128]{4,3,2,0,1:T(8,128)(2,1)S(1)} %get-tuple-element.82), channel_id=1, source_target_pairs={{0,16},{4,20},{8,24},{12,28},{16,0},{20,4},{24,8},{28,12},{1,17},{... | collective-permute-start | bytes 491528 | tf_op jit(solution)/shard_map/ppermute | solution.py:436
  68.6 11.1 %copy-start.12 = (pred[8,256,128]{2,1,0:T(8,128)(4,1)}, pred[8,256,128]{2,1,0:T(8,128)(4,1)S(1)}, u32[]{:S(2)}) copy-start(pred[8,256,128]{2,1,0:T(8,128)(4,1)S(1)} %fusion.57) | copy-start | bytes 786436
  75.9 5.1 %collective-permute-start.19 = (bf16[2,2,2,80,128]{4,3,2,0,1:T(8,128)(2,1)S(1)}, bf16[2,2,2,80,128]{4,3,2,0,1:T(8,128)(2,1)S(1)}, u32[]{:S(2)}, u32[]{:S(2)}) collective-permute-start(bf16[2,2,2,80,128]{4,3,2,0,1:T(8,128)(2,1)S(1)} %fusion.43), channel_id=1, source_target_pairs={{0,8},{4,12},{8,0},{12,4},{16,24},{20,28},{24,16},{28,20},{1,9},{5... | collective-permute-start | bytes 491528 | tf_op jit(solution)/shard_map/ppermute | solution.py:436
  77.4 5.0 %copy-start.6 = (bf16[2,8,2,2,80,128]{5,4,3,2,1,0:T(8,128)(2,1)S(1)}, bf16[2,8,2,2,80,128]{5,4,3,2,1,0:T(8,128)(2,1)}, u32[]{:S(2)}) copy-start(bf16[2,8,2,2,80,128]{5,4,3,2,1,0:T(8,128)(2,1)} %copy-done.5) | copy-start | bytes 3932164
  79.8 17.8 %collective-permute-start.9 = (bf16[8,2,2,80,128]{4,3,2,1,0:T(8,128)(2,1)}, bf16[8,2,2,80,128]{4,3,2,1,0:T(8,128)(2,1)}, u32[]{:S(2)}, u32[]{:S(2)}) collective-permute-start(bf16[8,2,2,80,128]{4,3,2,1,0:T(8,128)(2,1)} %fusion.11), channel_id=1, source_target_pairs={{0,2},{1,3},{2,0},{3,1},{4,6},{5,7},{6,4},{7,5},{8,10},{9,11},{10,... | collective-permute-start | bytes 1966088 | tf_op jit(solution)/shard_map/ppermute | solution.py:436
  81.1 14.6 %collective-permute-start.20 = (bf16[1,4,2,80,128]{4,3,2,1,0:T(8,128)(2,1)S(1)}, bf16[1,4,2,80,128]{4,3,2,1,0:T(8,128)(2,1)}, u32[]{:S(2)}, u32[]{:S(2)}) collective-permute-start(bf16[1,4,2,80,128]{4,3,2,1,0:T(8,128)(2,1)S(1)} %bitcast.254), channel_id=1, source_target_pairs={{0,4},{4,0},{8,12},{12,8},{16,20},{20,16},{24,28},{28,24},{1,5},{5... | collective-permute-start | bytes 491528 | tf_op jit(solution)/shard_map/ppermute | solution.py:436
  84.5 25.1 %collective-permute-start.1 = (bf16[8,2,2,80,128]{4,3,2,1,0:T(8,128)(2,1)}, bf16[8,2,2,80,128]{4,3,2,1,0:T(8,128)(2,1)}, u32[]{:S(2)}, u32[]{:S(2)}) collective-permute-start(bf16[8,2,2,80,128]{4,3,2,1,0:T(8,128)(2,1)} %fusion.10), channel_id=1, source_target_pairs={{0,2},{1,3},{2,0},{3,1},{4,6},{5,7},{6,4},{7,5},{8,10},{9,11},{10,... | collective-permute-start | bytes 1966088 | tf_op jit(solution)/shard_map/ppermute | solution.py:436
  88.3 9.2 %copy-start.9 = (bf16[2,8,2,2,80,128]{5,4,3,2,1,0:T(8,128)(2,1)S(1)}, bf16[2,8,2,2,80,128]{5,4,3,2,1,0:T(8,128)(2,1)}, u32[]{:S(2)}) copy-start(bf16[2,8,2,2,80,128]{5,4,3,2,1,0:T(8,128)(2,1)} %copy-done.8) | copy-start | bytes 3932164
  96.6 21.1 %collective-permute-start.22 = (bf16[8,2,80,128]{3,2,1,0:T(8,128)(2,1)S(1)}, bf16[8,2,80,128]{3,2,1,0:T(8,128)(2,1)S(1)}, u32[]{:S(2)}, u32[]{:S(2)}) collective-permute-start(bf16[8,2,80,128]{3,2,1,0:T(8,128)(2,1)S(1)} %bitcast.209), channel_id=1, source_target_pairs={{0,2},{1,3},{2,0},{3,1},{4,6},{5,7},{6,4},{7,5},{8,10},{9,11},{10,... | collective-permute-start | bytes 983048 | tf_op jit(solution)/shard_map/ppermute | solution.py:436
  99.2 10.4 %copy-start.7 = (bf16[2,8,2,2,80,128]{5,4,3,2,1,0:T(8,128)(2,1)S(1)}, bf16[2,8,2,2,80,128]{5,4,3,2,1,0:T(8,128)(2,1)}, u32[]{:S(2)}) copy-start(bf16[2,8,2,2,80,128]{5,4,3,2,1,0:T(8,128)(2,1)} %copy-done.5) | copy-start | bytes 3932164
  99.3 24.9 %collective-permute-start.10 = (bf16[4,1,2,2,80,128]{5,4,3,2,0,1:T(8,128)(2,1)S(1)}, bf16[4,1,2,2,80,128]{5,4,3,2,0,1:T(8,128)(2,1)S(1)}, u32[]{:S(2)}, u32[]{:S(2)}) collective-permute-start(bf16[4,1,2,2,80,128]{5,4,3,2,0,1:T(8,128)(2,1)S(1)} %get-tuple-element.68), channel_id=1, source_target_pairs={{0,16},{4,20},{8,24},{12,28},{16,0},{20,4},{24,8},{28,12},{1,17},{... | collective-permute-start | bytes 983048 | tf_op jit(solution)/shard_map/ppermute | solution.py:436
  111.2 20.0 %collective-permute-start.2 = (bf16[4,1,2,2,80,128]{5,4,3,2,0,1:T(8,128)(2,1)S(1)}, bf16[4,1,2,2,80,128]{5,4,3,2,0,1:T(8,128)(2,1)S(1)}, u32[]{:S(2)}, u32[]{:S(2)}) collective-permute-start(bf16[4,1,2,2,80,128]{5,4,3,2,0,1:T(8,128)(2,1)S(1)} %get-tuple-element.74), channel_id=1, source_target_pairs={{0,16},{4,20},{8,24},{12,28},{16,0},{20,4},{24,8},{28,12},{1,17},{... | collective-permute-start | bytes 983048 | tf_op jit(solution)/shard_map/ppermute | solution.py:436
  114.5 34.8 %collective-permute-start.21 = (bf16[8,2,80,128]{3,2,1,0:T(8,128)(2,1)S(1)}, bf16[8,2,80,128]{3,2,1,0:T(8,128)(2,1)S(1)}, u32[]{:S(2)}, u32[]{:S(2)}) collective-permute-start(bf16[8,2,80,128]{3,2,1,0:T(8,128)(2,1)S(1)} %bitcast.210), channel_id=1, source_target_pairs={{0,1},{1,0},{2,3},{3,2},{4,5},{5,4},{6,7},{7,6},{8,9},{9,8},{10,11... | collective-permute-start | bytes 983048 | tf_op jit(solution)/shard_map/ppermute | solution.py:436
  117.7 31.6 %collective-permute-start.23 = (bf16[8,2,80,128]{3,2,1,0:T(8,128)(2,1)S(1)}, bf16[8,2,80,128]{3,2,1,0:T(8,128)(2,1)S(1)}, u32[]{:S(2)}, u32[]{:S(2)}) collective-permute-start(bf16[8,2,80,128]{3,2,1,0:T(8,128)(2,1)S(1)} %collective-permute-done.22.refs_3_), channel_id=1, source_target_pairs={{0,1},{1,0},{2,3},{3,2},{4,5},{5,4},{6,7},{7,6},{8,9},{9,8},{10,11... | collective-permute-start | bytes 983048 | tf_op jit(solution)/shard_map/ppermute | solution.py:436
  124.2 14.9 %collective-permute-start.11 = (bf16[2,2,2,2,80,128]{5,4,3,2,0,1:T(8,128)(2,1)S(1)}, bf16[2,2,2,2,80,128]{5,4,3,2,0,1:T(8,128)(2,1)S(1)}, u32[]{:S(2)}, u32[]{:S(2)}) collective-permute-start(bf16[2,2,2,2,80,128]{5,4,3,2,0,1:T(8,128)(2,1)S(1)} %fusion.35), channel_id=1, source_target_pairs={{0,8},{4,12},{8,0},{12,4},{16,24},{20,28},{24,16},{28,20},{1,9},{5... | collective-permute-start | bytes 983048 | tf_op jit(solution)/shard_map/ppermute | solution.py:436
  131.3 14.9 %collective-permute-start.3 = (bf16[2,2,2,2,80,128]{5,4,3,2,0,1:T(8,128)(2,1)S(1)}, bf16[2,2,2,2,80,128]{5,4,3,2,0,1:T(8,128)(2,1)S(1)}, u32[]{:S(2)}, u32[]{:S(2)}) collective-permute-start(bf16[2,2,2,2,80,128]{5,4,3,2,0,1:T(8,128)(2,1)S(1)} %fusion.37), channel_id=1, source_target_pairs={{0,8},{4,12},{8,0},{12,4},{16,24},{20,28},{24,16},{28,20},{1,9},{5... | collective-permute-start | bytes 983048 | tf_op jit(solution)/shard_map/ppermute | solution.py:436
  139.2 8.7 %collective-permute-start.12 = (bf16[1,4,2,2,80,128]{5,4,3,2,1,0:T(8,128)(2,1)S(1)}, bf16[1,4,2,2,80,128]{5,4,3,2,1,0:T(8,128)(2,1)S(1)}, u32[]{:S(2)}, u32[]{:S(2)}) collective-permute-start(bf16[1,4,2,2,80,128]{5,4,3,2,1,0:T(8,128)(2,1)S(1)} %bitcast.247), channel_id=1, source_target_pairs={{0,4},{4,0},{8,12},{12,8},{16,20},{20,16},{24,28},{28,24},{1,5},{5... | collective-permute-start | bytes 983048 | tf_op jit(solution)/shard_map/ppermute | solution.py:436
  146.2 3.1 copy-start.4
  146.2 16.2 %collective-permute-start.4 = (bf16[1,4,2,2,80,128]{5,4,3,2,1,0:T(8,128)(2,1)S(1)}, bf16[1,4,2,2,80,128]{5,4,3,2,1,0:T(8,128)(2,1)S(1)}, u32[]{:S(2)}, u32[]{:S(2)}) collective-permute-start(bf16[1,4,2,2,80,128]{5,4,3,2,1,0:T(8,128)(2,1)S(1)} %bitcast.240), channel_id=1, source_target_pairs={{0,4},{4,0},{8,12},{12,8},{16,20},{20,16},{24,28},{28,24},{1,5},{5... | collective-permute-start | bytes 983048 | tf_op jit(solution)/shard_map/ppermute | solution.py:436
  148.0 15.3 %collective-permute-start.14 = (bf16[8,2,2,80,128]{4,3,2,1,0:T(8,128)(2,1)S(1)}, bf16[8,2,2,80,128]{4,3,2,1,0:T(8,128)(2,1)S(1)}, u32[]{:S(2)}, u32[]{:S(2)}) collective-permute-start(bf16[8,2,2,80,128]{4,3,2,1,0:T(8,128)(2,1)S(1)} %bitcast.212), channel_id=1, source_target_pairs={{0,2},{1,3},{2,0},{3,1},{4,6},{5,7},{6,4},{7,5},{8,10},{9,11},{10,... | collective-permute-start | bytes 1966088 | tf_op jit(solution)/shard_map/ppermute | solution.py:436
  160.6 19.1 %collective-permute-start.40 = (bf16[2,8,2,80,128]{4,3,2,1,0:T(8,128)(2,1)S(1)}, bf16[2,8,2,80,128]{4,3,2,1,0:T(8,128)(2,1)S(1)}, u32[]{:S(2)}, u32[]{:S(2)}) collective-permute-start(bf16[2,8,2,80,128]{4,3,2,1,0:T(8,128)(2,1)S(1)} %get-tuple-element.31), channel_id=1, source_target_pairs={{0,1},{1,0},{2,3},{3,2},{4,5},{5,4},{6,7},{7,6},{8,9},{9,8},{10,11... | collective-permute-start | bytes 1966088 | tf_op jit(solution)/shard_map/ppermute | solution.py:436
  162.5 16.4 %collective-permute-start.6 = (bf16[8,2,2,80,128]{4,3,2,1,0:T(8,128)(2,1)S(1)}, bf16[8,2,2,80,128]{4,3,2,1,0:T(8,128)(2,1)S(1)}, u32[]{:S(2)}, u32[]{:S(2)}) collective-permute-start(bf16[8,2,2,80,128]{4,3,2,1,0:T(8,128)(2,1)S(1)} %bitcast.215), channel_id=1, source_target_pairs={{0,2},{1,3},{2,0},{3,1},{4,6},{5,7},{6,4},{7,5},{8,10},{9,11},{10,... | collective-permute-start | bytes 1966088 | tf_op jit(solution)/shard_map/ppermute | solution.py:436
  162.9 17.7 %collective-permute-start.13 = (bf16[8,2,2,80,128]{4,3,2,1,0:T(8,128)(2,1)S(1)}, bf16[8,2,2,80,128]{4,3,2,1,0:T(8,128)(2,1)S(1)}, u32[]{:S(2)}, u32[]{:S(2)}) collective-permute-start(bf16[8,2,2,80,128]{4,3,2,1,0:T(8,128)(2,1)S(1)} %bitcast.213), channel_id=1, source_target_pairs={{0,1},{1,0},{2,3},{3,2},{4,5},{5,4},{6,7},{7,6},{8,9},{9,8},{10,11... | collective-permute-start | bytes 1966088 | tf_op jit(solution)/shard_map/ppermute | solution.py:436
  163.3 17.4 %collective-permute-start.15 = (bf16[8,2,2,80,128]{4,3,2,1,0:T(8,128)(2,1)S(1)}, bf16[8,2,2,80,128]{4,3,2,1,0:T(8,128)(2,1)S(1)}, u32[]{:S(2)}, u32[]{:S(2)}) collective-permute-start(bf16[8,2,2,80,128]{4,3,2,1,0:T(8,128)(2,1)S(1)} %collective-permute-done.14.refs_3_), channel_id=1, source_target_pairs={{0,1},{1,0},{2,3},{3,2},{4,5},{5,4},{6,7},{7,6},{8,9},{9,8},{10,11... | collective-permute-start | bytes 1966088 | tf_op jit(solution)/shard_map/ppermute | solution.py:436
  165.5 33.1 %collective-permute-start.5 = (bf16[8,2,2,80,128]{4,3,2,1,0:T(8,128)(2,1)S(1)}, bf16[8,2,2,80,128]{4,3,2,1,0:T(8,128)(2,1)S(1)}, u32[]{:S(2)}, u32[]{:S(2)}) collective-permute-start(bf16[8,2,2,80,128]{4,3,2,1,0:T(8,128)(2,1)S(1)} %bitcast.216), channel_id=1, source_target_pairs={{0,1},{1,0},{2,3},{3,2},{4,5},{5,4},{6,7},{7,6},{8,9},{9,8},{10,11... | collective-permute-start | bytes 1966088 | tf_op jit(solution)/shard_map/ppermute | solution.py:436
  178.9 19.8 %collective-permute-start.7 = (bf16[8,2,2,80,128]{4,3,2,1,0:T(8,128)(2,1)S(1)}, bf16[8,2,2,80,128]{4,3,2,1,0:T(8,128)(2,1)S(1)}, u32[]{:S(2)}, u32[]{:S(2)}) collective-permute-start(bf16[8,2,2,80,128]{4,3,2,1,0:T(8,128)(2,1)S(1)} %collective-permute-done.6.refs_3_), channel_id=1, source_target_pairs={{0,1},{1,0},{2,3},{3,2},{4,5},{5,4},{6,7},{7,6},{8,9},{9,8},{10,11... | collective-permute-start | bytes 1966088 | tf_op jit(solution)/shard_map/ppermute | solution.py:436
  179.8 37.1 %collective-permute-start.41 = (bf16[8,2,80,128]{3,2,1,0:T(8,128)(2,1)S(1)}, bf16[8,2,80,128]{3,2,1,0:T(8,128)(2,1)S(1)}, u32[]{:S(2)}, u32[]{:S(2)}) collective-permute-start(bf16[8,2,80,128]{3,2,1,0:T(8,128)(2,1)S(1)} %fusion.25), channel_id=1, source_target_pairs={{0,2},{1,3},{2,0},{3,1},{4,6},{5,7},{6,4},{7,5},{8,10},{9,11},{10,... | collective-permute-start | bytes 983048 | tf_op jit(solution)/shard_map/ppermute | solution.py:436
  198.3 24.4 %collective-permute-start.32 = (bf16[2,8,2,2,80,128]{5,4,3,2,1,0:T(8,128)(2,1)}, bf16[2,8,2,2,80,128]{5,4,3,2,1,0:T(8,128)(2,1)S(1)}, u32[]{:S(2)}, u32[]{:S(2)}) collective-permute-start(bf16[2,8,2,2,80,128]{5,4,3,2,1,0:T(8,128)(2,1)} %get-tuple-element.29), channel_id=1, source_target_pairs={{0,1},{1,0},{2,3},{3,2},{4,5},{5,4},{6,7},{7,6},{8,9},{9,8},{10,11... | collective-permute-start | bytes 3932168 | tf_op jit(solution)/shard_map/ppermute | solution.py:436
  216.6 6.1 %copy-start.10 = (bf16[2,8,2,2,80,128]{5,4,3,2,1,0:T(8,128)(2,1)S(1)}, bf16[2,8,2,2,80,128]{5,4,3,2,1,0:T(8,128)(2,1)}, u32[]{:S(2)}) copy-start(bf16[2,8,2,2,80,128]{5,4,3,2,1,0:T(8,128)(2,1)} %get-tuple-element.28) | copy-start | bytes 3932164
  216.6 7.2 %collective-permute-start.24 = (bf16[2,8,2,2,80,128]{5,4,3,2,1,0:T(8,128)(2,1)}, bf16[2,8,2,2,80,128]{5,4,3,2,1,0:T(8,128)(2,1)S(1)}, u32[]{:S(2)}, u32[]{:S(2)}) collective-permute-start(bf16[2,8,2,2,80,128]{5,4,3,2,1,0:T(8,128)(2,1)} %get-tuple-element.27), channel_id=1, source_target_pairs={{0,1},{1,0},{2,3},{3,2},{4,5},{5,4},{6,7},{7,6},{8,9},{9,8},{10,11... | collective-permute-start | bytes 3932168 | tf_op jit(solution)/shard_map/ppermute | solution.py:436
  217.1 5.6 %collective-permute-start.42 = (bf16[4,1,2,80,128]{4,3,2,0,1:T(8,128)(2,1)S(1)}, bf16[4,1,2,80,128]{4,3,2,0,1:T(8,128)(2,1)S(1)}, u32[]{:S(2)}, u32[]{:S(2)}) collective-permute-start(bf16[4,1,2,80,128]{4,3,2,0,1:T(8,128)(2,1)S(1)} %get-tuple-element.78), channel_id=1, source_target_pairs={{0,4},{4,0},{8,12},{12,8},{16,20},{20,16},{24,28},{28,24},{1,5},{5... | collective-permute-start | bytes 491528 | tf_op jit(solution)/shard_map/ppermute | solution.py:436
  222.9 15.2 %collective-permute-start.33 = (bf16[8,2,2,80,128]{4,3,2,1,0:T(8,128)(2,1)S(1)}, bf16[8,2,2,80,128]{4,3,2,1,0:T(8,128)(2,1)S(1)}, u32[]{:S(2)}, u32[]{:S(2)}) collective-permute-start(bf16[8,2,2,80,128]{4,3,2,1,0:T(8,128)(2,1)S(1)} %fusion.13), channel_id=1, source_target_pairs={{0,2},{1,3},{2,0},{3,1},{4,6},{5,7},{6,4},{7,5},{8,10},{9,11},{10,... | collective-permute-start | bytes 1966088 | tf_op jit(solution)/shard_map/ppermute | solution.py:436
  223.7 4.5 %collective-permute-start.43 = (bf16[2,2,2,80,128]{4,3,2,0,1:T(8,128)(2,1)S(1)}, bf16[2,2,2,80,128]{4,3,2,0,1:T(8,128)(2,1)S(1)}, u32[]{:S(2)}, u32[]{:S(2)}) collective-permute-start(bf16[2,2,2,80,128]{4,3,2,0,1:T(8,128)(2,1)S(1)} %fusion.41), channel_id=1, source_target_pairs={{0,8},{4,12},{8,0},{12,4},{16,24},{20,28},{24,16},{28,20},{1,9},{5... | collective-permute-start | bytes 491528 | tf_op jit(solution)/shard_map/ppermute | solution.py:436
  224.2 28.0 %collective-permute-start.25 = (bf16[8,2,2,80,128]{4,3,2,1,0:T(8,128)(2,1)S(1)}, bf16[8,2,2,80,128]{4,3,2,1,0:T(8,128)(2,1)S(1)}, u32[]{:S(2)}, u32[]{:S(2)}) collective-permute-start(bf16[8,2,2,80,128]{4,3,2,1,0:T(8,128)(2,1)S(1)} %fusion.12), channel_id=1, source_target_pairs={{0,2},{1,3},{2,0},{3,1},{4,6},{5,7},{6,4},{7,5},{8,10},{9,11},{10,... | collective-permute-start | bytes 1966088 | tf_op jit(solution)/shard_map/ppermute | solution.py:436
  228.2 34.0 %collective-permute-start.44 = (bf16[1,4,2,80,128]{4,3,2,1,0:T(8,128)(2,1)S(1)}, bf16[1,4,2,80,128]{4,3,2,1,0:T(8,128)(2,1)S(1)}, u32[]{:S(2)}, u32[]{:S(2)}) collective-permute-start(bf16[1,4,2,80,128]{4,3,2,1,0:T(8,128)(2,1)S(1)} %bitcast.252), channel_id=1, source_target_pairs={{0,16},{4,20},{8,24},{12,28},{16,0},{20,4},{24,8},{28,12},{1,17},{... | collective-permute-start | bytes 491528 | tf_op jit(solution)/shard_map/ppermute | solution.py:436
  238.4 14.3 %collective-permute-start.34 = (bf16[4,1,2,2,80,128]{5,4,3,2,0,1:T(8,128)(2,1)S(1)}, bf16[4,1,2,2,80,128]{5,4,3,2,0,1:T(8,128)(2,1)S(1)}, u32[]{:S(2)}, u32[]{:S(2)}) collective-permute-start(bf16[4,1,2,2,80,128]{5,4,3,2,0,1:T(8,128)(2,1)S(1)} %get-tuple-element.60), channel_id=1, source_target_pairs={{0,4},{4,0},{8,12},{12,8},{16,20},{20,16},{24,28},{28,24},{1,5},{5... | collective-permute-start | bytes 983048 | tf_op jit(solution)/shard_map/ppermute | solution.py:436
  252.5 10.5 %collective-permute-start.26 = (bf16[4,1,2,2,80,128]{5,4,3,2,0,1:T(8,128)(2,1)S(1)}, bf16[4,1,2,2,80,128]{5,4,3,2,0,1:T(8,128)(2,1)S(1)}, u32[]{:S(2)}, u32[]{:S(2)}) collective-permute-start(bf16[4,1,2,2,80,128]{5,4,3,2,0,1:T(8,128)(2,1)S(1)} %get-tuple-element.64), channel_id=1, source_target_pairs={{0,4},{4,0},{8,12},{12,8},{16,20},{20,16},{24,28},{28,24},{1,5},{5... | collective-permute-start | bytes 983048 | tf_op jit(solution)/shard_map/ppermute | solution.py:436
  252.8 7.0 %collective-permute-start.35 = (bf16[2,2,2,2,80,128]{5,4,3,2,0,1:T(8,128)(2,1)S(1)}, bf16[2,2,2,2,80,128]{5,4,3,2,0,1:T(8,128)(2,1)S(1)}, u32[]{:S(2)}, u32[]{:S(2)}) collective-permute-start(bf16[2,2,2,2,80,128]{5,4,3,2,0,1:T(8,128)(2,1)S(1)} %fusion.31), channel_id=1, source_target_pairs={{0,8},{4,12},{8,0},{12,4},{16,24},{20,28},{24,16},{28,20},{1,9},{5... | collective-permute-start | bytes 983048 | tf_op jit(solution)/shard_map/ppermute | solution.py:436
  259.9 16.7 %collective-permute-start.36 = (bf16[1,4,2,2,80,128]{5,4,3,2,1,0:T(8,128)(2,1)S(1)}, bf16[1,4,2,2,80,128]{5,4,3,2,1,0:T(8,128)(2,1)S(1)}, u32[]{:S(2)}, u32[]{:S(2)}) collective-permute-start(bf16[1,4,2,2,80,128]{5,4,3,2,1,0:T(8,128)(2,1)S(1)} %bitcast.242), channel_id=1, source_target_pairs={{0,16},{4,20},{8,24},{12,28},{16,0},{20,4},{24,8},{28,12},{1,17},{... | collective-permute-start | bytes 983048 | tf_op jit(solution)/shard_map/ppermute | solution.py:436
  262.3 17.3 %collective-permute-start.46 = (bf16[8,2,80,128]{3,2,1,0:T(8,128)(2,1)S(1)}, bf16[8,2,80,128]{3,2,1,0:T(8,128)(2,1)S(1)}, u32[]{:S(2)}, u32[]{:S(2)}) collective-permute-start(bf16[8,2,80,128]{3,2,1,0:T(8,128)(2,1)S(1)} %bitcast.206), channel_id=1, source_target_pairs={{0,2},{1,3},{2,0},{3,1},{4,6},{5,7},{6,4},{7,5},{8,10},{9,11},{10,... | collective-permute-start | bytes 983048 | tf_op jit(solution)/shard_map/ppermute | solution.py:436
  263.0 14.4 %collective-permute-start.27 = (bf16[2,2,2,2,80,128]{5,4,3,2,0,1:T(8,128)(2,1)S(1)}, bf16[2,2,2,2,80,128]{5,4,3,2,0,1:T(8,128)(2,1)S(1)}, u32[]{:S(2)}, u32[]{:S(2)}) collective-permute-start(bf16[2,2,2,2,80,128]{5,4,3,2,0,1:T(8,128)(2,1)S(1)} %fusion.33), channel_id=1, source_target_pairs={{0,8},{4,12},{8,0},{12,4},{16,24},{20,28},{24,16},{28,20},{1,9},{5... | collective-permute-start | bytes 983048 | tf_op jit(solution)/shard_map/ppermute | solution.py:436
  276.7 17.6 %collective-permute-start.38 = (bf16[8,2,2,80,128]{4,3,2,1,0:T(8,128)(2,1)S(1)}, bf16[8,2,2,80,128]{4,3,2,1,0:T(8,128)(2,1)S(1)}, u32[]{:S(2)}, u32[]{:S(2)}) collective-permute-start(bf16[8,2,2,80,128]{4,3,2,1,0:T(8,128)(2,1)S(1)} %bitcast.202), channel_id=1, source_target_pairs={{0,2},{1,3},{2,0},{3,1},{4,6},{5,7},{6,4},{7,5},{8,10},{9,11},{10,... | collective-permute-start | bytes 1966088 | tf_op jit(solution)/shard_map/ppermute | solution.py:436
  277.4 19.4 %copy-start.14 = (s32[336]{0:T(512)S(1)}, s32[336]{0:T(512)}, u32[]{:S(2)}) copy-start(s32[336]{0:T(512)} %copy-done.13) | copy-start | bytes 4036
  277.5 19.4 %copy-start.16 = (s32[80]{0:T(128)S(1)}, s32[80]{0:T(128)}, u32[]{:S(2)}) copy-start(s32[80]{0:T(128)} %copy-done.15) | copy-start | bytes 964
  277.5 19.4 %copy-start.17 = (s32[336]{0:T(512)S(1)}, s32[336]{0:T(512)}, u32[]{:S(2)}) copy-start(s32[336]{0:T(512)} %get-tuple-element.99) | copy-start | bytes 4036
  277.5 19.4 %copy-start.20 = (pred[336]{0:T(512)(128)(4,1)S(1)}, pred[336]{0:T(512)(128)(4,1)}, u32[]{:S(2)}) copy-start(pred[336]{0:T(512)(128)(4,1)} %copy-done.19) | copy-start | bytes 1012
  277.5 19.4 %copy-start.21 = (s32[80]{0:T(128)S(1)}, s32[80]{0:T(128)}, u32[]{:S(2)}) copy-start(s32[80]{0:T(128)} %get-tuple-element.53) | copy-start | bytes 964
  277.5 19.5 %copy-start.22 = (f32[4]{0:T(128)S(1)}, f32[4]{0:T(128)}, u32[]{:S(2)}) copy-start(f32[4]{0:T(128)} %param.11) | copy-start | bytes 52
  277.6 15.8 %collective-permute-start.28 = (bf16[1,4,2,2,80,128]{5,4,3,2,1,0:T(8,128)(2,1)S(1)}, bf16[1,4,2,2,80,128]{5,4,3,2,1,0:T(8,128)(2,1)S(1)}, u32[]{:S(2)}, u32[]{:S(2)}) collective-permute-start(bf16[1,4,2,2,80,128]{5,4,3,2,1,0:T(8,128)(2,1)S(1)} %bitcast.248), channel_id=1, source_target_pairs={{0,16},{4,20},{8,24},{12,28},{16,0},{20,4},{24,8},{28,12},{1,17},{... | collective-permute-start | bytes 983048 | tf_op jit(solution)/shard_map/ppermute | solution.py:436
  277.7 19.5 %collective-permute-start.45 = (bf16[8,2,80,128]{3,2,1,0:T(8,128)(2,1)S(1)}, bf16[8,2,80,128]{3,2,1,0:T(8,128)(2,1)S(1)}, u32[]{:S(2)}, u32[]{:S(2)}) collective-permute-start(bf16[8,2,80,128]{3,2,1,0:T(8,128)(2,1)S(1)} %bitcast.207), channel_id=1, source_target_pairs={{0,1},{1,0},{2,3},{3,2},{4,5},{5,4},{6,7},{7,6},{8,9},{9,8},{10,11... | collective-permute-start | bytes 983048 | tf_op jit(solution)/shard_map/ppermute | solution.py:436
  279.6 17.6 %collective-permute-start.47 = (bf16[8,2,80,128]{3,2,1,0:T(8,128)(2,1)S(1)}, bf16[8,2,80,128]{3,2,1,0:T(8,128)(2,1)S(1)}, u32[]{:S(2)}, u32[]{:S(2)}) collective-permute-start(bf16[8,2,80,128]{3,2,1,0:T(8,128)(2,1)S(1)} %collective-permute-done.46.refs_3_), channel_id=1, source_target_pairs={{0,1},{1,0},{2,3},{3,2},{4,5},{5,4},{6,7},{7,6},{8,9},{9,8},{10,11... | collective-permute-start | bytes 983048 | tf_op jit(solution)/shard_map/ppermute | solution.py:436
  279.6 31.0 %collective-permute-start.37 = (bf16[8,2,2,80,128]{4,3,2,1,0:T(8,128)(2,1)S(1)}, bf16[8,2,2,80,128]{4,3,2,1,0:T(8,128)(2,1)S(1)}, u32[]{:S(2)}, u32[]{:S(2)}) collective-permute-start(bf16[8,2,2,80,128]{4,3,2,1,0:T(8,128)(2,1)S(1)} %bitcast.203), channel_id=1, source_target_pairs={{0,1},{1,0},{2,3},{3,2},{4,5},{5,4},{6,7},{7,6},{8,9},{9,8},{10,11... | collective-permute-start | bytes 1966088 | tf_op jit(solution)/shard_map/ppermute | solution.py:436
  293.4 14.4 %collective-permute-start.30 = (bf16[8,2,2,80,128]{4,3,2,1,0:T(8,128)(2,1)S(1)}, bf16[8,2,2,80,128]{4,3,2,1,0:T(8,128)(2,1)S(1)}, u32[]{:S(2)}, u32[]{:S(2)}) collective-permute-start(bf16[8,2,2,80,128]{4,3,2,1,0:T(8,128)(2,1)S(1)} %bitcast.199), channel_id=1, source_target_pairs={{0,2},{1,3},{2,0},{3,1},{4,6},{5,7},{6,4},{7,5},{8,10},{9,11},{10,... | collective-permute-start | bytes 1966088 | tf_op jit(solution)/shard_map/ppermute | solution.py:436
  294.3 16.4 %collective-permute-start.39 = (bf16[8,2,2,80,128]{4,3,2,1,0:T(8,128)(2,1)S(1)}, bf16[8,2,2,80,128]{4,3,2,1,0:T(8,128)(2,1)S(1)}, u32[]{:S(2)}, u32[]{:S(2)}) collective-permute-start(bf16[8,2,2,80,128]{4,3,2,1,0:T(8,128)(2,1)S(1)} %collective-permute-done.38.refs_3_), channel_id=1, source_target_pairs={{0,1},{1,0},{2,3},{3,2},{4,5},{5,4},{6,7},{7,6},{8,9},{9,8},{10,11... | collective-permute-start | bytes 1966088 | tf_op jit(solution)/shard_map/ppermute | solution.py:436
  307.8 19.1 %collective-permute-start.29 = (bf16[8,2,2,80,128]{4,3,2,1,0:T(8,128)(2,1)S(1)}, bf16[8,2,2,80,128]{4,3,2,1,0:T(8,128)(2,1)S(1)}, u32[]{:S(2)}, u32[]{:S(2)}) collective-permute-start(bf16[8,2,2,80,128]{4,3,2,1,0:T(8,128)(2,1)S(1)} %bitcast.200), channel_id=1, source_target_pairs={{0,1},{1,0},{2,3},{3,2},{4,5},{5,4},{6,7},{7,6},{8,9},{9,8},{10,11... | collective-permute-start | bytes 1966088 | tf_op jit(solution)/shard_map/ppermute | solution.py:436
  307.9 19.0 %collective-permute-start.31 = (bf16[8,2,2,80,128]{4,3,2,1,0:T(8,128)(2,1)S(1)}, bf16[8,2,2,80,128]{4,3,2,1,0:T(8,128)(2,1)S(1)}, u32[]{:S(2)}, u32[]{:S(2)}) collective-permute-start(bf16[8,2,2,80,128]{4,3,2,1,0:T(8,128)(2,1)S(1)} %collective-permute-done.30.refs_3_), channel_id=1, source_target_pairs={{0,1},{1,0},{2,3},{3,2},{4,5},{5,4},{6,7},{7,6},{8,9},{9,8},{10,11... | collective-permute-start | bytes 1966088 | tf_op jit(solution)/shard_map/ppermute | solution.py:436
  (8 other events, 10.0 us)
where the time goes:
time: 344 us; the launch traced here: 343 us
  Pallas kernels  135 us (39%)
  waiting for transfers between devices  120 us (35%)
  starting transfers between devices  51.7 us (15%)
  other arithmetic  26 us (8%)
  local copies, waits for them, and re-layouts  8.2 us (2%)
    ppermute x48, waiting for transfers between devices, swap(): return lax.ppermute(value, axis, pairs)  120 us
    ppermute x48, starting transfers between devices, swap(): return lax.ppermute(value, axis, pairs)  51.7 us
    pallas_call x3, Pallas kernels, zonal_chunk(): pl.pallas_call(lambda *refs: zonal_kernel(*refs, packed=packed, first=fir...  46.9 us
    pallas_call x3, Pallas kernels, down_chunk(): pl.pallas_call(lambda *refs: down_kernel(*refs, tiles=tiles, packed=packe...  41.1 us
    pallas_call x3, Pallas kernels, up_chunk(): pl.pallas_call(lambda *refs: up_kernel(*refs, tiles=tiles, packed=packed,...  39.9 us
    convert_element_type x12, other arithmetic, add(): return sum((v.astype(F32) for v in values)).astype(BF16)  11 us
    pallas_call x1, Pallas kernels, make_table(): pl.pallas_call(table_kernel, out_shape=jax.ShapeDtypeStruct((2, groups, c...  7.34 us
  transfers between devices with their start and end apart: 48, of which 16 were waited for; matrix products, arithmetic and copies ran while one was open for 7% of the time, Pallas kernels for 32%

commit v1 on v0

--- a/solution.py
+++ b/solution.py
@@ -112,6 +112,10 @@
     divisor = 1.0 + helm_coef[:, None, None, None] * (degree * (degree + 1.0))[None, None]
     spec_new = valid_cols[None, None] * (spec + spectral_tendency) / divisor
     return (grid_field, spec_new)
+
+
+SOURCES = (0, 4, 2, 6, 1, 5, 3, 7)
+STEPS = (0, 1, 0, 2, 0, 1, 2, 1, None, 0, 2, 1, 0, 1, 2, 0, 2, 1, 0, 1, 3, 4, 0, 2, 0, 1, 2, 1, 5, 2, 0, 2, 1, 2)
 
 
 def row_of(h, q, d, r):
@@ -312,113 +316,136 @@
     )(jnp.cos(far), jnp.sin(far), jnp.cos(near), jnp.sin(near))
 
 
-def zonal_kernel(place, *refs, packed, first, scale):
-    coefs, rest = refs[:4], list(refs[4:])
-    table, flip, spread, waves, row_waves, forcing = rest[:6]
-    rest = rest[6:] if first else rest[7:]
-    grid, keep, send, weight, lines, force, field, tend, read_sem, write_sem = rest
-    mine, offset = place[1], pl.multiple_of(place[2], 8)
-    parts, groups, per_group, width = table.shape
+def zonal_kernel(place, *refs, packed, first, groups, scale):
+    blocks, rest = pieces_of([ref.at for ref in refs[:4]]), list(refs[4:])
+    table, flip, spread, waves, row_waves, turns, unturns, local, f1, f2, f3 = rest[:11]
+    rest = rest[11:] if first else rest[12:]
+    grid, near_out, far_out, stay, leave = rest[:5]
+    outs = [half.at[n] for half in (stay, leave) for n in range(groups // 2)]
+    weight, values, lines, near, far, field, tend, read_sem, write_sem = rest[5:]
+    mine, offset = place[1], pl.multiple_of(place[2], 16)
+    far_offset = pl.multiple_of(place[3], 16)
+    per_group, width = table.shape[2:]
     count = groups * per_group
     rows = HALF if packed else LANES
-    passes = ((1, 3, 0, 2),) if packed else ((1, 3), (0, 2))
     block = 256
     wave_block = groups // 2
 
-    def force_copy(d):
-        source = forcing.at[mine ^ d, pl.ds(offset, rows), :]
-        return pltpu.make_async_copy(source, force.at[d], read_sem.at[d])
-
-    def grid_copy(d):
-        target = grid.at[mine ^ d, pl.ds(offset, rows), :]
-        return pltpu.make_async_copy(field.at[d], target, write_sem.at[d])
-
-    for d in range(4):
-        force_copy(d).start()
+    reads = [pltpu.make_async_copy(local.at[mine, pl.ds(offset, rows), :], near, read_sem.at[0])]
+    for n, ref in enumerate((f1, f2, f3)):
+        reads.append(
+            pltpu.make_async_copy(ref.at[pl.ds(far_offset, rows), :], far.at[n], read_sem.at[n + 1])
+        )
+    for read in reads:
+        read.start()
     kept = waves[...] < row_waves[...]
     weight[...] = jnp.where(kept, jnp.where(waves[...] == 0, 1.0, 2.0), 0.0).astype(BF16)
-    for fields in passes:
-        for n, d in enumerate(fields):
-            for r in range(2):
+    turned = []
+    for r in range(2):
+        for n in range(groups):
+            here = slice(n * per_group, (n + 1) * per_group)
+            part = blocks[n][...] if packed else blocks[n][r]
+            values[here, :] = part.reshape(per_group, LANES) * weight[here, :]
+        turned.append(dot_nt(flip[r] if packed else flip[...], values[...]))
+    real, imag = turned
+    for d in range(4):
+        here = slice(d * rows, (d + 1) * rows)
+        cos, sin = turns[2 * d : 2 * d + 1, :], turns[2 * d + 1 : 2 * d + 2, :]
+        lines[0, here, :] = (cos * real - sin * imag).astype(BF16)
+        lines[1, here, :] = (sin * real + cos * imag).astype(BF16)
+    for read in reads:
+        read.wait()
+
+    @pl.loop(0, width // block)
+    def _(step):
+        lanes = pl.ds(pl.multiple_of(step * block, block), block)
+        total = dot(lines[0], table[0, :, :, lanes].reshape(count, block))
+        total += dot(lines[1], table[1, :, :, lanes].reshape(count, block))
+        for d in range(4):
+            here = slice(d * rows, (d + 1) * rows)
+            part = total[here]
+            force = far[d - 1, :, lanes].astype(F32) if d else near[:, lanes]
+            if d == 0:
+                field[:, lanes] = part
+            elif d == 1:
+                near_out[:, lanes] = part.astype(BF16)
+            else:
+                far_out[d - 2, :, lanes] = part.astype(BF16)
+            tend[here, lanes] = (force - 0.5 * part * part).astype(BF16)
+
+    write = pltpu.make_async_copy(field, grid.at[mine, pl.ds(offset, rows), :], write_sem)
+    write.start()
+    some = wave_block * per_group
+    for step in range(groups // wave_block):
+        several = slice(step * wave_block, (step + 1) * wave_block)
+        here = slice(step * some, (step + 1) * some)
+        mask = weight[here, :].astype(F32) > 0
+        real = dot_nt(table[0, several].reshape(some, width), tend[...])
+        imag = dot_nt(table[1, several].reshape(some, width), tend[...])
+        sum_real, sum_imag = 0.0, 0.0
+        for n in range(4 * rows // LANES):
+            lanes = slice(n * LANES, (n + 1) * LANES)
+            if packed:
+                low = lax.broadcasted_iota(jnp.int32, (some, LANES), 1) < HALF
+                cos = jnp.where(low, unturns[here, 4 * n : 4 * n + 1], unturns[here, 4 * n + 2 : 4 * n + 3])
+                sin = jnp.where(low, unturns[here, 4 * n + 1 : 4 * n + 2], unturns[here, 4 * n + 3 : 4 * n + 4])
+            else:
+                cos, sin = unturns[here, 2 * n : 2 * n + 1], unturns[here, 2 * n + 1 : 2 * n + 2]
+            sum_real += cos * real[:, lanes] + sin * imag[:, lanes]
+            sum_imag += cos * imag[:, lanes] - sin * real[:, lanes]
+        sums = [(v * scale).astype(BF16) for v in (sum_real, sum_imag)]
+        if packed:
+            parts = [dot(sums[0], spread[0]) + dot(sums[1], spread[1])]
+        else:
+            parts = [dot(v, flip[...]) for v in sums]
+        for r, part in enumerate(parts):
+            part = jnp.where(mask, part, 0.0).astype(BF16)
+            for n in range(wave_block):
+                out = outs[step * wave_block + n]
+                piece = part[n * per_group : (n + 1) * per_group]
                 if packed:
-                    values = coefs[d][...].reshape(count, LANES) * weight[...]
-                    turn = flip[r]
+                    out[...] = piece.reshape(out.shape)
                 else:
-                    values = coefs[d][:, r].reshape(count, LANES) * weight[...]
-                    turn = flip[...]
-                lines[r, n * rows : (n + 1) * rows, :] = dot_nt(turn, values).astype(BF16)
-        for d in fields:
-            force_copy(d).wait()
-
-        @pl.loop(0, width // block)
-        def _(step):
-            lanes = pl.ds(pl.multiple_of(step * block, block), block)
-            total = dot(lines[0], table[0, :, :, lanes].reshape(count, block))
-            total += dot(lines[1], table[1, :, :, lanes].reshape(count, block))
-            for n, d in enumerate(fields):
-                here = slice(n * rows, (n + 1) * rows)
-                part = total[here]
-                field[d, :, lanes] = part
-                tend[here, lanes] = (force[d, :, lanes] - 0.5 * part * part).astype(BF16)
-
-        for d in fields:
-            grid_copy(d).start()
-
-        @pl.loop(0, groups // wave_block)
-        def _(step):
-            several = pl.ds(step * wave_block, wave_block)
-            some = wave_block * per_group
-            mask = weight[pl.ds(pl.multiple_of(step * some, some), some), :].astype(F32) > 0
-            found = []
-            for r in range(2):
-                sums = dot_nt(table[r, several].reshape(some, width), tend[...])
-                found.append((sums * scale).astype(BF16))
-            for n, d in enumerate(fields):
-                target = (keep, send)[d % 2]
-                if packed:
-                    turned = dot(found[0], spread[n, 0]) + dot(found[1], spread[n, 1])
-                    turned = jnp.where(mask, turned, 0.0).astype(BF16)
-                    target[d // 2, several] = turned.reshape((wave_block,) + target.shape[2:])
-                else:
-                    for r in range(2):
-                        turned = dot(found[r][:, n * rows : (n + 1) * rows], flip[...])
-                        turned = jnp.where(mask, turned, 0.0).astype(BF16)
-                        target[d // 2, several, r] = turned.reshape(
-                            (wave_block,) + target.shape[3:]
-                        )
-
-    for d in range(4):
-        grid_copy(d).wait()
-
-
-def zonal_chunk(place, coefs, table, flip, spread, waves, row_waves, forcing, grid, packed, scale):
-    parts, groups, per_group, width = table.shape
+                    out[r] = piece.reshape(out.shape[1:])
+    write.wait()
+
+
+def zonal_chunk(place, arrays, table, setup, waves, turns, forcing, far_forcing, grid, packed, scale):
+    flip, spread, row_waves = setup
+    _, groups, per_group, width = table.shape
     count = groups * per_group
     rows = HALF if packed else LANES
-    batch = 4 * rows if packed else 2 * rows
     first = grid is None
-    sent = jax.ShapeDtypeStruct((2,) + coefs[0].shape, BF16)
+    half = jax.ShapeDtypeStruct(arrays[0].shape, BF16)
     vmem, anywhere = pl.BlockSpec(memory_space=pltpu.VMEM), pl.BlockSpec(memory_space=pl.ANY)
-    operands = [place, *coefs, table, flip, spread, waves, row_waves, forcing]
-    specs = [pl.BlockSpec(memory_space=pltpu.SMEM)] + [vmem] * 9 + [anywhere]
+    operands = [place, *arrays, table, flip, spread, waves, row_waves, turns, turns.T, forcing, *far_forcing]
+    specs = [pl.BlockSpec(memory_space=pltpu.SMEM)] + [vmem] * 11 + [anywhere] * 4
     aliases = {}
     if not first:
         aliases = {len(operands): 0}
         operands.append(grid)
         specs.append(anywhere)
-    return pl.pallas_call(
-        lambda *refs: zonal_kernel(*refs, packed=packed, first=first, scale=scale),
-        out_shape=(jax.ShapeDtypeStruct(forcing.shape, F32), sent, sent),
+    grid, near, far, stay, leave = pl.pallas_call(
+        lambda *refs: zonal_kernel(*refs, packed=packed, first=first, groups=groups, scale=scale),
+        out_shape=(
+            jax.ShapeDtypeStruct(forcing.shape, F32),
+            jax.ShapeDtypeStruct((rows, width), BF16),
+            jax.ShapeDtypeStruct((2, rows, width), BF16),
+            half,
+            half,
+        ),
         in_specs=specs,
-        out_specs=(anywhere, vmem, vmem),
+        out_specs=(anywhere, vmem, vmem, vmem, vmem),
         scratch_shapes=[
             pltpu.VMEM((count, LANES), BF16),
-            pltpu.VMEM((2, batch, count), BF16),
-            pltpu.VMEM((4, rows, width), F32),
-            pltpu.VMEM((4, rows, width), F32),
-            pltpu.VMEM((batch, width), BF16),
+            pltpu.VMEM((count, LANES), BF16),
+            pltpu.VMEM((2, 4 * rows, count), BF16),
+            pltpu.VMEM((rows, width), F32),
+            pltpu.VMEM((3, rows, width), BF16),
+            pltpu.VMEM((rows, width), F32),
+            pltpu.VMEM((4 * rows, width), BF16),
             pltpu.SemaphoreType.DMA((4,)),
-            pltpu.SemaphoreType.DMA((4,)),
+            pltpu.SemaphoreType.DMA,
         ],
         input_output_aliases=aliases,
         compiler_params=pltpu.CompilerParams(vmem_limit_bytes=VMEM_BYTES),
@@ -429,6 +456,34 @@
         ),
         name="zonal",
     )(*operands)
+    return grid, near, far, stay, leave
+
+
+def settle_kernel(place, g1, g2, g3, before, grid, wide, sem):
+    mine, offset = place[1], pl.multiple_of(place[2], 8)
+    rows = g1.shape[0]
+    copies = []
+    for n, ref in enumerate((g1, g2, g3)):
+        wide[n] = ref[...].astype(F32)
+        target = grid.at[mine ^ (n + 1), pl.ds(offset, rows), :]
+        copies.append(pltpu.make_async_copy(wide.at[n], target, sem.at[n]))
+        copies[-1].start()
+    for copy in copies:
+        copy.wait()
+
+
+def settle(place, pieces, grid):
+    vmem, anywhere = pl.BlockSpec(memory_space=pltpu.VMEM), pl.BlockSpec(memory_space=pl.ANY)
+    return pl.pallas_call(
+        settle_kernel,
+        out_shape=jax.ShapeDtypeStruct(grid.shape, F32),
+        in_specs=[pl.BlockSpec(memory_space=pltpu.SMEM), vmem, vmem, vmem, anywhere],
+        out_specs=anywhere,
+        scratch_shapes=[pltpu.VMEM((3,) + pieces[0].shape, F32), pltpu.SemaphoreType.DMA((3,))],
+        input_output_aliases={4: 0},
+        compiler_params=pltpu.CompilerParams(vmem_limit_bytes=VMEM_BYTES),
+        name="settle",
+    )(place, *pieces, grid)
 
 
 def swap(value, axis, bit):
@@ -440,25 +495,36 @@
     return sum(v.astype(F32) for v in values).astype(BF16)
 
 
-def reduce_lon(keep, send):
-    other = swap(send, "lon", 1)
-    away = swap(add(keep[1], other[1]), "lon", 2)
-    return add(keep[0], other[0], away)
-
-
-def gather_lon(own):
-    across = swap(own, "lon", 2)
-    return own, swap(own, "lon", 1), across, swap(across, "lon", 1)
-
-
-def exchange_lat(value, bits):
-    value = value[:, None]
-    for bit in bits:
-        size = value.shape[0] // 2
-        arrived = swap(value[size:], "lat", bit)
-        value = jnp.stack([value[:size], arrived], axis=1)
-        value = value.reshape((size, 2 * value.shape[2]) + value.shape[3:])
-    return value[0]
+def spread_lon(near, far):
+    arrived = swap(far, "lon", 2)
+    return swap(near, "lon", 1), arrived[0], swap(arrived[1], "lon", 1)
+
+
+def pieces_of(arrays):
+    kept, one, two, three = arrays
+    return [kept[0], one[0], two[0], two[2], three[0], three[1], three[2], three[3]]
+
+
+class Turns:
+    def __init__(self):
+        self.last = None
+
+    def run(self, step, *inputs):
+        if self.last is not None:
+            inputs, _ = lax.optimization_barrier((inputs, self.last))
+        found = step(*inputs)
+        self.last = jax.tree.leaves(found)[-1]
+        return found
+
+
+def exchange_lat(run, stay, leave, bits):
+    one = swap(leave, "lat", bits[0])
+    yield
+    two = swap(run(lambda s, a: jnp.concatenate([s[2:], a[2:]]), stay, one), "lat", bits[1])
+    yield
+    leave = run(lambda s, a, b: jnp.stack([s[1], a[1], b[1], b[3]]), stay, one, two)
+    three = swap(leave, "lat", bits[2])
+    return stay, one, two, three
 
 
 def fast_plan(spec, legendre, row_waves, forcing):
@@ -466,7 +532,7 @@
     fields, _, slots, _ = spec.shape
     half_lats, band, width = legendre.shape[2], row_waves.shape[0], forcing.shape[2]
     per_pair, odd = divmod(2 * band, LANES)
-    if (groups, lon_size, fields) != (8, 4, 4) or odd or per_pair % 2 == 0:
+    if (groups, lon_size, fields) != (8, 4, 4) or odd or per_pair != 5:
         return None
     if slots % STEP or half_lats != 4 * band or width % 256 or 2 * slots % STEP:
         return None
@@ -489,7 +555,6 @@
     band, seg_width = row_waves.shape[0], forcing.shape[2]
     length = seg_width * lax.axis_size("lon")
     top = groups // 2
-    bits = [1 << n for n in range(groups.bit_length() - 1)]
 
     my_pairs = lax.dynamic_slice_in_dim(wave_pairs, lat_id * slots, slots)
     columns = lon_id * col_width + jnp.arange(col_width, dtype=jnp.int32)
@@ -503,20 +568,22 @@
     divisor = 1.0 + helm_coef[:, None, None] * (degree * (degree + 1.0))[None]
     inverse = (first_part + second_part)[None] / divisor
 
-    positions = [sum(((p >> n) & 1) << (len(bits) - 1 - n) for n in range(len(bits))) for p in range(groups)]
     grouped = wave_pairs.reshape(groups, slots)
     near_pairs = jnp.stack(
-        [lax.dynamic_index_in_dim(grouped, lat_id ^ e, 0, False) for e in positions]
+        [lax.dynamic_index_in_dim(grouped, lat_id ^ e, 0, False) for e in SOURCES]
     )
     waves = jnp.stack([near_pairs, M - 1 - near_pairs], axis=1).reshape(-1)
-    table = make_table(waves, lon_id * seg_width, seg_width, length, groups)
+    quarter = waves[None] * (lon_id ^ jnp.arange(4, dtype=jnp.int32))[:, None] % 4
+    cosine = jnp.where(quarter == 0, 1, jnp.where(quarter == 2, -1, 0))
+    sine = jnp.where(quarter == 1, 1, jnp.where(quarter == 3, -1, 0))
+    turns = jnp.stack([cosine, sine], axis=1).reshape(8, -1).astype(F32)
 
     south = lat_id >= top
     north = jnp.where(south, groups - 1 - lat_id, lat_id)
     row = jnp.arange(LANES, dtype=jnp.int32)
     place = jnp.stack([lat_id, lon_id])
-    chunks = [(shared_tiles, True, 0)] + [(t, False, n) for n, t in enumerate(full_tiles)]
-    setups = []
+    chunks = [(full_tiles[0], False, 0), (shared_tiles, True, 0), (full_tiles[1], False, 1)]
+    setups, starts = [], []
     for tiles, packed, n in chunks:
         rows = HALF if packed else LANES
         start = band - rows if packed else n * LANES
@@ -526,38 +593,86 @@
         if packed:
             target = HALF * jnp.arange(2)[:, None] + mirrored[None]
             flip = target[..., None] == row
-            spread = [
-                jnp.concatenate([flip[r] if m == k else jnp.zeros_like(flip[r]) for m in range(4)])
-                for k in range(4)
-                for r in range(2)
-            ]
-            spread = jnp.stack(spread).reshape(4, 2, 4 * rows, LANES).astype(BF16)
+            spread = jnp.concatenate([flip, flip], axis=1).astype(BF16)
         else:
             flip = mirrored[:, None] == row
             spread = jnp.zeros((8, LANES), BF16)
         kept = lax.dynamic_slice_in_dim(row_waves, start, rows)
         kept = jnp.sum(jnp.where(flip, kept[:, None], 0), axis=tuple(range(flip.ndim - 1)))
-        spot = jnp.stack([lat_id, lon_id, start]).astype(jnp.int32)
-        setups.append((spot, flip.astype(BF16), spread, kept[None].astype(jnp.int32)))
-
-    scale = 0.5 / math.sqrt(M)
-    grid_field, total = None, None
-    sums = [up_chunk(place, mix, legendre, t, packed, groups, scale) for t, packed, _ in chunks]
-    owns = [exchange_lat(reduce_lon(*s), bits[::-1]) for s in sums]
-    fans = []
-    for (tiles, packed, _), own, (spot, flip, spread, kept) in zip(chunks, owns, setups):
-        coefs = gather_lon(own)
-        grid_field, keep, send = zonal_chunk(
-            spot, coefs, table, flip, spread, waves[:, None], kept, forcing, grid_field, packed, 1.0 / length
+        starts.append(start)
+        setups.append(((flip.astype(BF16), spread, kept[None].astype(jnp.int32))))
+
+    def far_rows(forcing, start, rows):
+        near, *far = [
+            lax.dynamic_slice(forcing, (lon_id ^ d, start, 0), (1, rows, seg_width))[0].astype(BF16)
+            for d in (1, 2, 3)
+        ]
+        return near, jnp.stack(far)
+
+    split = [LANES, band - LANES]
+    after_first = jnp.where(starts[0] == 0, LANES, 0)
+    offsets = [jnp.zeros_like(starts[0])] + [s - after_first for s in starts[1:]]
+    spots = [
+        jnp.stack([lat_id, lon_id, s, o]).astype(jnp.int32) for s, o in zip(starts, offsets)
+    ]
+    turn = Turns()
+    run = turn.run
+    first_force = spread_lon(*run(lambda f: far_rows(f, starts[0], split[0]), forcing))
+    state = {"grid": None, "total": None, "force": None, "table": None}
+
+    def chunk_steps(n):
+        tiles, packed, _ = chunks[n]
+        keep, send = run(
+            lambda p, m, l: up_chunk(p, m, l, tiles, packed, groups, 0.5 / math.sqrt(M)), place, mix, legendre
         )
-        fans.append(gather_lon(exchange_lat(reduce_lon(keep, send), bits)))
-    for n, (tiles, packed, _) in enumerate(chunks):
-        last = n == len(chunks) - 1
-        total = down_chunk(
-            place, fans[n], legendre, factors, total, spec if last else None,
-            inverse if last else None, tiles, packed, groups,
+        yield
+        other_far, other_own = swap(send[1], "lon", 1), swap(send[0], "lon", 1)
+        away = swap(run(lambda k, o: add(k[1], o), keep, other_far), "lon", 2)
+        if n == 2:
+            state["force"] = spread_lon(*run(lambda f: far_rows(f, after_first, split[1]), forcing))
+        yield
+        half = groups // 2
+        stay, leave = run(
+            lambda k, o, a: (add(k[0, :half], o[:half], a[:half]), add(k[0, half:], o[half:], a[half:])),
+            keep, other_own, away,
         )
-    return grid_field, total
+        arrays = yield from exchange_lat(run, stay, leave, (4, 2, 1))
+        yield
+        force = state["force"] if n else first_force
+        grid, near, far, stay, leave = run(
+            lambda *a: zonal_chunk(
+                spots[n], a[:4], a[4], setups[n], waves[:, None], turns, forcing, a[5:], state["grid"], packed, 1.0 / length
+            ),
+            *arrays, state["table"], *force,
+        )
+        state["grid"] = grid
+        settled.append((spots[n], spread_lon(near, far)))
+        arrays = yield from exchange_lat(run, stay, leave, (1, 2, 4))
+        yield
+        own = run(lambda *a: jnp.stack(pieces_of(a)), *arrays)
+        across = swap(own, "lon", 2)
+        fans = own, swap(own, "lon", 1), across, swap(across, "lon", 1)
+        yield
+        state["total"] = run(
+            lambda *a: down_chunk(
+                place, a, legendre, factors, state["total"], spec if n == 2 else None,
+                inverse if n == 2 else None, tiles, packed, groups,
+            ),
+            *fans,
+        )
+        yield
+
+    settled = []
+    walks = [chunk_steps(n) for n in range(3)]
+    for step in STEPS:
+        if step is None:
+            state["table"] = run(lambda w: make_table(w, 0, seg_width, length, groups), waves)
+        elif step < 3:
+            next(walks[step])
+        else:
+            spot, parts = settled[step - 3]
+            state["grid"] = run(lambda *a: settle(spot, a, state["grid"]), *parts)
+    return state["grid"], state["total"]
 
 
 def solution(mesh):

time: 344 us -> 300 us (0.87)
  waiting for transfers between devices: 120 us -> 69 us
  local copies, waits for them, and re-layouts: 8.2 us -> 16 us
  Pallas kernels: 135 us -> 130 us
  starting transfers between devices: 51.7 us -> 56.3 us
    ppermute x48 -> x51, waiting for transfers between devices: 120 us -> 69 us  [swap(): return lax.ppermute(value, axis, pairs)]
    pallas_call x3, Pallas kernels: 46.9 us -> 38 us  [zonal_chunk(): pl.pallas_call(lambda *refs: zonal_kernel(*refs, packed=packed, first=fir...]
    convert_element_type x0 -> x4, local copies, waits for them, and re-layouts: none -> 6.2 us  [the longest x2 5.05 us: far_rows(): lax.dynamic_slice(forcing, (lon_id ^ d, start, 0), (1, rows, seg_width))[0]]
    pallas_call x0 -> x3, Pallas kernels: none -> 5.29 us  [settle(): pl.pallas_call(settle_kernel, out_shape=jax.ShapeDtypeStruct(grid.shape,...]
    squeeze x1 -> x8, local copies, waits for them, and re-layouts: 0.01 us -> 4.97 us  [the longest x3 2.92 us: chunk_steps(): other_far, other_own = (swap(send[1], 'lon', 1), swap(send[0], 'lon', 1))]
    ppermute x48 -> x51, starting transfers between devices: 51.7 us -> 56.3 us  [swap(): return lax.ppermute(value, axis, pairs)]
    unnamed x55 -> x67, local copies, waits for them, and re-layouts: 5.51 us -> 1.68 us
    convert_element_type x12 -> x6, other arithmetic: 11 us -> 8.15 us  [add(): return sum((v.astype(F32) for v in values)).astype(BF16)]
  transfers between devices with their start and end apart: 48 -> 51, of which waited for: 16 -> 15; matrix products, arithmetic and copies ran while one was open for 7% -> 12% of each run, Pallas kernels for 32% -> 38%
where the time goes in v1:
time: 300 us; the launch traced here: 296 us
  Pallas kernels  130 us (43%)
  waiting for transfers between devices  69 us (23%)
  starting transfers between devices  56.3 us (19%)
  other arithmetic  22.9 us (8%)
  local copies, waits for them, and re-layouts  16 us (5%)
    ppermute x51, waiting for transfers between devices, swap(): return lax.ppermute(value, axis, pairs)  69 us
    ppermute x51, starting transfers between devices, swap(): return lax.ppermute(value, axis, pairs)  56.3 us
    pallas_call x3, Pallas kernels, down_chunk(): pl.pallas_call(lambda *refs: down_kernel(*refs, tiles=tiles, packed=packe...  41.3 us
    pallas_call x3, Pallas kernels, zonal_chunk(): pl.pallas_call(lambda *refs: zonal_kernel(*refs, packed=packed, first=fir...  38 us
    pallas_call x3, Pallas kernels, up_chunk(): pl.pallas_call(lambda *refs: up_kernel(*refs, tiles=tiles, packed=packed,...  37.6 us
    convert_element_type x6, other arithmetic, add(): return sum((v.astype(F32) for v in values)).astype(BF16)  8.15 us
    pallas_call x1, Pallas kernels, make_table(): pl.pallas_call(table_kernel, out_shape=jax.ShapeDtypeStruct((2, groups, c...  7.48 us
  transfers between devices with their start and end apart: 51, of which 15 were waited for; matrix products, arithmetic and copies ran while one was open for 12% of the time, Pallas kernels for 38%

profile of v1, /device:TPU:1, one launch (start us, length us, event | category | flops | bytes accessed | tf_op | source)
XLA Modules:
  0.0 295.9 jit_solution(7457944238841833635)
XLA Ops:
  0.7 2.3 fusion.20
  3.9 2.0 collective-permute-start.17
  9.2 1.7 multiply_bitcast_fusion.refs_1_
  10.9 14.7 %legendre_up.3 = (bf16[2,8,2,2,80,128]{5,4,3,2,1,0:T(8,128)(2,1)S(1)}, bf16[2,8,2,2,80,128]{5,4,3,2,1,0:T(8,128)(2,1)S(1)}) custom-call(s32[2]{0:T(128)S(1)} %pad_add_fusion.3.refs_0_, bf16[80,32,336]{2,1,0:T(8,128)(2,1)} %multiply_bitcast_fusion.refs_1_, bf16[80,336,1280]{2,1,0:T(8,128)(2,1)} %refs_8_.3, bf16[80,336,1280]{2,1,0:T(8,128)(2,1)} %refs_8_.3, ...), custom_call_target="tpu_custom_call" | custom-call | flops 7046430720 | bytes 27525120 | tf_op jit(solution)/shard_map/legendre_up/pallas_call | solution.py:182
  28.0 8.7 %legendre_up.4 = (bf16[2,8,2,80,128]{4,3,2,1,0:T(8,128)(2,1)S(1)}, bf16[2,8,2,80,128]{4,3,2,1,0:T(8,128)(2,1)S(1)}) custom-call(s32[2]{0:T(128)S(1)} %pad_add_fusion.3.refs_0_, bf16[80,32,336]{2,1,0:T(8,128)(2,1)S(1)} %copy-done, bf16[80,336,1280]{2,1,0:T(8,128)(2,1)} %refs_8_.3, bf16[80,336,1280]{2,1,0:T(8,128)(2,1)} %refs_8_.3), custom_call_target="tpu_custom_call" | custom-call | flops 3523215360 | bytes 13762560 | tf_op jit(solution)/shard_map/legendre_up/pallas_call | solution.py:182
  38.9 1.2 broadcast_in_dim_reshape.3.refs_8_
  40.3 1.1 copy.24
  42.3 1.3 fusion.1
  43.7 14.2 %legendre_up.5 = (bf16[2,8,2,2,80,128]{5,4,3,2,1,0:T(8,128)(2,1)S(1)}, bf16[2,8,2,2,80,128]{5,4,3,2,1,0:T(8,128)(2,1)S(1)}) custom-call(s32[2]{0:T(128)S(1)} %pad_add_fusion.3.refs_0_, bf16[80,32,336]{2,1,0:T(8,128)(2,1)} %multiply_bitcast_fusion.refs_1_, bf16[80,336,1280]{2,1,0:T(8,128)(2,1)} %refs_8_.3, bf16[80,336,1280]{2,1,0:T(8,128)(2,1)} %refs_8_.3, ...), custom_call_target="tpu_custom_call" | custom-call | flops 7046430720 | bytes 27525120 | tf_op jit(solution)/shard_map/legendre_up/pallas_call | solution.py:182
  57.9 1.1 slice_bitcast_fusion.1
  59.5 1.9 slice_bitcast_fusion.10
  61.9 2.1 fusion.9
  64.1 1.1 fusion.10
  65.2 1.8 collective-permute-start.9
  67.0 1.0 fusion
  68.0 2.7 fusion.18
  70.8 1.0 pad_maximum_fusion
  71.8 2.3 collective-permute-start.7
  74.7 1.2 collective-permute-start.6
  75.8 1.1 fusion.22
  77.1 1.1 copy.23
  78.2 3.6 %multiply_sine_fusion = (f32[1280,10]{1,0:T(8,128)S(1)}, f32[1280,10]{1,0:T(8,128)S(1)}) fusion(f32[1280,10]{1,0:T(8,128)} %copy.23), kind=kLoop, calls=%fused_computation.40 | loop fusion | flops 12800 | bytes 153600 | tf_op jit(solution)/shard_map/sin | solution.py:316
  81.8 2.7 fusion.15
  84.5 7.5 %zonal_table.1.refs_5_ = bf16[2,8,160,1280]{3,2,1,0:T(8,128)(2,1)} custom-call(f32[1280,10]{1,0:T(8,128)S(1)} %get-tuple-element.321.cos_far, f32[1280,10]{1,0:T(8,128)S(1)} %get-tuple-element.320.sin_far, f32[1280,128]{1,0:T(8,128)S(1)} %get-tuple-element.341.cos_near, f32[1280,128]{1,0:T(8,128)S(1)} %get-tuple-element.340.sin_near), custom_call_target="tpu_custom_call" | custom-call | tf_op jit(solution)/shard_map/zonal_table/pallas_call | solution.py:308
  92.5 2.3 collective-permute-start.11
  94.9 1.3 collective-permute-start.13
  96.2 1.5 fusion.5
  97.7 3.4 %collective-permute-done.11.refs_2_ = bf16[4,2,80,128]{3,2,1,0:T(8,128)(2,1)S(1)} collective-permute-done((bf16[4,2,80,128]{3,2,1,0:T(8,128)(2,1)S(1)}, bf16[4,2,80,128]{3,2,1,0:T(8,128)(2,1)S(1)}, u32[]{:S(2)}, u32[]{:S(2)}) %collective-permute-start.11) | collective-permute-done | bytes 163872 | tf_op jit(solution)/shard_map/ppermute | solution.py:491
  101.2 6.7 %collective-permute-done.13.refs_3_ = bf16[4,2,2,80,128]{4,3,2,1,0:T(8,128)(2,1)S(1)} collective-permute-done((bf16[4,2,2,80,128]{4,3,2,1,0:T(8,128)(2,1)S(1)}, bf16[4,2,2,80,128]{4,3,2,1,0:T(8,128)(2,1)S(1)}, u32[]{:S(2)}, u32[]{:S(2)}) %collective-permute-start.13) | collective-permute-done | bytes 327712 | tf_op jit(solution)/shard_map/ppermute | solution.py:491
  108.0 6.2 %collective-permute-done.12.refs_3_ = bf16[4,2,80,128]{3,2,1,0:T(8,128)(2,1)S(1)} collective-permute-done((bf16[4,2,80,128]{3,2,1,0:T(8,128)(2,1)S(1)}, bf16[4,2,80,128]{3,2,1,0:T(8,128)(2,1)S(1)}, u32[]{:S(2)}, u32[]{:S(2)}) %collective-permute-start.12) | collective-permute-done | bytes 163872 | tf_op jit(solution)/shard_map/ppermute | solution.py:491
  114.1 1.2 collective-permute-start.15
  116.2 5.2 %collective-permute-start.20 = (bf16[192,1280]{1,0:T(8,128)(2,1)S(1)}, bf16[192,1280]{1,0:T(8,128)(2,1)S(1)}, u32[]{:S(2)}, u32[]{:S(2)}) collective-permute-start(bf16[192,1280]{1,0:T(8,128)(2,1)S(1)} %copy-done.11), channel_id=1, source_target_pairs={{0,1},{1,0},{2,3},{3,2},{4,5},{5,4},{6,7},{7,6},{8,9},{9,8},{10,11... | collective-permute-start | bytes 1474568 | tf_op jit(solution)/shard_map/ppermute | solution.py:491
  121.9 6.8 %collective-permute-start.22 = (bf16[192,1280]{1,0:T(8,128)(2,1)S(1)}, bf16[192,1280]{1,0:T(8,128)(2,1)S(1)}, u32[]{:S(2)}, u32[]{:S(2)}) collective-permute-start(bf16[192,1280]{1,0:T(8,128)(2,1)S(1)} %get-tuple-element.308), channel_id=1, source_target_pairs={{0,1},{1,0},{2,3},{3,2},{4,5},{5,4},{6,7},{7,6},{8,9},{9,8},{10,11... | collective-permute-start | bytes 1474568 | tf_op jit(solution)/shard_map/ppermute | solution.py:491
  128.8 13.4 %zonal.3 = (f32[4,320,1280]{2,1,0:T(8,128)}, bf16[128,1280]{1,0:T(8,128)(2,1)S(1)}, bf16[2,128,1280]{2,1,0:T(8,128)(2,1)S(1)}, bf16[4,2,2,80,128]{4,3,2,1,0:T(8,128)(2,1)S(1)}, bf16[4,2,2,80,128]{4,3,2,1,0:T(8,128)(2,1)S(1)}) custom-call(s32[4]{0:T(128)S(1)} %pad_add_fusion.4.refs_0_.place, bf16[4,2,2,80,128]{4,3,2,1,0:T(8,128)(2,1)S(1)} %get-tuple-element.180.refs_1_, ...), custom_call_target="tpu_custom_call" | custom-call | flops 6710886400 | bytes 11796480 | tf_op jit(solution)/shard_map/zonal/pallas_call | solution.py:428
  142.2 1.3 collective-permute-start.23
  143.4 1.2 collective-permute-start.30
  145.4 10.1 %zonal.4 = (f32[4,320,1280]{2,1,0:T(8,128)}, bf16[64,1280]{1,0:T(8,128)(2,1)S(1)}, bf16[2,64,1280]{2,1,0:T(8,128)(2,1)S(1)}, bf16[4,2,80,128]{3,2,1,0:T(8,128)(2,1)S(1)}, bf16[4,2,80,128]{3,2,1,0:T(8,128)(2,1)S(1)}) custom-call(s32[4]{0:T(128)S(1)} %pad_add_fusion.5.refs_0_.place, ...), custom_call_target="tpu_custom_call", output_to_operand_aliasing={{0}: (16, {})} | custom-call | flops 3355443200 | bytes 9175040 | tf_op jit(solution)/shard_map/zonal/pallas_call | solution.py:428
  156.8 2.7 collective-permute-done.30
  159.5 7.0 %collective-permute-done.27 = bf16[2,64,1280]{2,1,0:T(8,128)(2,1)S(1)} collective-permute-done((bf16[2,64,1280]{2,1,0:T(8,128)(2,1)S(1)}, bf16[2,64,1280]{2,1,0:T(8,128)(2,1)S(1)}, u32[]{:S(2)}, u32[]{:S(2)}) %collective-permute-start.27) | collective-permute-done | bytes 327712 | tf_op jit(solution)/shard_map/ppermute | solution.py:491
  166.5 1.1 collective-permute-start.31
  168.9 1.9 settle.3.before
  170.8 1.5 settle.4.refs_16_
  172.4 1.1 collective-permute-start.37
  173.6 3.1 %collective-permute-done.19.refs_4_ = bf16[4,2,2,80,128]{4,3,2,1,0:T(8,128)(2,1)S(1)} collective-permute-done((bf16[4,2,2,80,128]{4,3,2,1,0:T(8,128)(2,1)S(1)}, bf16[4,2,2,80,128]{4,3,2,1,0:T(8,128)(2,1)S(1)}, u32[]{:S(2)}, u32[]{:S(2)}) %collective-permute-start.19) | collective-permute-done | bytes 327712 | tf_op jit(solution)/shard_map/ppermute | solution.py:491
  176.7 14.5 %zonal.5 = (f32[4,320,1280]{2,1,0:T(8,128)}, bf16[128,1280]{1,0:T(8,128)(2,1)S(1)}, bf16[2,128,1280]{2,1,0:T(8,128)(2,1)}, bf16[4,2,2,80,128]{4,3,2,1,0:T(8,128)(2,1)S(1)}, bf16[4,2,2,80,128]{4,3,2,1,0:T(8,128)(2,1)S(1)}) custom-call(s32[4]{0:T(128)S(1)} %pad_add_fusion.1.refs_0_.place, ...), custom_call_target="tpu_custom_call", output_to_operand_aliasing={{0}: (16, {})} | custom-call | flops 6710886400 | bytes 11796480 | tf_op jit(solution)/shard_map/zonal/pallas_call | solution.py:428
  191.8 1.1 collective-permute-start.38
  192.9 1.2 collective-permute-start.34
  194.1 2.2 collective-permute-start.33
  196.6 2.6 collective-permute-done.39
  199.2 2.3 collective-permute-start.42
  201.7 5.6 %collective-permute-done.34 = bf16[2,128,1280]{2,1,0:T(8,128)(2,1)S(1)} collective-permute-done((bf16[2,128,1280]{2,1,0:T(8,128)(2,1)S(1)}, bf16[2,128,1280]{2,1,0:T(8,128)(2,1)S(1)}, u32[]{:S(2)}, u32[]{:S(2)}) %collective-permute-start.34) | collective-permute-done | bytes 655392 | tf_op jit(solution)/shard_map/ppermute | solution.py:491
  207.3 5.3 %collective-permute-start.35 = (bf16[128,1280]{1,0:T(8,128)(2,1)S(1)}, bf16[128,1280]{1,0:T(8,128)(2,1)S(1)}, u32[]{:S(2)}, u32[]{:S(2)}) collective-permute-start(bf16[128,1280]{1,0:T(8,128)(2,1)S(1)} %get-tuple-element.314), channel_id=1, source_target_pairs={{0,1},{1,0},{2,3},{3,2},{4,5},{5,4},{6,7},{7,6},{8,9},{9,8},{10,11... | collective-permute-start | bytes 983048 | tf_op jit(solution)/shard_map/ppermute | solution.py:491
  212.6 8.7 %collective-permute-done.43.refs_3_ = bf16[8,2,2,80,128]{4,3,2,1,0:T(8,128)(2,1)S(1)} collective-permute-done((bf16[8,2,2,80,128]{4,3,2,1,0:T(8,128)(2,1)S(1)}, bf16[8,2,2,80,128]{4,3,2,1,0:T(8,128)(2,1)S(1)}, u32[]{:S(2)}, u32[]{:S(2)}) %collective-permute-start.43) | collective-permute-done | bytes 655392 | tf_op jit(solution)/shard_map/ppermute | solution.py:491
  221.3 2.8 collective-permute-start.44
  224.2 1.9 settle.5
  226.2 1.4 collective-permute-start.41
  227.6 15.5 %legendre_down.3.refs_8_ = f32[4,2,80,336]{3,2,1,0:T(8,128)S(1)} custom-call(s32[2]{0:T(128)S(1)} %pad_add_fusion.3.refs_0_, bf16[8,2,2,80,128]{4,3,2,1,0:T(8,128)(2,1)S(1)} %constant_dynamic-update-slice_fusion.8.refs_1_, bf16[8,2,2,80,128]{4,3,2,1,0:T(8,128)(2,1)S(1)} %collective-permute-done.42.refs_2_, ...), custom_call_target="tpu_custom_call" | custom-call | flops 7046430720 | bytes 27525120 | tf_op jit(solution)/shard_map/legendre_down/pallas_call | solution.py:268
  243.3 1.3 collective-permute-start.46
  244.9 1.0 collective-permute-start.48
  245.9 20.4 %collective-permute-done.49.refs_3_ = bf16[8,2,80,128]{3,2,1,0:T(8,128)(2,1)S(1)} collective-permute-done((bf16[8,2,80,128]{3,2,1,0:T(8,128)(2,1)S(1)}, bf16[8,2,80,128]{3,2,1,0:T(8,128)(2,1)S(1)}, u32[]{:S(2)}, u32[]{:S(2)}) %collective-permute-start.49) | collective-permute-done | bytes 327712 | tf_op jit(solution)/shard_map/ppermute | solution.py:491
  266.3 1.3 collective-permute-start.50
  268.8 9.7 %legendre_down.4.refs_10_ = f32[4,2,80,336]{3,2,1,0:T(8,128)S(1)} custom-call(s32[2]{0:T(128)S(1)} %pad_add_fusion.3.refs_0_, bf16[8,2,80,128]{3,2,1,0:T(8,128)(2,1)S(1)} %constant_dynamic-update-slice_fusion.9.refs_1_, bf16[8,2,80,128]{3,2,1,0:T(8,128)(2,1)S(1)} %collective-permute-done.48.refs_2_, ...), custom_call_target="tpu_custom_call" | custom-call | flops 3523215360 | bytes 13762560 | tf_op jit(solution)/shard_map/legendre_down/pallas_call | solution.py:268
  278.5 1.0 copy-done.1
  279.5 16.2 %legendre_down.5 = f32[4,2,80,336]{3,2,1,0:T(8,128)} custom-call(s32[2]{0:T(128)S(1)} %pad_add_fusion.3.refs_0_, bf16[8,2,2,80,128]{4,3,2,1,0:T(8,128)(2,1)S(1)} %constant_dynamic-update-slice_fusion.14.refs_1_, bf16[8,2,2,80,128]{4,3,2,1,0:T(8,128)(2,1)S(1)} %collective-permute-done.45.refs_2_, ...), custom_call_target="tpu_custom_call" | custom-call | flops 7046430720 | bytes 27525120 | tf_op jit(solution)/shard_map/legendre_down/pallas_call | solution.py:268
  (227 shorter events, 19.5 us)
Async XLA Ops:
  0.7 5.9 %copy-start.17 = (s32[640]{0:T(1024)S(1)}, s32[640]{0:T(1024)}, u32[]{:S(2)}) copy-start(s32[640]{0:T(1024)} %param.8) | copy-start | bytes 7684
  3.0 5.3 %copy-start.9 = (f32[4,2,80,336]{3,2,1,0:T(8,128)S(1)}, f32[4,2,80,336]{3,2,1,0:T(8,128)}, u32[]{:S(2)}) copy-start(f32[4,2,80,336]{3,2,1,0:T(8,128)} %refs_11_.1) | copy-start | bytes 2580484
  3.9 55.1 %collective-permute-start.17 = (bf16[2,128,1280]{2,1,0:T(8,128)(2,1)}, bf16[2,128,1280]{2,1,0:T(8,128)(2,1)}, u32[]{:S(2)}, u32[]{:S(2)}) collective-permute-start(bf16[2,128,1280]{2,1,0:T(8,128)(2,1)} %pad_maximum_fusion.1), channel_id=1, source_target_pairs={{0,2},{1,3},{2,0},{3,1},{4,6},{5,7},{6,4},{7,5},{8,10},{9,11},{10,... | collective-permute-start | bytes 1966088 | tf_op jit(solution)/shard_map/ppermute | solution.py:491
  27.0 15.3 %collective-permute-start = (bf16[8,2,2,80,128]{4,3,2,1,0:T(8,128)(2,1)S(1)}, bf16[8,2,2,80,128]{4,3,2,1,0:T(8,128)(2,1)}, u32[]{:S(2)}, u32[]{:S(2)}) collective-permute-start(bf16[8,2,2,80,128]{4,3,2,1,0:T(8,128)(2,1)S(1)} %get-tuple-element.305), channel_id=1, source_target_pairs={{0,1},{1,0},{2,3},{3,2},{4,5},{5,4},{6,7},{7,6},{8,9},{9,8},{10,11... | collective-permute-start | bytes 1966088 | tf_op jit(solution)/shard_map/ppermute | solution.py:491
  27.9 33.5 %collective-permute-start.4 = (bf16[8,2,2,80,128]{4,3,2,1,0:T(8,128)(2,1)}, bf16[8,2,2,80,128]{4,3,2,1,0:T(8,128)(2,1)}, u32[]{:S(2)}, u32[]{:S(2)}) collective-permute-start(bf16[8,2,2,80,128]{4,3,2,1,0:T(8,128)(2,1)} %get-tuple-element.304), channel_id=1, source_target_pairs={{0,1},{1,0},{2,3},{3,2},{4,5},{5,4},{6,7},{7,6},{8,9},{9,8},{10,11... | collective-permute-start | bytes 1966088 | tf_op jit(solution)/shard_map/ppermute | solution.py:491
  37.6 26.5 %collective-permute-start.3 = (bf16[8,2,80,128]{3,2,1,0:T(8,128)(2,1)}, bf16[8,2,80,128]{3,2,1,0:T(8,128)(2,1)}, u32[]{:S(2)}, u32[]{:S(2)}) collective-permute-start(bf16[8,2,80,128]{3,2,1,0:T(8,128)(2,1)} %get-tuple-element.323), channel_id=1, source_target_pairs={{0,1},{1,0},{2,3},{3,2},{4,5},{5,4},{6,7},{7,6},{8,9},{9,8},{10,11... | collective-permute-start | bytes 983048 | tf_op jit(solution)/shard_map/ppermute | solution.py:491
  38.5 33.3 %collective-permute-start.8 = (bf16[8,2,80,128]{3,2,1,0:T(8,128)(2,1)}, bf16[8,2,80,128]{3,2,1,0:T(8,128)(2,1)}, u32[]{:S(2)}, u32[]{:S(2)}) collective-permute-start(bf16[8,2,80,128]{3,2,1,0:T(8,128)(2,1)} %get-tuple-element.322), channel_id=1, source_target_pairs={{0,1},{1,0},{2,3},{3,2},{4,5},{5,4},{6,7},{7,6},{8,9},{9,8},{10,11... | collective-permute-start | bytes 983048 | tf_op jit(solution)/shard_map/ppermute | solution.py:491
  43.6 17.8 %collective-permute-start.5 = (bf16[8,2,2,80,128]{4,3,2,1,0:T(8,128)(2,1)S(1)}, bf16[8,2,2,80,128]{4,3,2,1,0:T(8,128)(2,1)S(1)}, u32[]{:S(2)}, u32[]{:S(2)}) collective-permute-start(bf16[8,2,2,80,128]{4,3,2,1,0:T(8,128)(2,1)S(1)} %fusion.1), channel_id=1, source_target_pairs={{0,2},{1,3},{2,0},{3,1},{4,6},{5,7},{6,4},{7,5},{8,10},{9,11},{10,... | collective-permute-start | bytes 1966088 | tf_op jit(solution)/shard_map/ppermute | solution.py:491
  57.9 9.1 %copy-start.5 = (bf16[2,8,2,2,80,128]{5,4,3,2,1,0:T(8,128)(2,1)}, bf16[2,8,2,2,80,128]{5,4,3,2,1,0:T(8,128)(2,1)S(1)}, u32[]{:S(2)}) copy-start(bf16[2,8,2,2,80,128]{5,4,3,2,1,0:T(8,128)(2,1)S(1)} %get-tuple-element.167) | copy-start | bytes 3932164
  59.0 6.2 %collective-permute-start.2 = (bf16[8,2,2,80,128]{4,3,2,1,0:T(8,128)(2,1)S(1)}, bf16[8,2,2,80,128]{4,3,2,1,0:T(8,128)(2,1)S(1)}, u32[]{:S(2)}, u32[]{:S(2)}) collective-permute-start(bf16[8,2,2,80,128]{4,3,2,1,0:T(8,128)(2,1)S(1)} %get-tuple-element.306), channel_id=1, source_target_pairs={{0,1},{1,0},{2,3},{3,2},{4,5},{5,4},{6,7},{7,6},{8,9},{9,8},{10,11... | collective-permute-start | bytes 1966088 | tf_op jit(solution)/shard_map/ppermute | solution.py:491
  61.4 60.1 %collective-permute-start.16 = (bf16[128,1280]{1,0:T(8,128)(2,1)}, bf16[128,1280]{1,0:T(8,128)(2,1)}, u32[]{:S(2)}, u32[]{:S(2)}) collective-permute-start(bf16[128,1280]{1,0:T(8,128)(2,1)} %get-tuple-element.295), channel_id=1, source_target_pairs={{0,1},{1,0},{2,3},{3,2},{4,5},{5,4},{6,7},{7,6},{8,9},{9,8},{10,11... | collective-permute-start | bytes 983048 | tf_op jit(solution)/shard_map/ppermute | solution.py:491
  61.4 31.1 %collective-permute-start.1 = (bf16[8,2,2,80,128]{4,3,2,1,0:T(8,128)(2,1)}, bf16[8,2,2,80,128]{4,3,2,1,0:T(8,128)(2,1)}, u32[]{:S(2)}, u32[]{:S(2)}) collective-permute-start(bf16[8,2,2,80,128]{4,3,2,1,0:T(8,128)(2,1)} %get-tuple-element.307), channel_id=1, source_target_pairs={{0,1},{1,0},{2,3},{3,2},{4,5},{5,4},{6,7},{7,6},{8,9},{9,8},{10,11... | collective-permute-start | bytes 1966088 | tf_op jit(solution)/shard_map/ppermute | solution.py:491
  64.1 57.8 %collective-permute-start.18 = (bf16[128,1280]{1,0:T(8,128)(2,1)}, bf16[128,1280]{1,0:T(8,128)(2,1)}, u32[]{:S(2)}, u32[]{:S(2)}) collective-permute-start(bf16[128,1280]{1,0:T(8,128)(2,1)} %get-tuple-element.318), channel_id=1, source_target_pairs={{0,1},{1,0},{2,3},{3,2},{4,5},{5,4},{6,7},{7,6},{8,9},{9,8},{10,11... | collective-permute-start | bytes 983048 | tf_op jit(solution)/shard_map/ppermute | solution.py:491
  65.2 9.5 %collective-permute-start.9 = (bf16[8,2,80,128]{3,2,1,0:T(8,128)(2,1)S(1)}, bf16[8,2,80,128]{3,2,1,0:T(8,128)(2,1)S(1)}, u32[]{:S(2)}, u32[]{:S(2)}) collective-permute-start(bf16[8,2,80,128]{3,2,1,0:T(8,128)(2,1)S(1)} %fusion.10), channel_id=1, source_target_pairs={{0,2},{1,3},{2,0},{3,1},{4,6},{5,7},{6,4},{7,5},{8,10},{9,11},{10,... | collective-permute-start | bytes 983048 | tf_op jit(solution)/shard_map/ppermute | solution.py:491
  71.8 20.3 %collective-permute-start.7 = (bf16[4,2,2,80,128]{4,3,2,1,0:T(8,128)(2,1)}, bf16[4,2,2,80,128]{4,3,2,1,0:T(8,128)(2,1)S(1)}, u32[]{:S(2)}, u32[]{:S(2)}) collective-permute-start(bf16[4,2,2,80,128]{4,3,2,1,0:T(8,128)(2,1)} %get-tuple-element.301), channel_id=1, source_target_pairs={{0,16},{4,20},{8,24},{12,28},{16,0},{20,4},{24,8},{28,12},{1,17},{... | collective-permute-start | bytes 983048 | tf_op jit(solution)/shard_map/ppermute | solution.py:491
  74.7 20.2 %collective-permute-start.6 = (bf16[8,2,2,80,128]{4,3,2,1,0:T(8,128)(2,1)}, bf16[8,2,2,80,128]{4,3,2,1,0:T(8,128)(2,1)}, u32[]{:S(2)}, u32[]{:S(2)}) collective-permute-start(bf16[8,2,2,80,128]{4,3,2,1,0:T(8,128)(2,1)} %fusion), channel_id=1, source_target_pairs={{0,2},{1,3},{2,0},{3,1},{4,6},{5,7},{6,4},{7,5},{8,10},{9,11},{10,... | collective-permute-start | bytes 1966088 | tf_op jit(solution)/shard_map/ppermute | solution.py:491
  84.5 7.5 %copy-start.10 = (bf16[2,192,1280]{2,1,0:T(8,128)(2,1)S(1)}, bf16[2,192,1280]{2,1,0:T(8,128)(2,1)}, u32[]{:S(2)}) copy-start(bf16[2,192,1280]{2,1,0:T(8,128)(2,1)} %pad_maximum_fusion) | copy-start | bytes 2949124
  92.1 15.8 %copy-start.7 = (bf16[4,2,2,80,128]{4,3,2,1,0:T(8,128)(2,1)}, bf16[4,2,2,80,128]{4,3,2,1,0:T(8,128)(2,1)S(1)}, u32[]{:S(2)}) copy-start(bf16[4,2,2,80,128]{4,3,2,1,0:T(8,128)(2,1)S(1)} %collective-permute-done.7.refs_2_) | copy-start | bytes 983044
  92.1 29.8 %collective-permute-start.21 = (bf16[2,192,1280]{2,1,0:T(8,128)(2,1)S(1)}, bf16[2,192,1280]{2,1,0:T(8,128)(2,1)S(1)}, u32[]{:S(2)}, u32[]{:S(2)}) collective-permute-start(bf16[2,192,1280]{2,1,0:T(8,128)(2,1)S(1)} %copy-done.10), channel_id=1, source_target_pairs={{0,2},{1,3},{2,0},{3,1},{4,6},{5,7},{6,4},{7,5},{8,10},{9,11},{10,... | collective-permute-start | bytes 2949128 | tf_op jit(solution)/shard_map/ppermute | solution.py:491
  92.5 8.6 %collective-permute-start.11 = (bf16[4,2,80,128]{3,2,1,0:T(8,128)(2,1)S(1)}, bf16[4,2,80,128]{3,2,1,0:T(8,128)(2,1)S(1)}, u32[]{:S(2)}, u32[]{:S(2)}) collective-permute-start(bf16[4,2,80,128]{3,2,1,0:T(8,128)(2,1)S(1)} %get-tuple-element.303), channel_id=1, source_target_pairs={{0,16},{4,20},{8,24},{12,28},{16,0},{20,4},{24,8},{28,12},{1,17},{... | collective-permute-start | bytes 491528 | tf_op jit(solution)/shard_map/ppermute | solution.py:491
  94.9 13.0 %collective-permute-start.13 = (bf16[4,2,2,80,128]{4,3,2,1,0:T(8,128)(2,1)S(1)}, bf16[4,2,2,80,128]{4,3,2,1,0:T(8,128)(2,1)S(1)}, u32[]{:S(2)}, u32[]{:S(2)}) collective-permute-start(bf16[4,2,2,80,128]{4,3,2,1,0:T(8,128)(2,1)S(1)} %pad_maximum_fusion.4), channel_id=1, source_target_pairs={{0,8},{4,12},{8,0},{12,4},{16,24},{20,28},{24,16},{28,20},{1,9},{5... | collective-permute-start | bytes 983048 | tf_op jit(solution)/shard_map/ppermute | solution.py:491
  101.1 15.1 %collective-permute-start.10 = (bf16[4,2,2,80,128]{4,3,2,1,0:T(8,128)(2,1)S(1)}, bf16[4,2,2,80,128]{4,3,2,1,0:T(8,128)(2,1)S(1)}, u32[]{:S(2)}, u32[]{:S(2)}) collective-permute-start(bf16[4,2,2,80,128]{4,3,2,1,0:T(8,128)(2,1)S(1)} %get-tuple-element.298), channel_id=1, source_target_pairs={{0,16},{4,20},{8,24},{12,28},{16,0},{20,4},{24,8},{28,12},{1,17},{... | collective-permute-start | bytes 983048 | tf_op jit(solution)/shard_map/ppermute | solution.py:491
  101.1 15.1 %copy-start.11 = (bf16[192,1280]{1,0:T(8,128)(2,1)S(1)}, bf16[192,1280]{1,0:T(8,128)(2,1)}, u32[]{:S(2)}) copy-start(bf16[192,1280]{1,0:T(8,128)(2,1)} %get-tuple-element.292) | copy-start | bytes 1474564
  107.9 6.3 %collective-permute-start.12 = (bf16[4,2,80,128]{3,2,1,0:T(8,128)(2,1)S(1)}, bf16[4,2,80,128]{3,2,1,0:T(8,128)(2,1)S(1)}, u32[]{:S(2)}, u32[]{:S(2)}) collective-permute-start(bf16[4,2,80,128]{3,2,1,0:T(8,128)(2,1)S(1)} %pad_maximum_fusion.12), channel_id=1, source_target_pairs={{0,8},{4,12},{8,0},{12,4},{16,24},{20,28},{24,16},{28,20},{1,9},{5... | collective-permute-start | bytes 491528 | tf_op jit(solution)/shard_map/ppermute | solution.py:491
  114.1 7.7 %collective-permute-start.15 = (bf16[4,2,2,80,128]{4,3,2,1,0:T(8,128)(2,1)S(1)}, bf16[4,2,2,80,128]{4,3,2,1,0:T(8,128)(2,1)S(1)}, u32[]{:S(2)}, u32[]{:S(2)}) collective-permute-start(bf16[4,2,2,80,128]{4,3,2,1,0:T(8,128)(2,1)S(1)} %pad_maximum_fusion.5), channel_id=1, source_target_pairs={{0,4},{4,0},{8,12},{12,8},{16,20},{20,16},{24,28},{28,24},{1,5},{5... | collective-permute-start | bytes 983048 | tf_op jit(solution)/shard_map/ppermute | solution.py:491
  116.2 28.6 %collective-permute-start.20 = (bf16[192,1280]{1,0:T(8,128)(2,1)S(1)}, bf16[192,1280]{1,0:T(8,128)(2,1)S(1)}, u32[]{:S(2)}, u32[]{:S(2)}) collective-permute-start(bf16[192,1280]{1,0:T(8,128)(2,1)S(1)} %copy-done.11), channel_id=1, source_target_pairs={{0,1},{1,0},{2,3},{3,2},{4,5},{5,4},{6,7},{7,6},{8,9},{9,8},{10,11... | collective-permute-start | bytes 1474568 | tf_op jit(solution)/shard_map/ppermute | solution.py:491
  121.4 7.3 %copy-start.8 = (bf16[4,2,2,80,128]{4,3,2,1,0:T(8,128)(2,1)S(1)}, bf16[4,2,2,80,128]{4,3,2,1,0:T(8,128)(2,1)}, u32[]{:S(2)}) copy-start(bf16[4,2,2,80,128]{4,3,2,1,0:T(8,128)(2,1)} %copy-done.7) | copy-start | bytes 983044
  121.5 23.9 %collective-permute-start.24 = (bf16[4,2,80,128]{3,2,1,0:T(8,128)(2,1)S(1)}, bf16[4,2,80,128]{3,2,1,0:T(8,128)(2,1)S(1)}, u32[]{:S(2)}, u32[]{:S(2)}) collective-permute-start(bf16[4,2,80,128]{3,2,1,0:T(8,128)(2,1)S(1)} %pad_maximum_fusion.13), channel_id=1, source_target_pairs={{0,4},{4,0},{8,12},{12,8},{16,20},{20,16},{24,28},{28,24},{1,5},{5... | collective-permute-start | bytes 491528 | tf_op jit(solution)/shard_map/ppermute | solution.py:491
  121.8 21.6 %collective-permute-start.14 = (bf16[4,2,2,80,128]{4,3,2,1,0:T(8,128)(2,1)S(1)}, bf16[4,2,2,80,128]{4,3,2,1,0:T(8,128)(2,1)S(1)}, u32[]{:S(2)}, u32[]{:S(2)}) collective-permute-start(bf16[4,2,2,80,128]{4,3,2,1,0:T(8,128)(2,1)S(1)} %pad_maximum_fusion.6), channel_id=1, source_target_pairs={{0,8},{4,12},{8,0},{12,4},{16,24},{20,28},{24,16},{28,20},{1,9},{5... | collective-permute-start | bytes 983048 | tf_op jit(solution)/shard_map/ppermute | solution.py:491
  121.9 23.5 %collective-permute-start.22 = (bf16[192,1280]{1,0:T(8,128)(2,1)S(1)}, bf16[192,1280]{1,0:T(8,128)(2,1)S(1)}, u32[]{:S(2)}, u32[]{:S(2)}) collective-permute-start(bf16[192,1280]{1,0:T(8,128)(2,1)S(1)} %get-tuple-element.308), channel_id=1, source_target_pairs={{0,1},{1,0},{2,3},{3,2},{4,5},{5,4},{6,7},{7,6},{8,9},{9,8},{10,11... | collective-permute-start | bytes 1474568 | tf_op jit(solution)/shard_map/ppermute | solution.py:491
  142.2 13.6 %collective-permute-start.23 = (bf16[4,2,2,80,128]{4,3,2,1,0:T(8,128)(2,1)S(1)}, bf16[4,2,2,80,128]{4,3,2,1,0:T(8,128)(2,1)S(1)}, u32[]{:S(2)}, u32[]{:S(2)}) collective-permute-start(bf16[4,2,2,80,128]{4,3,2,1,0:T(8,128)(2,1)S(1)} %get-tuple-element.188), channel_id=1, source_target_pairs={{0,4},{4,0},{8,12},{12,8},{16,20},{20,16},{24,28},{28,24},{1,5},{5... | collective-permute-start | bytes 983048 | tf_op jit(solution)/shard_map/ppermute | solution.py:491
  143.4 16.0 %collective-permute-start.30 = (bf16[2,128,1280]{2,1,0:T(8,128)(2,1)S(1)}, bf16[2,128,1280]{2,1,0:T(8,128)(2,1)S(1)}, u32[]{:S(2)}, u32[]{:S(2)}) collective-permute-start(bf16[2,128,1280]{2,1,0:T(8,128)(2,1)S(1)} %get-tuple-element.208), channel_id=1, source_target_pairs={{0,2},{1,3},{2,0},{3,1},{4,6},{5,7},{6,4},{7,5},{8,10},{9,11},{10,... | collective-permute-start | bytes 1966088 | tf_op jit(solution)/shard_map/ppermute | solution.py:491
  144.8 23.1 %collective-permute-start.29 = (bf16[128,1280]{1,0:T(8,128)(2,1)S(1)}, bf16[128,1280]{1,0:T(8,128)(2,1)S(1)}, u32[]{:S(2)}, u32[]{:S(2)}) collective-permute-start(bf16[128,1280]{1,0:T(8,128)(2,1)S(1)} %get-tuple-element.207), channel_id=1, source_target_pairs={{0,1},{1,0},{2,3},{3,2},{4,5},{5,4},{6,7},{7,6},{8,9},{9,8},{10,11... | collective-permute-start | bytes 983048 | tf_op jit(solution)/shard_map/ppermute | solution.py:491
  155.5 12.2 %collective-permute-start.32 = (bf16[4,2,80,128]{3,2,1,0:T(8,128)(2,1)S(1)}, bf16[4,2,80,128]{3,2,1,0:T(8,128)(2,1)S(1)}, u32[]{:S(2)}, u32[]{:S(2)}) collective-permute-start(bf16[4,2,80,128]{3,2,1,0:T(8,128)(2,1)S(1)} %get-tuple-element.202), channel_id=1, source_target_pairs={{0,4},{4,0},{8,12},{12,8},{16,20},{20,16},{24,28},{28,24},{1,5},{5... | collective-permute-start | bytes 491528 | tf_op jit(solution)/shard_map/ppermute | solution.py:491
  155.8 10.7 %collective-permute-start.27 = (bf16[2,64,1280]{2,1,0:T(8,128)(2,1)S(1)}, bf16[2,64,1280]{2,1,0:T(8,128)(2,1)S(1)}, u32[]{:S(2)}, u32[]{:S(2)}) collective-permute-start(bf16[2,64,1280]{2,1,0:T(8,128)(2,1)S(1)} %get-tuple-element.206), channel_id=1, source_target_pairs={{0,2},{1,3},{2,0},{3,1},{4,6},{5,7},{6,4},{7,5},{8,10},{9,11},{10,... | collective-permute-start | bytes 983048 | tf_op jit(solution)/shard_map/ppermute | solution.py:491
  156.2 14.6 %collective-permute-start.26 = (bf16[64,1280]{1,0:T(8,128)(2,1)S(1)}, bf16[64,1280]{1,0:T(8,128)(2,1)S(1)}, u32[]{:S(2)}, u32[]{:S(2)}) collective-permute-start(bf16[64,1280]{1,0:T(8,128)(2,1)S(1)} %get-tuple-element.205), channel_id=1, source_target_pairs={{0,1},{1,0},{2,3},{3,2},{4,5},{5,4},{6,7},{7,6},{8,9},{9,8},{10,11... | collective-permute-start | bytes 491528 | tf_op jit(solution)/shard_map/ppermute | solution.py:491
  159.5 12.9 %collective-permute-start.25 = (bf16[4,2,2,80,128]{4,3,2,1,0:T(8,128)(2,1)S(1)}, bf16[4,2,2,80,128]{4,3,2,1,0:T(8,128)(2,1)S(1)}, u32[]{:S(2)}, u32[]{:S(2)}) collective-permute-start(bf16[4,2,2,80,128]{4,3,2,1,0:T(8,128)(2,1)S(1)} %pad_maximum_fusion.8), channel_id=1, source_target_pairs={{0,8},{4,12},{8,0},{12,4},{16,24},{20,28},{24,16},{28,20},{1,9},{5... | collective-permute-start | bytes 983048 | tf_op jit(solution)/shard_map/ppermute | solution.py:491
  166.5 2.4 collective-permute-start.31
  167.7 3.1 %collective-permute-start.28 = (bf16[64,1280]{1,0:T(8,128)(2,1)S(1)}, bf16[64,1280]{1,0:T(8,128)(2,1)S(1)}, u32[]{:S(2)}, u32[]{:S(2)}) collective-permute-start(bf16[64,1280]{1,0:T(8,128)(2,1)S(1)} %get-tuple-element.328), channel_id=1, source_target_pairs={{0,1},{1,0},{2,3},{3,2},{4,5},{5,4},{6,7},{7,6},{8,9},{9,8},{10,11... | collective-permute-start | bytes 491528 | tf_op jit(solution)/shard_map/ppermute | solution.py:491
  167.9 8.9 %collective-permute-start.19 = (bf16[4,2,2,80,128]{4,3,2,1,0:T(8,128)(2,1)S(1)}, bf16[4,2,2,80,128]{4,3,2,1,0:T(8,128)(2,1)S(1)}, u32[]{:S(2)}, u32[]{:S(2)}) collective-permute-start(bf16[4,2,2,80,128]{4,3,2,1,0:T(8,128)(2,1)S(1)} %pad_maximum_fusion.7), channel_id=1, source_target_pairs={{0,4},{4,0},{8,12},{12,8},{16,20},{20,16},{24,28},{28,24},{1,5},{5... | collective-permute-start | bytes 983048 | tf_op jit(solution)/shard_map/ppermute | solution.py:491
  168.9 22.9 %collective-permute-start.36 = (bf16[4,2,80,128]{3,2,1,0:T(8,128)(2,1)S(1)}, bf16[4,2,80,128]{3,2,1,0:T(8,128)(2,1)S(1)}, u32[]{:S(2)}, u32[]{:S(2)}) collective-permute-start(bf16[4,2,80,128]{3,2,1,0:T(8,128)(2,1)S(1)} %pad_maximum_fusion.14), channel_id=1, source_target_pairs={{0,8},{4,12},{8,0},{12,4},{16,24},{20,28},{24,16},{28,20},{1,9},{5... | collective-permute-start | bytes 491528 | tf_op jit(solution)/shard_map/ppermute | solution.py:491
  172.4 19.2 %collective-permute-start.37 = (bf16[4,2,2,80,128]{4,3,2,1,0:T(8,128)(2,1)S(1)}, bf16[4,2,2,80,128]{4,3,2,1,0:T(8,128)(2,1)S(1)}, u32[]{:S(2)}, u32[]{:S(2)}) collective-permute-start(bf16[4,2,2,80,128]{4,3,2,1,0:T(8,128)(2,1)S(1)} %pad_maximum_fusion.9), channel_id=1, source_target_pairs={{0,16},{4,20},{8,24},{12,28},{16,0},{20,4},{24,8},{28,12},{1,17},{... | collective-permute-start | bytes 983048 | tf_op jit(solution)/shard_map/ppermute | solution.py:491
  191.3 7.9 %collective-permute-start.39 = (bf16[4,2,2,80,128]{4,3,2,1,0:T(8,128)(2,1)S(1)}, bf16[4,2,2,80,128]{4,3,2,1,0:T(8,128)(2,1)S(1)}, u32[]{:S(2)}, u32[]{:S(2)}) collective-permute-start(bf16[4,2,2,80,128]{4,3,2,1,0:T(8,128)(2,1)S(1)} %get-tuple-element.232), channel_id=1, source_target_pairs={{0,4},{4,0},{8,12},{12,8},{16,20},{20,16},{24,28},{28,24},{1,5},{5... | collective-permute-start | bytes 983048 | tf_op jit(solution)/shard_map/ppermute | solution.py:491
  191.8 9.7 %collective-permute-start.38 = (bf16[4,2,80,128]{3,2,1,0:T(8,128)(2,1)S(1)}, bf16[4,2,80,128]{3,2,1,0:T(8,128)(2,1)S(1)}, u32[]{:S(2)}, u32[]{:S(2)}) collective-permute-start(bf16[4,2,80,128]{3,2,1,0:T(8,128)(2,1)S(1)} %pad_maximum_fusion.15), channel_id=1, source_target_pairs={{0,16},{4,20},{8,24},{12,28},{16,0},{20,4},{24,8},{28,12},{1,17},{... | collective-permute-start | bytes 491528 | tf_op jit(solution)/shard_map/ppermute | solution.py:491
  192.9 14.3 %collective-permute-start.34 = (bf16[2,128,1280]{2,1,0:T(8,128)(2,1)S(1)}, bf16[2,128,1280]{2,1,0:T(8,128)(2,1)S(1)}, u32[]{:S(2)}, u32[]{:S(2)}) collective-permute-start(bf16[2,128,1280]{2,1,0:T(8,128)(2,1)S(1)} %copy-done.23), channel_id=1, source_target_pairs={{0,2},{1,3},{2,0},{3,1},{4,6},{5,7},{6,4},{7,5},{8,10},{9,11},{10,... | collective-permute-start | bytes 1966088 | tf_op jit(solution)/shard_map/ppermute | solution.py:491
  194.1 30.0 %collective-permute-start.33 = (bf16[128,1280]{1,0:T(8,128)(2,1)S(1)}, bf16[128,1280]{1,0:T(8,128)(2,1)S(1)}, u32[]{:S(2)}, u32[]{:S(2)}) collective-permute-start(bf16[128,1280]{1,0:T(8,128)(2,1)S(1)} %get-tuple-element.230), channel_id=1, source_target_pairs={{0,1},{1,0},{2,3},{3,2},{4,5},{5,4},{6,7},{7,6},{8,9},{9,8},{10,11... | collective-permute-start | bytes 983048 | tf_op jit(solution)/shard_map/ppermute | solution.py:491
  196.3 25.0 %collective-permute-start.43 = (bf16[8,2,2,80,128]{4,3,2,1,0:T(8,128)(2,1)S(1)}, bf16[8,2,2,80,128]{4,3,2,1,0:T(8,128)(2,1)S(1)}, u32[]{:S(2)}, u32[]{:S(2)}) collective-permute-start(bf16[8,2,2,80,128]{4,3,2,1,0:T(8,128)(2,1)S(1)} %constant_dynamic-update-slice_fusion.8.refs_1_), channel_id=1, source_target_pairs={{0,2},{1,3},{2,0},{3,1},{4,6},{5,7},{6,4},{7,5},{8,10},{9,11},{10,... | collective-permute-start | bytes 1966088 | tf_op jit(solution)/shard_map/ppermute | solution.py:491
  199.2 28.4 %collective-permute-start.42 = (bf16[8,2,2,80,128]{4,3,2,1,0:T(8,128)(2,1)S(1)}, bf16[8,2,2,80,128]{4,3,2,1,0:T(8,128)(2,1)S(1)}, u32[]{:S(2)}, u32[]{:S(2)}) collective-permute-start(bf16[8,2,2,80,128]{4,3,2,1,0:T(8,128)(2,1)S(1)} %constant_dynamic-update-slice_fusion.8.refs_1_), channel_id=1, source_target_pairs={{0,1},{1,0},{2,3},{3,2},{4,5},{5,4},{6,7},{7,6},{8,9},{9,8},{10,11... | collective-permute-start | bytes 1966088 | tf_op jit(solution)/shard_map/ppermute | solution.py:491
  201.6 24.5 %collective-permute-start.40 = (bf16[4,2,2,80,128]{4,3,2,1,0:T(8,128)(2,1)S(1)}, bf16[4,2,2,80,128]{4,3,2,1,0:T(8,128)(2,1)S(1)}, u32[]{:S(2)}, u32[]{:S(2)}) collective-permute-start(bf16[4,2,2,80,128]{4,3,2,1,0:T(8,128)(2,1)S(1)} %pad_maximum_fusion.10), channel_id=1, source_target_pairs={{0,8},{4,12},{8,0},{12,4},{16,24},{20,28},{24,16},{28,20},{1,9},{5... | collective-permute-start | bytes 983048 | tf_op jit(solution)/shard_map/ppermute | solution.py:491
  207.3 16.9 %collective-permute-start.35 = (bf16[128,1280]{1,0:T(8,128)(2,1)S(1)}, bf16[128,1280]{1,0:T(8,128)(2,1)S(1)}, u32[]{:S(2)}, u32[]{:S(2)}) collective-permute-start(bf16[128,1280]{1,0:T(8,128)(2,1)S(1)} %get-tuple-element.314), channel_id=1, source_target_pairs={{0,1},{1,0},{2,3},{3,2},{4,5},{5,4},{6,7},{7,6},{8,9},{9,8},{10,11... | collective-permute-start | bytes 983048 | tf_op jit(solution)/shard_map/ppermute | solution.py:491
  221.3 6.3 %collective-permute-start.44 = (bf16[8,2,2,80,128]{4,3,2,1,0:T(8,128)(2,1)S(1)}, bf16[8,2,2,80,128]{4,3,2,1,0:T(8,128)(2,1)S(1)}, u32[]{:S(2)}, u32[]{:S(2)}) collective-permute-start(bf16[8,2,2,80,128]{4,3,2,1,0:T(8,128)(2,1)S(1)} %collective-permute-done.43.refs_3_), channel_id=1, source_target_pairs={{0,1},{1,0},{2,3},{3,2},{4,5},{5,4},{6,7},{7,6},{8,9},{9,8},{10,11... | collective-permute-start | bytes 1966088 | tf_op jit(solution)/shard_map/ppermute | solution.py:491
  226.2 17.0 %collective-permute-start.41 = (bf16[4,2,2,80,128]{4,3,2,1,0:T(8,128)(2,1)S(1)}, bf16[4,2,2,80,128]{4,3,2,1,0:T(8,128)(2,1)S(1)}, u32[]{:S(2)}, u32[]{:S(2)}) collective-permute-start(bf16[4,2,2,80,128]{4,3,2,1,0:T(8,128)(2,1)S(1)} %pad_maximum_fusion.11), channel_id=1, source_target_pairs={{0,16},{4,20},{8,24},{12,28},{16,0},{20,4},{24,8},{28,12},{1,17},{... | collective-permute-start | bytes 983048 | tf_op jit(solution)/shard_map/ppermute | solution.py:491
  243.1 25.0 %copy-start.13 = (s32[336]{0:T(512)S(1)}, s32[336]{0:T(512)}, u32[]{:S(2)}) copy-start(s32[336]{0:T(512)} %copy-done.12) | copy-start | bytes 4036
  243.1 25.0 %copy-start.15 = (s32[80]{0:T(128)S(1)}, s32[80]{0:T(128)}, u32[]{:S(2)}) copy-start(s32[80]{0:T(128)} %copy-done.14) | copy-start | bytes 964
  243.1 25.0 %copy-start.16 = (s32[336]{0:T(512)S(1)}, s32[336]{0:T(512)}, u32[]{:S(2)}) copy-start(s32[336]{0:T(512)} %get-tuple-element.353) | copy-start | bytes 4036
  243.1 25.0 %copy-start.19 = (pred[336]{0:T(512)(128)(4,1)S(1)}, pred[336]{0:T(512)(128)(4,1)}, u32[]{:S(2)}) copy-start(pred[336]{0:T(512)(128)(4,1)} %copy-done.18) | copy-start | bytes 1012
  243.1 25.0 %copy-start.20 = (s32[80]{0:T(128)S(1)}, s32[80]{0:T(128)}, u32[]{:S(2)}) copy-start(s32[80]{0:T(128)} %get-tuple-element.291) | copy-start | bytes 964
  243.1 25.1 %copy-start.21 = (f32[4]{0:T(128)S(1)}, f32[4]{0:T(128)}, u32[]{:S(2)}) copy-start(f32[4]{0:T(128)} %param.11) | copy-start | bytes 52
  243.3 24.2 %collective-permute-start.46 = (bf16[8,2,2,80,128]{4,3,2,1,0:T(8,128)(2,1)S(1)}, bf16[8,2,2,80,128]{4,3,2,1,0:T(8,128)(2,1)S(1)}, u32[]{:S(2)}, u32[]{:S(2)}) collective-permute-start(bf16[8,2,2,80,128]{4,3,2,1,0:T(8,128)(2,1)S(1)} %constant_dynamic-update-slice_fusion.14.refs_1_), channel_id=1, source_target_pairs={{0,2},{1,3},{2,0},{3,1},{4,6},{5,7},{6,4},{7,5},{8,10},{9,11},{10,... | collective-permute-start | bytes 1966088 | tf_op jit(solution)/shard_map/ppermute | solution.py:491
  244.6 21.7 %collective-permute-start.49 = (bf16[8,2,80,128]{3,2,1,0:T(8,128)(2,1)S(1)}, bf16[8,2,80,128]{3,2,1,0:T(8,128)(2,1)S(1)}, u32[]{:S(2)}, u32[]{:S(2)}) collective-permute-start(bf16[8,2,80,128]{3,2,1,0:T(8,128)(2,1)S(1)} %constant_dynamic-update-slice_fusion.9.refs_1_), channel_id=1, source_target_pairs={{0,2},{1,3},{2,0},{3,1},{4,6},{5,7},{6,4},{7,5},{8,10},{9,11},{10,... | collective-permute-start | bytes 983048 | tf_op jit(solution)/shard_map/ppermute | solution.py:491
  244.9 23.5 %collective-permute-start.48 = (bf16[8,2,80,128]{3,2,1,0:T(8,128)(2,1)S(1)}, bf16[8,2,80,128]{3,2,1,0:T(8,128)(2,1)S(1)}, u32[]{:S(2)}, u32[]{:S(2)}) collective-permute-start(bf16[8,2,80,128]{3,2,1,0:T(8,128)(2,1)S(1)} %constant_dynamic-update-slice_fusion.9.refs_1_), channel_id=1, source_target_pairs={{0,1},{1,0},{2,3},{3,2},{4,5},{5,4},{6,7},{7,6},{8,9},{9,8},{10,11... | collective-permute-start | bytes 983048 | tf_op jit(solution)/shard_map/ppermute | solution.py:491
  266.3 2.5 collective-permute-start.50
  267.6 11.9 %collective-permute-start.45 = (bf16[8,2,2,80,128]{4,3,2,1,0:T(8,128)(2,1)S(1)}, bf16[8,2,2,80,128]{4,3,2,1,0:T(8,128)(2,1)S(1)}, u32[]{:S(2)}, u32[]{:S(2)}) collective-permute-start(bf16[8,2,2,80,128]{4,3,2,1,0:T(8,128)(2,1)S(1)} %constant_dynamic-update-slice_fusion.14.refs_1_), channel_id=1, source_target_pairs={{0,1},{1,0},{2,3},{3,2},{4,5},{5,4},{6,7},{7,6},{8,9},{9,8},{10,11... | collective-permute-start | bytes 1966088 | tf_op jit(solution)/shard_map/ppermute | solution.py:491
  267.6 11.9 %collective-permute-start.47 = (bf16[8,2,2,80,128]{4,3,2,1,0:T(8,128)(2,1)S(1)}, bf16[8,2,2,80,128]{4,3,2,1,0:T(8,128)(2,1)S(1)}, u32[]{:S(2)}, u32[]{:S(2)}) collective-permute-start(bf16[8,2,2,80,128]{4,3,2,1,0:T(8,128)(2,1)S(1)} %collective-permute-done.46.refs_3_), channel_id=1, source_target_pairs={{0,1},{1,0},{2,3},{3,2},{4,5},{5,4},{6,7},{7,6},{8,9},{9,8},{10,11... | collective-permute-start | bytes 1966088 | tf_op jit(solution)/shard_map/ppermute | solution.py:491
  (11 other events, 28.1 us)

commit v2 on v1

--- a/solution.py
+++ b/solution.py
@@ -115,7 +115,7 @@
 
 
 SOURCES = (0, 4, 2, 6, 1, 5, 3, 7)
-STEPS = (0, 1, 0, 2, 0, 1, 2, 1, None, 0, 2, 1, 0, 1, 2, 0, 2, 1, 0, 1, 3, 4, 0, 2, 0, 1, 2, 1, 5, 2, 0, 2, 1, 2)
+STEPS = (0, 1, 0, 2, 0, 1, 2, 1, None, 0, 2, 1, "force", 0, 1, 2, 0, 2, 1, 0, 1, 3, 4, 0, 2, 0, 1, 2, 1, 2, 0, 2, "grid", 1, 2, 5)
 
 
 def row_of(h, q, d, r):
@@ -509,6 +509,9 @@
     def __init__(self):
         self.last = None
 
+    def hold(self, values):
+        return lax.optimization_barrier((values, self.last))[0]
+
     def run(self, step, *inputs):
         if self.last is not None:
             inputs, _ = lax.optimization_barrier((inputs, self.last))
@@ -618,7 +621,7 @@
     turn = Turns()
     run = turn.run
     first_force = spread_lon(*run(lambda f: far_rows(f, starts[0], split[0]), forcing))
-    state = {"grid": None, "total": None, "force": None, "table": None}
+    state = {"grid": None, "total": None, "force": None, "table": None, "first": first_force}
 
     def chunk_steps(n):
         tiles, packed, _ = chunks[n]
@@ -627,9 +630,9 @@
         )
         yield
         other_far, other_own = swap(send[1], "lon", 1), swap(send[0], "lon", 1)
+        if n == 2:
+            keep, state["first"] = lax.optimization_barrier((keep, state["first"]))
         away = swap(run(lambda k, o: add(k[1], o), keep, other_far), "lon", 2)
-        if n == 2:
-            state["force"] = spread_lon(*run(lambda f: far_rows(f, after_first, split[1]), forcing))
         yield
         half = groups // 2
         stay, leave = run(
@@ -638,7 +641,7 @@
         )
         arrays = yield from exchange_lat(run, stay, leave, (4, 2, 1))
         yield
-        force = state["force"] if n else first_force
+        force = state["force"] if n else state["first"]
         grid, near, far, stay, leave = run(
             lambda *a: zonal_chunk(
                 spots[n], a[:4], a[4], setups[n], waves[:, None], turns, forcing, a[5:], state["grid"], packed, 1.0 / length
@@ -646,7 +649,7 @@
             *arrays, state["table"], *force,
         )
         state["grid"] = grid
-        settled.append((spots[n], spread_lon(near, far)))
+        settled.append((spots[n], (near, far) if n == 2 else spread_lon(near, far)))
         arrays = yield from exchange_lat(run, stay, leave, (1, 2, 4))
         yield
         own = run(lambda *a: jnp.stack(pieces_of(a)), *arrays)
@@ -667,6 +670,10 @@
     for step in STEPS:
         if step is None:
             state["table"] = run(lambda w: make_table(w, 0, seg_width, length, groups), waves)
+        elif step == "force":
+            state["force"] = spread_lon(*run(lambda f: far_rows(f, after_first, split[1]), forcing))
+        elif step == "grid":
+            settled[2] = settled[2][0], spread_lon(*turn.hold(settled[2][1]))
         elif step < 3:
             next(walks[step])
         else:

time: 300 us -> 283 us (0.943)
  waiting for transfers between devices: 69 us -> 44.8 us
  other arithmetic: 22.9 us -> 28.3 us
  local copies, waits for them, and re-layouts: 16 us -> 19.6 us
    ppermute x51, waiting for transfers between devices: 69 us -> 44.8 us  [swap(): return lax.ppermute(value, axis, pairs)]
  transfers between devices with their start and end apart: 51 -> 51, of which waited for: 15 -> 14; matrix products, arithmetic and copies ran while one was open for 12% -> 15% of each run, Pallas kernels for 38% -> 46%
where the time goes in v2:
time: 283 us; the launch traced here: 280 us
  Pallas kernels  130 us (46%)
  starting transfers between devices  55.6 us (20%)
  waiting for transfers between devices  44.8 us (16%)
  other arithmetic  28.3 us (10%)
  local copies, waits for them, and re-layouts  19.6 us (7%)
    ppermute x51, starting transfers between devices, swap(): return lax.ppermute(value, axis, pairs)  55.6 us
    ppermute x51, waiting for transfers between devices, swap(): return lax.ppermute(value, axis, pairs)  44.8 us
    pallas_call x3, Pallas kernels, down_chunk(): pl.pallas_call(lambda *refs: down_kernel(*refs, tiles=tiles, packed=packe...  41.2 us
    pallas_call x3, Pallas kernels, zonal_chunk(): pl.pallas_call(lambda *refs: zonal_kernel(*refs, packed=packed, first=fir...  38 us
    pallas_call x3, Pallas kernels, up_chunk(): pl.pallas_call(lambda *refs: up_kernel(*refs, tiles=tiles, packed=packed,...  37.6 us
    convert_element_type x6, other arithmetic, add(): return sum((v.astype(F32) for v in values)).astype(BF16)  10.4 us
    pallas_call x1, Pallas kernels, make_table(): pl.pallas_call(table_kernel, out_shape=jax.ShapeDtypeStruct((2, groups, c...  7.46 us
  transfers between devices with their start and end apart: 51, of which 14 were waited for; matrix products, arithmetic and copies ran while one was open for 15% of the time, Pallas kernels for 46%

profile of v2, /device:TPU:1, one launch (start us, length us, event | category | flops | bytes accessed | tf_op | source)
XLA Modules:
  0.0 279.9 jit_solution(8865400314660188195)
XLA Ops:
  0.7 2.3 fusion.20
  4.0 2.0 collective-permute-start.2
  9.2 1.7 multiply_bitcast_fusion.refs_1_
  10.9 14.7 %legendre_up.3 = (bf16[2,8,2,2,80,128]{5,4,3,2,1,0:T(8,128)(2,1)S(1)}, bf16[2,8,2,2,80,128]{5,4,3,2,1,0:T(8,128)(2,1)S(1)}) custom-call(s32[2]{0:T(128)S(1)} %pad_add_fusion.3.refs_0_, bf16[80,32,336]{2,1,0:T(8,128)(2,1)} %multiply_bitcast_fusion.refs_1_, bf16[80,336,1280]{2,1,0:T(8,128)(2,1)} %refs_8_.3, bf16[80,336,1280]{2,1,0:T(8,128)(2,1)} %refs_8_.3, ...), custom_call_target="tpu_custom_call" | custom-call | flops 7046430720 | bytes 27525120 | tf_op jit(solution)/shard_map/legendre_up/pallas_call | solution.py:182
  26.9 1.0 collective-permute-start
  27.9 8.6 %legendre_up.4 = (bf16[2,8,2,80,128]{4,3,2,1,0:T(8,128)(2,1)S(1)}, bf16[2,8,2,80,128]{4,3,2,1,0:T(8,128)(2,1)S(1)}) custom-call(s32[2]{0:T(128)S(1)} %pad_add_fusion.3.refs_0_, bf16[80,32,336]{2,1,0:T(8,128)(2,1)S(1)} %copy-done, bf16[80,336,1280]{2,1,0:T(8,128)(2,1)} %refs_8_.3, bf16[80,336,1280]{2,1,0:T(8,128)(2,1)} %refs_8_.3), custom_call_target="tpu_custom_call" | custom-call | flops 3523215360 | bytes 13762560 | tf_op jit(solution)/shard_map/legendre_up/pallas_call | solution.py:182
  43.1 14.2 %legendre_up.5 = (bf16[2,8,2,2,80,128]{5,4,3,2,1,0:T(8,128)(2,1)S(1)}, bf16[2,8,2,2,80,128]{5,4,3,2,1,0:T(8,128)(2,1)S(1)}) custom-call(s32[2]{0:T(128)S(1)} %pad_add_fusion.3.refs_0_, bf16[80,32,336]{2,1,0:T(8,128)(2,1)} %multiply_bitcast_fusion.refs_1_, bf16[80,336,1280]{2,1,0:T(8,128)(2,1)} %refs_8_.3, bf16[80,336,1280]{2,1,0:T(8,128)(2,1)} %refs_8_.3, ...), custom_call_target="tpu_custom_call" | custom-call | flops 7046430720 | bytes 27525120 | tf_op jit(solution)/shard_map/legendre_up/pallas_call | solution.py:182
  57.3 1.2 slice_bitcast_fusion.1
  59.0 2.0 slice_bitcast_fusion.10
  61.5 2.1 fusion.9
  63.6 1.9 fusion.10
  65.4 1.7 collective-permute-start.12
  67.7 2.3 collective-permute-start.10
  70.0 2.1 fusion
  72.3 3.1 %collective-permute-done.12 = bf16[8,2,80,128]{3,2,1,0:T(8,128)(2,1)} collective-permute-done((bf16[8,2,80,128]{3,2,1,0:T(8,128)(2,1)}, bf16[8,2,80,128]{3,2,1,0:T(8,128)(2,1)}, u32[]{:S(2)}, u32[]{:S(2)}) %collective-permute-start.12) | collective-permute-done | bytes 327712 | tf_op jit(solution)/shard_map/ppermute | solution.py:491
  75.5 1.9 fusion.22
  77.4 2.3 collective-permute-start.14
  79.8 1.1 copy.23
  80.9 3.6 %multiply_sine_fusion = (f32[1280,10]{1,0:T(8,128)S(1)}, f32[1280,10]{1,0:T(8,128)S(1)}) fusion(f32[1280,10]{1,0:T(8,128)} %copy.23), kind=kLoop, calls=%fused_computation.40 | loop fusion | flops 12800 | bytes 153600 | tf_op jit(solution)/shard_map/sin | solution.py:316
  84.5 2.7 fusion.15
  87.2 7.5 %zonal_table.1.refs_5_ = bf16[2,8,160,1280]{3,2,1,0:T(8,128)(2,1)} custom-call(f32[1280,10]{1,0:T(8,128)S(1)} %get-tuple-element.331.cos_far, f32[1280,10]{1,0:T(8,128)S(1)} %get-tuple-element.330.sin_far, f32[1280,128]{1,0:T(8,128)S(1)} %get-tuple-element.353.cos_near, f32[1280,128]{1,0:T(8,128)S(1)} %get-tuple-element.352.sin_near), custom_call_target="tpu_custom_call" | custom-call | tf_op jit(solution)/shard_map/zonal_table/pallas_call | solution.py:308
  95.6 1.3 collective-permute-start.16
  96.9 2.3 fusion.5
  99.9 2.7 fusion.18
  102.6 1.0 pad_maximum_fusion
  103.7 1.2 collective-permute-start.21
  105.0 1.1 broadcast_in_dim_reshape.3.refs_8_
  106.1 1.1 copy.24
  108.7 1.3 collective-permute-start.18
  110.0 3.2 %collective-permute-start.20 = (bf16[192,1280]{1,0:T(8,128)(2,1)}, bf16[192,1280]{1,0:T(8,128)(2,1)S(1)}, u32[]{:S(2)}, u32[]{:S(2)}) collective-permute-start(bf16[192,1280]{1,0:T(8,128)(2,1)} %get-tuple-element.304), channel_id=1, source_target_pairs={{0,1},{1,0},{2,3},{3,2},{4,5},{5,4},{6,7},{7,6},{8,9},{9,8},{10,11... | collective-permute-start | bytes 1474568 | tf_op jit(solution)/shard_map/ppermute | solution.py:491
  113.4 1.3 collective-permute-start.24
  114.7 8.8 %collective-permute-done.13.refs_2_ = bf16[4,2,2,80,128]{4,3,2,1,0:T(8,128)(2,1)S(1)} collective-permute-done((bf16[4,2,2,80,128]{4,3,2,1,0:T(8,128)(2,1)S(1)}, bf16[4,2,2,80,128]{4,3,2,1,0:T(8,128)(2,1)S(1)}, u32[]{:S(2)}, u32[]{:S(2)}) %collective-permute-start.13) | collective-permute-done | bytes 327712 | tf_op jit(solution)/shard_map/ppermute | solution.py:491
  123.7 1.4 collective-permute-done.21
  125.2 1.2 slice_bitcast_fusion.4
  126.4 3.0 %collective-permute-start.22 = (bf16[192,1280]{1,0:T(8,128)(2,1)S(1)}, bf16[192,1280]{1,0:T(8,128)(2,1)S(1)}, u32[]{:S(2)}, u32[]{:S(2)}) collective-permute-start(bf16[192,1280]{1,0:T(8,128)(2,1)S(1)} %get-tuple-element.320), channel_id=1, source_target_pairs={{0,1},{1,0},{2,3},{3,2},{4,5},{5,4},{6,7},{7,6},{8,9},{9,8},{10,11... | collective-permute-start | bytes 1474568 | tf_op jit(solution)/shard_map/ppermute | solution.py:491
  129.5 13.5 %zonal.3 = (f32[4,320,1280]{2,1,0:T(8,128)}, bf16[128,1280]{1,0:T(8,128)(2,1)S(1)}, bf16[2,128,1280]{2,1,0:T(8,128)(2,1)S(1)}, bf16[4,2,2,80,128]{4,3,2,1,0:T(8,128)(2,1)S(1)}, bf16[4,2,2,80,128]{4,3,2,1,0:T(8,128)(2,1)S(1)}) custom-call(s32[4]{0:T(128)S(1)} %pad_add_fusion.4.refs_0_.place, bf16[4,2,2,80,128]{4,3,2,1,0:T(8,128)(2,1)S(1)} %get-tuple-element.190.refs_1_, ...), custom_call_target="tpu_custom_call" | custom-call | flops 6710886400 | bytes 11796480 | tf_op jit(solution)/shard_map/zonal/pallas_call | solution.py:428
  143.0 1.3 collective-permute-start.23
  144.3 1.2 collective-permute-start.30
  146.3 10.0 %zonal.4 = (f32[4,320,1280]{2,1,0:T(8,128)}, bf16[64,1280]{1,0:T(8,128)(2,1)S(1)}, bf16[2,64,1280]{2,1,0:T(8,128)(2,1)S(1)}, bf16[4,2,80,128]{3,2,1,0:T(8,128)(2,1)S(1)}, bf16[4,2,80,128]{3,2,1,0:T(8,128)(2,1)S(1)}) custom-call(s32[4]{0:T(128)S(1)} %pad_add_fusion.5.refs_0_.place, ...), custom_call_target="tpu_custom_call", output_to_operand_aliasing={{0}: (16, {})} | custom-call | flops 3355443200 | bytes 9175040 | tf_op jit(solution)/shard_map/zonal/pallas_call | solution.py:428
  156.6 3.7 %collective-permute-done.30 = bf16[2,128,1280]{2,1,0:T(8,128)(2,1)S(1)} collective-permute-done((bf16[2,128,1280]{2,1,0:T(8,128)(2,1)S(1)}, bf16[2,128,1280]{2,1,0:T(8,128)(2,1)S(1)}, u32[]{:S(2)}, u32[]{:S(2)}) %collective-permute-start.30) | collective-permute-done | bytes 655392 | tf_op jit(solution)/shard_map/ppermute | solution.py:491
  160.3 1.9 collective-permute-start.31
  163.0 4.3 %collective-permute-done.27 = bf16[2,64,1280]{2,1,0:T(8,128)(2,1)S(1)} collective-permute-done((bf16[2,64,1280]{2,1,0:T(8,128)(2,1)S(1)}, bf16[2,64,1280]{2,1,0:T(8,128)(2,1)S(1)}, u32[]{:S(2)}, u32[]{:S(2)}) %collective-permute-start.27) | collective-permute-done | bytes 327712 | tf_op jit(solution)/shard_map/ppermute | solution.py:491
  169.4 1.3 collective-permute-start.34
  170.7 1.9 settle.3.before
  172.6 1.5 settle.4.refs_16_
  174.2 1.2 collective-permute-done.25
  175.6 2.9 %collective-permute-done.19.refs_4_ = bf16[4,2,2,80,128]{4,3,2,1,0:T(8,128)(2,1)S(1)} collective-permute-done((bf16[4,2,2,80,128]{4,3,2,1,0:T(8,128)(2,1)S(1)}, bf16[4,2,2,80,128]{4,3,2,1,0:T(8,128)(2,1)S(1)}, u32[]{:S(2)}, u32[]{:S(2)}) %collective-permute-start.19) | collective-permute-done | bytes 327712 | tf_op jit(solution)/shard_map/ppermute | solution.py:491
  178.5 14.5 %zonal.5 = (f32[4,320,1280]{2,1,0:T(8,128)}, bf16[128,1280]{1,0:T(8,128)(2,1)S(1)}, bf16[2,128,1280]{2,1,0:T(8,128)(2,1)}, bf16[4,2,2,80,128]{4,3,2,1,0:T(8,128)(2,1)S(1)}, bf16[4,2,2,80,128]{4,3,2,1,0:T(8,128)(2,1)S(1)}) custom-call(s32[4]{0:T(128)S(1)} %pad_add_fusion.1.refs_0_.place, ...), custom_call_target="tpu_custom_call", output_to_operand_aliasing={{0}: (16, {})} | custom-call | flops 6710886400 | bytes 11796480 | tf_op jit(solution)/shard_map/zonal/pallas_call | solution.py:428
  193.7 1.2 collective-permute-start.40
  194.9 4.1 %collective-permute-start.39 = (bf16[8,2,2,80,128]{4,3,2,1,0:T(8,128)(2,1)S(1)}, bf16[8,2,2,80,128]{4,3,2,1,0:T(8,128)(2,1)S(1)}, u32[]{:S(2)}, u32[]{:S(2)}) collective-permute-start(bf16[8,2,2,80,128]{4,3,2,1,0:T(8,128)(2,1)S(1)} %constant_dynamic-update-slice_fusion.8.refs_1_), channel_id=1, source_target_pairs={{0,1},{1,0},{2,3},{3,2},{4,5},{5,4},{6,7},{7,6},{8,9},{9,8},{10,11... | collective-permute-start | bytes 1966088 | tf_op jit(solution)/shard_map/ppermute | solution.py:491
  199.1 2.2 collective-permute-done.33
  201.4 1.6 collective-permute-start.36
  203.1 3.0 %collective-permute-done.40.refs_3_ = bf16[8,2,2,80,128]{4,3,2,1,0:T(8,128)(2,1)S(1)} collective-permute-done((bf16[8,2,2,80,128]{4,3,2,1,0:T(8,128)(2,1)S(1)}, bf16[8,2,2,80,128]{4,3,2,1,0:T(8,128)(2,1)S(1)}, u32[]{:S(2)}, u32[]{:S(2)}) %collective-permute-start.40) | collective-permute-done | bytes 655392 | tf_op jit(solution)/shard_map/ppermute | solution.py:491
  206.1 4.8 %collective-permute-start.41 = (bf16[8,2,2,80,128]{4,3,2,1,0:T(8,128)(2,1)S(1)}, bf16[8,2,2,80,128]{4,3,2,1,0:T(8,128)(2,1)S(1)}, u32[]{:S(2)}, u32[]{:S(2)}) collective-permute-start(bf16[8,2,2,80,128]{4,3,2,1,0:T(8,128)(2,1)S(1)} %collective-permute-done.40.refs_3_), channel_id=1, source_target_pairs={{0,1},{1,0},{2,3},{3,2},{4,5},{5,4},{6,7},{7,6},{8,9},{9,8},{10,11... | collective-permute-start | bytes 1966088 | tf_op jit(solution)/shard_map/ppermute | solution.py:491
  210.9 1.2 collective-permute-start.49
  212.3 2.4 collective-permute-start.38
  214.6 15.4 %legendre_down.3.refs_8_ = f32[4,2,80,336]{3,2,1,0:T(8,128)S(1)} custom-call(s32[2]{0:T(128)S(1)} %pad_add_fusion.3.refs_0_, bf16[8,2,2,80,128]{4,3,2,1,0:T(8,128)(2,1)S(1)} %constant_dynamic-update-slice_fusion.8.refs_1_, bf16[8,2,2,80,128]{4,3,2,1,0:T(8,128)(2,1)S(1)} %collective-permute-done.39.refs_2_, ...), custom_call_target="tpu_custom_call" | custom-call | flops 7046430720 | bytes 27525120 | tf_op jit(solution)/shard_map/legendre_down/pallas_call | solution.py:268
  231.4 1.3 collective-permute-start.43
  233.9 12.1 %collective-permute-done.46.refs_3_ = bf16[8,2,2,80,128]{4,3,2,1,0:T(8,128)(2,1)S(1)} collective-permute-done((bf16[8,2,2,80,128]{4,3,2,1,0:T(8,128)(2,1)S(1)}, bf16[8,2,2,80,128]{4,3,2,1,0:T(8,128)(2,1)S(1)}, u32[]{:S(2)}, u32[]{:S(2)}) %collective-permute-start.46) | collective-permute-done | bytes 655392 | tf_op jit(solution)/shard_map/ppermute | solution.py:491
  246.1 2.5 collective-permute-start.47
  248.5 9.7 %legendre_down.4.refs_10_ = f32[4,2,80,336]{3,2,1,0:T(8,128)S(1)} custom-call(s32[2]{0:T(128)S(1)} %pad_add_fusion.3.refs_0_, bf16[8,2,80,128]{3,2,1,0:T(8,128)(2,1)S(1)} %constant_dynamic-update-slice_fusion.9.refs_1_, bf16[8,2,80,128]{3,2,1,0:T(8,128)(2,1)S(1)} %collective-permute-done.48.refs_2_, ...), custom_call_target="tpu_custom_call" | custom-call | flops 3523215360 | bytes 13762560 | tf_op jit(solution)/shard_map/legendre_down/pallas_call | solution.py:268
  260.2 1.5 collective-permute-start.44
  261.7 16.1 %legendre_down.5 = f32[4,2,80,336]{3,2,1,0:T(8,128)} custom-call(s32[2]{0:T(128)S(1)} %pad_add_fusion.3.refs_0_, bf16[8,2,2,80,128]{4,3,2,1,0:T(8,128)(2,1)S(1)} %constant_dynamic-update-slice_fusion.14.refs_1_, bf16[8,2,2,80,128]{4,3,2,1,0:T(8,128)(2,1)S(1)} %collective-permute-done.45.refs_2_, ...), custom_call_target="tpu_custom_call" | custom-call | flops 7046430720 | bytes 27525120 | tf_op jit(solution)/shard_map/legendre_down/pallas_call | solution.py:268
  277.7 1.9 settle.5
  (255 shorter events, 26.5 us)
Async XLA Ops:
  0.7 5.9 %copy-start.26 = (s32[640]{0:T(1024)S(1)}, s32[640]{0:T(1024)}, u32[]{:S(2)}) copy-start(s32[640]{0:T(1024)} %param.8) | copy-start | bytes 7684
  3.0 5.3 %copy-start.14 = (f32[4,2,80,336]{3,2,1,0:T(8,128)S(1)}, f32[4,2,80,336]{3,2,1,0:T(8,128)}, u32[]{:S(2)}) copy-start(f32[4,2,80,336]{3,2,1,0:T(8,128)} %refs_11_.1) | copy-start | bytes 2580484
  4.0 54.5 %collective-permute-start.2 = (bf16[2,128,1280]{2,1,0:T(8,128)(2,1)}, bf16[2,128,1280]{2,1,0:T(8,128)(2,1)}, u32[]{:S(2)}, u32[]{:S(2)}) collective-permute-start(bf16[2,128,1280]{2,1,0:T(8,128)(2,1)} %pad_maximum_fusion.1), channel_id=1, source_target_pairs={{0,2},{1,3},{2,0},{3,1},{4,6},{5,7},{6,4},{7,5},{8,10},{9,11},{10,... | collective-permute-start | bytes 1966088 | tf_op jit(solution)/shard_map/ppermute | solution.py:491
  26.9 15.9 %collective-permute-start = (bf16[8,2,2,80,128]{4,3,2,1,0:T(8,128)(2,1)S(1)}, bf16[8,2,2,80,128]{4,3,2,1,0:T(8,128)(2,1)S(1)}, u32[]{:S(2)}, u32[]{:S(2)}) collective-permute-start(bf16[8,2,2,80,128]{4,3,2,1,0:T(8,128)(2,1)S(1)} %get-tuple-element.317), channel_id=1, source_target_pairs={{0,1},{1,0},{2,3},{3,2},{4,5},{5,4},{6,7},{7,6},{8,9},{9,8},{10,11... | collective-permute-start | bytes 1966088 | tf_op jit(solution)/shard_map/ppermute | solution.py:491
  27.9 33.1 %collective-permute-start.7 = (bf16[8,2,2,80,128]{4,3,2,1,0:T(8,128)(2,1)}, bf16[8,2,2,80,128]{4,3,2,1,0:T(8,128)(2,1)}, u32[]{:S(2)}, u32[]{:S(2)}) collective-permute-start(bf16[8,2,2,80,128]{4,3,2,1,0:T(8,128)(2,1)} %get-tuple-element.316), channel_id=1, source_target_pairs={{0,1},{1,0},{2,3},{3,2},{4,5},{5,4},{6,7},{7,6},{8,9},{9,8},{10,11... | collective-permute-start | bytes 1966088 | tf_op jit(solution)/shard_map/ppermute | solution.py:491
  37.4 5.4 %copy-start.4 = (bf16[2,8,2,2,80,128]{5,4,3,2,1,0:T(8,128)(2,1)S(1)}, bf16[2,8,2,2,80,128]{5,4,3,2,1,0:T(8,128)(2,1)}, u32[]{:S(2)}) copy-start(bf16[2,8,2,2,80,128]{5,4,3,2,1,0:T(8,128)(2,1)} %copy-done.3) | copy-start | bytes 3932164
  38.3 25.3 %collective-permute-start.6 = (bf16[8,2,80,128]{3,2,1,0:T(8,128)(2,1)}, bf16[8,2,80,128]{3,2,1,0:T(8,128)(2,1)}, u32[]{:S(2)}, u32[]{:S(2)}) collective-permute-start(bf16[8,2,80,128]{3,2,1,0:T(8,128)(2,1)} %get-tuple-element.333), channel_id=1, source_target_pairs={{0,1},{1,0},{2,3},{3,2},{4,5},{5,4},{6,7},{7,6},{8,9},{9,8},{10,11... | collective-permute-start | bytes 983048 | tf_op jit(solution)/shard_map/ppermute | solution.py:491
  39.2 28.0 %collective-permute-start.1 = (bf16[128,1280]{1,0:T(8,128)(2,1)}, bf16[128,1280]{1,0:T(8,128)(2,1)}, u32[]{:S(2)}, u32[]{:S(2)}) collective-permute-start(bf16[128,1280]{1,0:T(8,128)(2,1)} %get-tuple-element.307), channel_id=1, source_target_pairs={{0,1},{1,0},{2,3},{3,2},{4,5},{5,4},{6,7},{7,6},{8,9},{9,8},{10,11... | collective-permute-start | bytes 983048 | tf_op jit(solution)/shard_map/ppermute | solution.py:491
  40.2 17.1 %copy-start.17 = (s32[1280]{0:T(1024)}, s32[1280]{0:T(1024)S(1)}, u32[]{:S(2)}) copy-start(s32[1280]{0:T(1024)S(1)} %reshape.872) | copy-start | bytes 15364
  43.0 18.0 %collective-permute-start.8 = (bf16[8,2,2,80,128]{4,3,2,1,0:T(8,128)(2,1)S(1)}, bf16[8,2,2,80,128]{4,3,2,1,0:T(8,128)(2,1)S(1)}, u32[]{:S(2)}, u32[]{:S(2)}) collective-permute-start(bf16[8,2,2,80,128]{4,3,2,1,0:T(8,128)(2,1)S(1)} %fusion.1), channel_id=1, source_target_pairs={{0,2},{1,3},{2,0},{3,1},{4,6},{5,7},{6,4},{7,5},{8,10},{9,11},{10,... | collective-permute-start | bytes 1966088 | tf_op jit(solution)/shard_map/ppermute | solution.py:491
  58.5 11.5 %collective-permute-start.5 = (bf16[8,2,2,80,128]{4,3,2,1,0:T(8,128)(2,1)}, bf16[8,2,2,80,128]{4,3,2,1,0:T(8,128)(2,1)}, u32[]{:S(2)}, u32[]{:S(2)}) collective-permute-start(bf16[8,2,2,80,128]{4,3,2,1,0:T(8,128)(2,1)} %get-tuple-element.318), channel_id=1, source_target_pairs={{0,1},{1,0},{2,3},{3,2},{4,5},{5,4},{6,7},{7,6},{8,9},{9,8},{10,11... | collective-permute-start | bytes 1966088 | tf_op jit(solution)/shard_map/ppermute | solution.py:491
  61.0 11.4 %collective-permute-start.11 = (bf16[8,2,80,128]{3,2,1,0:T(8,128)(2,1)}, bf16[8,2,80,128]{3,2,1,0:T(8,128)(2,1)}, u32[]{:S(2)}, u32[]{:S(2)}) collective-permute-start(bf16[8,2,80,128]{3,2,1,0:T(8,128)(2,1)} %get-tuple-element.332), channel_id=1, source_target_pairs={{0,1},{1,0},{2,3},{3,2},{4,5},{5,4},{6,7},{7,6},{8,9},{9,8},{10,11... | collective-permute-start | bytes 983048 | tf_op jit(solution)/shard_map/ppermute | solution.py:491
  61.0 6.7 %collective-permute-start.3 = (bf16[128,1280]{1,0:T(8,128)(2,1)}, bf16[128,1280]{1,0:T(8,128)(2,1)}, u32[]{:S(2)}, u32[]{:S(2)}) collective-permute-start(bf16[128,1280]{1,0:T(8,128)(2,1)} %get-tuple-element.334), channel_id=1, source_target_pairs={{0,1},{1,0},{2,3},{3,2},{4,5},{5,4},{6,7},{7,6},{8,9},{9,8},{10,11... | collective-permute-start | bytes 983048 | tf_op jit(solution)/shard_map/ppermute | solution.py:491
  63.5 11.9 %copy-start.7 = (bf16[2,8,2,80,128]{4,3,2,1,0:T(8,128)(2,1)S(1)}, bf16[2,8,2,80,128]{4,3,2,1,0:T(8,128)(2,1)}, u32[]{:S(2)}) copy-start(bf16[2,8,2,80,128]{4,3,2,1,0:T(8,128)(2,1)} %copy-done.5) | copy-start | bytes 1966084
  65.4 10.0 %collective-permute-start.12 = (bf16[8,2,80,128]{3,2,1,0:T(8,128)(2,1)}, bf16[8,2,80,128]{3,2,1,0:T(8,128)(2,1)}, u32[]{:S(2)}, u32[]{:S(2)}) collective-permute-start(bf16[8,2,80,128]{3,2,1,0:T(8,128)(2,1)} %fusion.10), channel_id=1, source_target_pairs={{0,2},{1,3},{2,0},{3,1},{4,6},{5,7},{6,4},{7,5},{8,10},{9,11},{10,... | collective-permute-start | bytes 983048 | tf_op jit(solution)/shard_map/ppermute | solution.py:491
  67.2 29.7 %collective-permute-start.4 = (bf16[8,2,2,80,128]{4,3,2,1,0:T(8,128)(2,1)}, bf16[8,2,2,80,128]{4,3,2,1,0:T(8,128)(2,1)}, u32[]{:S(2)}, u32[]{:S(2)}) collective-permute-start(bf16[8,2,2,80,128]{4,3,2,1,0:T(8,128)(2,1)} %get-tuple-element.319), channel_id=1, source_target_pairs={{0,1},{1,0},{2,3},{3,2},{4,5},{5,4},{6,7},{7,6},{8,9},{9,8},{10,11... | collective-permute-start | bytes 1966088 | tf_op jit(solution)/shard_map/ppermute | solution.py:491
  67.7 12.0 %copy-start.18 = (s32[1280]{0:T(1024)S(1)}, s32[1280]{0:T(1024)}, u32[]{:S(2)}) copy-start(s32[1280]{0:T(1024)} %copy-done.17) | copy-start | bytes 15364
  67.7 12.0 %copy-start.35 = (s32[10]{0:T(128)S(1)}, s32[10]{0:T(128)}, u32[]{:S(2)}) copy-start(s32[10]{0:T(128)} %iota_multiply_fusion.1) | copy-start | bytes 124
  67.7 27.0 %collective-permute-start.10 = (bf16[4,2,2,80,128]{4,3,2,1,0:T(8,128)(2,1)}, bf16[4,2,2,80,128]{4,3,2,1,0:T(8,128)(2,1)S(1)}, u32[]{:S(2)}, u32[]{:S(2)}) collective-permute-start(bf16[4,2,2,80,128]{4,3,2,1,0:T(8,128)(2,1)} %get-tuple-element.313), channel_id=1, source_target_pairs={{0,16},{4,20},{8,24},{12,28},{16,0},{20,4},{24,8},{28,12},{1,17},{... | collective-permute-start | bytes 983048 | tf_op jit(solution)/shard_map/ppermute | solution.py:491
  72.1 24.8 %collective-permute-start.9 = (bf16[8,2,2,80,128]{4,3,2,1,0:T(8,128)(2,1)}, bf16[8,2,2,80,128]{4,3,2,1,0:T(8,128)(2,1)}, u32[]{:S(2)}, u32[]{:S(2)}) collective-permute-start(bf16[8,2,2,80,128]{4,3,2,1,0:T(8,128)(2,1)} %fusion), channel_id=1, source_target_pairs={{0,2},{1,3},{2,0},{3,1},{4,6},{5,7},{6,4},{7,5},{8,10},{9,11},{10,... | collective-permute-start | bytes 1966088 | tf_op jit(solution)/shard_map/ppermute | solution.py:491
  77.4 21.7 %collective-permute-start.14 = (bf16[4,2,80,128]{3,2,1,0:T(8,128)(2,1)}, bf16[4,2,80,128]{3,2,1,0:T(8,128)(2,1)S(1)}, u32[]{:S(2)}, u32[]{:S(2)}) collective-permute-start(bf16[4,2,80,128]{3,2,1,0:T(8,128)(2,1)} %get-tuple-element.315), channel_id=1, source_target_pairs={{0,16},{4,20},{8,24},{12,28},{16,0},{20,4},{24,8},{28,12},{1,17},{... | collective-permute-start | bytes 491528 | tf_op jit(solution)/shard_map/ppermute | solution.py:491
  94.7 13.9 %copy-start.9 = (bf16[4,2,2,80,128]{4,3,2,1,0:T(8,128)(2,1)}, bf16[4,2,2,80,128]{4,3,2,1,0:T(8,128)(2,1)S(1)}, u32[]{:S(2)}) copy-start(bf16[4,2,2,80,128]{4,3,2,1,0:T(8,128)(2,1)S(1)} %collective-permute-done.10.refs_2_) | copy-start | bytes 983044
  95.6 12.1 %collective-permute-start.16 = (bf16[4,2,2,80,128]{4,3,2,1,0:T(8,128)(2,1)}, bf16[4,2,2,80,128]{4,3,2,1,0:T(8,128)(2,1)}, u32[]{:S(2)}, u32[]{:S(2)}) collective-permute-start(bf16[4,2,2,80,128]{4,3,2,1,0:T(8,128)(2,1)} %pad_maximum_fusion.4), channel_id=1, source_target_pairs={{0,8},{4,12},{8,0},{12,4},{16,24},{20,28},{24,16},{28,20},{1,9},{5... | collective-permute-start | bytes 983048 | tf_op jit(solution)/shard_map/ppermute | solution.py:491
  103.7 21.5 %collective-permute-start.21 = (bf16[2,192,1280]{2,1,0:T(8,128)(2,1)}, bf16[2,192,1280]{2,1,0:T(8,128)(2,1)}, u32[]{:S(2)}, u32[]{:S(2)}) collective-permute-start(bf16[2,192,1280]{2,1,0:T(8,128)(2,1)} %pad_maximum_fusion), channel_id=1, source_target_pairs={{0,2},{1,3},{2,0},{3,1},{4,6},{5,7},{6,4},{7,5},{8,10},{9,11},{10,... | collective-permute-start | bytes 2949128 | tf_op jit(solution)/shard_map/ppermute | solution.py:491
  107.3 6.0 %collective-permute-start.15 = (bf16[4,2,80,128]{3,2,1,0:T(8,128)(2,1)}, bf16[4,2,80,128]{3,2,1,0:T(8,128)(2,1)S(1)}, u32[]{:S(2)}, u32[]{:S(2)}) collective-permute-start(bf16[4,2,80,128]{3,2,1,0:T(8,128)(2,1)} %pad_maximum_fusion.12), channel_id=1, source_target_pairs={{0,8},{4,12},{8,0},{12,4},{16,24},{20,28},{24,16},{28,20},{1,9},{5... | collective-permute-start | bytes 491528 | tf_op jit(solution)/shard_map/ppermute | solution.py:491
  107.6 16.0 %collective-permute-start.13 = (bf16[4,2,2,80,128]{4,3,2,1,0:T(8,128)(2,1)S(1)}, bf16[4,2,2,80,128]{4,3,2,1,0:T(8,128)(2,1)S(1)}, u32[]{:S(2)}, u32[]{:S(2)}) collective-permute-start(bf16[4,2,2,80,128]{4,3,2,1,0:T(8,128)(2,1)S(1)} %copy-done.15), channel_id=1, source_target_pairs={{0,16},{4,20},{8,24},{12,28},{16,0},{20,4},{24,8},{28,12},{1,17},{... | collective-permute-start | bytes 983048 | tf_op jit(solution)/shard_map/ppermute | solution.py:491
  108.7 15.0 %collective-permute-start.18 = (bf16[4,2,2,80,128]{4,3,2,1,0:T(8,128)(2,1)S(1)}, bf16[4,2,2,80,128]{4,3,2,1,0:T(8,128)(2,1)S(1)}, u32[]{:S(2)}, u32[]{:S(2)}) collective-permute-start(bf16[4,2,2,80,128]{4,3,2,1,0:T(8,128)(2,1)S(1)} %pad_maximum_fusion.5), channel_id=1, source_target_pairs={{0,4},{4,0},{8,12},{12,8},{16,20},{20,16},{24,28},{28,24},{1,5},{5... | collective-permute-start | bytes 983048 | tf_op jit(solution)/shard_map/ppermute | solution.py:491
  110.0 36.3 %collective-permute-start.20 = (bf16[192,1280]{1,0:T(8,128)(2,1)}, bf16[192,1280]{1,0:T(8,128)(2,1)S(1)}, u32[]{:S(2)}, u32[]{:S(2)}) collective-permute-start(bf16[192,1280]{1,0:T(8,128)(2,1)} %get-tuple-element.304), channel_id=1, source_target_pairs={{0,1},{1,0},{2,3},{3,2},{4,5},{5,4},{6,7},{7,6},{8,9},{9,8},{10,11... | collective-permute-start | bytes 1474568 | tf_op jit(solution)/shard_map/ppermute | solution.py:491
  113.4 32.2 %collective-permute-start.24 = (bf16[4,2,80,128]{3,2,1,0:T(8,128)(2,1)S(1)}, bf16[4,2,80,128]{3,2,1,0:T(8,128)(2,1)S(1)}, u32[]{:S(2)}, u32[]{:S(2)}) collective-permute-start(bf16[4,2,80,128]{3,2,1,0:T(8,128)(2,1)S(1)} %pad_maximum_fusion.13), channel_id=1, source_target_pairs={{0,4},{4,0},{8,12},{12,8},{16,20},{20,16},{24,28},{28,24},{1,5},{5... | collective-permute-start | bytes 491528 | tf_op jit(solution)/shard_map/ppermute | solution.py:491
  123.6 5.9 %copy-start.8 = (bf16[128,1280]{1,0:T(8,128)(2,1)S(1)}, bf16[128,1280]{1,0:T(8,128)(2,1)}, u32[]{:S(2)}) copy-start(bf16[128,1280]{1,0:T(8,128)(2,1)} %get-tuple-element.196.refs_14_) | copy-start | bytes 983044
  123.6 5.9 %copy-start.10 = (bf16[4,2,2,80,128]{4,3,2,1,0:T(8,128)(2,1)S(1)}, bf16[4,2,2,80,128]{4,3,2,1,0:T(8,128)(2,1)}, u32[]{:S(2)}) copy-start(bf16[4,2,2,80,128]{4,3,2,1,0:T(8,128)(2,1)} %copy-done.9) | copy-start | bytes 983044
  123.6 5.9 %copy-start.11 = (bf16[128,128]{1,0:T(8,128)(2,1)S(1)}, bf16[128,128]{1,0:T(8,128)(2,1)}, u32[]{:S(2)}) copy-start(bf16[128,128]{1,0:T(8,128)(2,1)} %fusion.36.refs_6_) | copy-start | bytes 98308
  123.6 20.6 %collective-permute-start.17 = (bf16[4,2,2,80,128]{4,3,2,1,0:T(8,128)(2,1)S(1)}, bf16[4,2,2,80,128]{4,3,2,1,0:T(8,128)(2,1)S(1)}, u32[]{:S(2)}, u32[]{:S(2)}) collective-permute-start(bf16[4,2,2,80,128]{4,3,2,1,0:T(8,128)(2,1)S(1)} %pad_maximum_fusion.6), channel_id=1, source_target_pairs={{0,8},{4,12},{8,0},{12,4},{16,24},{20,28},{24,16},{28,20},{1,9},{5... | collective-permute-start | bytes 983048 | tf_op jit(solution)/shard_map/ppermute | solution.py:491
  126.4 19.8 %collective-permute-start.22 = (bf16[192,1280]{1,0:T(8,128)(2,1)S(1)}, bf16[192,1280]{1,0:T(8,128)(2,1)S(1)}, u32[]{:S(2)}, u32[]{:S(2)}) collective-permute-start(bf16[192,1280]{1,0:T(8,128)(2,1)S(1)} %get-tuple-element.320), channel_id=1, source_target_pairs={{0,1},{1,0},{2,3},{3,2},{4,5},{5,4},{6,7},{7,6},{8,9},{9,8},{10,11... | collective-permute-start | bytes 1474568 | tf_op jit(solution)/shard_map/ppermute | solution.py:491
  143.0 19.5 %collective-permute-start.23 = (bf16[4,2,2,80,128]{4,3,2,1,0:T(8,128)(2,1)S(1)}, bf16[4,2,2,80,128]{4,3,2,1,0:T(8,128)(2,1)S(1)}, u32[]{:S(2)}, u32[]{:S(2)}) collective-permute-start(bf16[4,2,2,80,128]{4,3,2,1,0:T(8,128)(2,1)S(1)} %get-tuple-element.198), channel_id=1, source_target_pairs={{0,4},{4,0},{8,12},{12,8},{16,20},{20,16},{24,28},{28,24},{1,5},{5... | collective-permute-start | bytes 983048 | tf_op jit(solution)/shard_map/ppermute | solution.py:491
  144.3 16.0 %collective-permute-start.30 = (bf16[2,128,1280]{2,1,0:T(8,128)(2,1)S(1)}, bf16[2,128,1280]{2,1,0:T(8,128)(2,1)S(1)}, u32[]{:S(2)}, u32[]{:S(2)}) collective-permute-start(bf16[2,128,1280]{2,1,0:T(8,128)(2,1)S(1)} %get-tuple-element.218), channel_id=1, source_target_pairs={{0,2},{1,3},{2,0},{3,1},{4,6},{5,7},{6,4},{7,5},{8,10},{9,11},{10,... | collective-permute-start | bytes 1966088 | tf_op jit(solution)/shard_map/ppermute | solution.py:491
  145.6 23.5 %collective-permute-start.29 = (bf16[128,1280]{1,0:T(8,128)(2,1)S(1)}, bf16[128,1280]{1,0:T(8,128)(2,1)S(1)}, u32[]{:S(2)}, u32[]{:S(2)}) collective-permute-start(bf16[128,1280]{1,0:T(8,128)(2,1)S(1)} %get-tuple-element.217), channel_id=1, source_target_pairs={{0,1},{1,0},{2,3},{3,2},{4,5},{5,4},{6,7},{7,6},{8,9},{9,8},{10,11... | collective-permute-start | bytes 983048 | tf_op jit(solution)/shard_map/ppermute | solution.py:491
  156.3 11.0 %collective-permute-start.27 = (bf16[2,64,1280]{2,1,0:T(8,128)(2,1)S(1)}, bf16[2,64,1280]{2,1,0:T(8,128)(2,1)S(1)}, u32[]{:S(2)}, u32[]{:S(2)}) collective-permute-start(bf16[2,64,1280]{2,1,0:T(8,128)(2,1)S(1)} %get-tuple-element.216), channel_id=1, source_target_pairs={{0,2},{1,3},{2,0},{3,1},{4,6},{5,7},{6,4},{7,5},{8,10},{9,11},{10,... | collective-permute-start | bytes 983048 | tf_op jit(solution)/shard_map/ppermute | solution.py:491
  160.3 9.1 %collective-permute-start.31 = (bf16[128,1280]{1,0:T(8,128)(2,1)S(1)}, bf16[128,1280]{1,0:T(8,128)(2,1)S(1)}, u32[]{:S(2)}, u32[]{:S(2)}) collective-permute-start(bf16[128,1280]{1,0:T(8,128)(2,1)S(1)} %get-tuple-element.328), channel_id=1, source_target_pairs={{0,1},{1,0},{2,3},{3,2},{4,5},{5,4},{6,7},{7,6},{8,9},{9,8},{10,11... | collective-permute-start | bytes 983048 | tf_op jit(solution)/shard_map/ppermute | solution.py:491
  162.3 5.8 %collective-permute-start.32 = (bf16[4,2,80,128]{3,2,1,0:T(8,128)(2,1)S(1)}, bf16[4,2,80,128]{3,2,1,0:T(8,128)(2,1)S(1)}, u32[]{:S(2)}, u32[]{:S(2)}) collective-permute-start(bf16[4,2,80,128]{3,2,1,0:T(8,128)(2,1)S(1)} %get-tuple-element.212), channel_id=1, source_target_pairs={{0,4},{4,0},{8,12},{12,8},{16,20},{20,16},{24,28},{28,24},{1,5},{5... | collective-permute-start | bytes 491528 | tf_op jit(solution)/shard_map/ppermute | solution.py:491
  162.5 10.1 %collective-permute-start.26 = (bf16[64,1280]{1,0:T(8,128)(2,1)S(1)}, bf16[64,1280]{1,0:T(8,128)(2,1)S(1)}, u32[]{:S(2)}, u32[]{:S(2)}) collective-permute-start(bf16[64,1280]{1,0:T(8,128)(2,1)S(1)} %get-tuple-element.215), channel_id=1, source_target_pairs={{0,1},{1,0},{2,3},{3,2},{4,5},{5,4},{6,7},{7,6},{8,9},{9,8},{10,11... | collective-permute-start | bytes 491528 | tf_op jit(solution)/shard_map/ppermute | solution.py:491
  167.3 8.1 %collective-permute-start.25 = (bf16[4,2,2,80,128]{4,3,2,1,0:T(8,128)(2,1)S(1)}, bf16[4,2,2,80,128]{4,3,2,1,0:T(8,128)(2,1)S(1)}, u32[]{:S(2)}, u32[]{:S(2)}) collective-permute-start(bf16[4,2,2,80,128]{4,3,2,1,0:T(8,128)(2,1)S(1)} %pad_maximum_fusion.8), channel_id=1, source_target_pairs={{0,8},{4,12},{8,0},{12,4},{16,24},{20,28},{24,16},{28,20},{1,9},{5... | collective-permute-start | bytes 983048 | tf_op jit(solution)/shard_map/ppermute | solution.py:491
  168.0 4.6 %collective-permute-start.28 = (bf16[64,1280]{1,0:T(8,128)(2,1)S(1)}, bf16[64,1280]{1,0:T(8,128)(2,1)S(1)}, u32[]{:S(2)}, u32[]{:S(2)}) collective-permute-start(bf16[64,1280]{1,0:T(8,128)(2,1)S(1)} %get-tuple-element.340), channel_id=1, source_target_pairs={{0,1},{1,0},{2,3},{3,2},{4,5},{5,4},{6,7},{7,6},{8,9},{9,8},{10,11... | collective-permute-start | bytes 491528 | tf_op jit(solution)/shard_map/ppermute | solution.py:491
  169.1 9.5 %copy-start.12 = (s32[4]{0:T(128)}, s32[4]{0:T(128)S(1)}, u32[]{:S(2)}) copy-start(s32[4]{0:T(128)S(1)} %pad_add_fusion.1.refs_0_.place) | copy-start | bytes 52
  169.1 9.4 %collective-permute-start.19 = (bf16[4,2,2,80,128]{4,3,2,1,0:T(8,128)(2,1)S(1)}, bf16[4,2,2,80,128]{4,3,2,1,0:T(8,128)(2,1)S(1)}, u32[]{:S(2)}, u32[]{:S(2)}) collective-permute-start(bf16[4,2,2,80,128]{4,3,2,1,0:T(8,128)(2,1)S(1)} %pad_maximum_fusion.7), channel_id=1, source_target_pairs={{0,4},{4,0},{8,12},{12,8},{16,20},{20,16},{24,28},{28,24},{1,5},{5... | collective-permute-start | bytes 983048 | tf_op jit(solution)/shard_map/ppermute | solution.py:491
  169.4 24.1 %collective-permute-start.34 = (bf16[4,2,80,128]{3,2,1,0:T(8,128)(2,1)S(1)}, bf16[4,2,80,128]{3,2,1,0:T(8,128)(2,1)S(1)}, u32[]{:S(2)}, u32[]{:S(2)}) collective-permute-start(bf16[4,2,80,128]{3,2,1,0:T(8,128)(2,1)S(1)} %pad_maximum_fusion.14), channel_id=1, source_target_pairs={{0,8},{4,12},{8,0},{12,4},{16,24},{20,28},{24,16},{28,20},{1,9},{5... | collective-permute-start | bytes 491528 | tf_op jit(solution)/shard_map/ppermute | solution.py:491
  175.5 17.9 %collective-permute-start.35 = (bf16[4,2,2,80,128]{4,3,2,1,0:T(8,128)(2,1)S(1)}, bf16[4,2,2,80,128]{4,3,2,1,0:T(8,128)(2,1)S(1)}, u32[]{:S(2)}, u32[]{:S(2)}) collective-permute-start(bf16[4,2,2,80,128]{4,3,2,1,0:T(8,128)(2,1)S(1)} %pad_maximum_fusion.9), channel_id=1, source_target_pairs={{0,16},{4,20},{8,24},{12,28},{16,0},{20,4},{24,8},{28,12},{1,17},{... | collective-permute-start | bytes 983048 | tf_op jit(solution)/shard_map/ppermute | solution.py:491
  193.1 8.2 %collective-permute-start.33 = (bf16[4,2,2,80,128]{4,3,2,1,0:T(8,128)(2,1)S(1)}, bf16[4,2,2,80,128]{4,3,2,1,0:T(8,128)(2,1)S(1)}, u32[]{:S(2)}, u32[]{:S(2)}) collective-permute-start(bf16[4,2,2,80,128]{4,3,2,1,0:T(8,128)(2,1)S(1)} %get-tuple-element.243), channel_id=1, source_target_pairs={{0,4},{4,0},{8,12},{12,8},{16,20},{20,16},{24,28},{28,24},{1,5},{5... | collective-permute-start | bytes 983048 | tf_op jit(solution)/shard_map/ppermute | solution.py:491
  193.6 9.5 %collective-permute-start.37 = (bf16[4,2,80,128]{3,2,1,0:T(8,128)(2,1)S(1)}, bf16[4,2,80,128]{3,2,1,0:T(8,128)(2,1)S(1)}, u32[]{:S(2)}, u32[]{:S(2)}) collective-permute-start(bf16[4,2,80,128]{3,2,1,0:T(8,128)(2,1)S(1)} %pad_maximum_fusion.15), channel_id=1, source_target_pairs={{0,16},{4,20},{8,24},{12,28},{16,0},{20,4},{24,8},{28,12},{1,17},{... | collective-permute-start | bytes 491528 | tf_op jit(solution)/shard_map/ppermute | solution.py:491
  193.7 12.4 %collective-permute-start.40 = (bf16[8,2,2,80,128]{4,3,2,1,0:T(8,128)(2,1)S(1)}, bf16[8,2,2,80,128]{4,3,2,1,0:T(8,128)(2,1)S(1)}, u32[]{:S(2)}, u32[]{:S(2)}) collective-permute-start(bf16[8,2,2,80,128]{4,3,2,1,0:T(8,128)(2,1)S(1)} %constant_dynamic-update-slice_fusion.8.refs_1_), channel_id=1, source_target_pairs={{0,2},{1,3},{2,0},{3,1},{4,6},{5,7},{6,4},{7,5},{8,10},{9,11},{10,... | collective-permute-start | bytes 1966088 | tf_op jit(solution)/shard_map/ppermute | solution.py:491
  194.9 19.7 %collective-permute-start.39 = (bf16[8,2,2,80,128]{4,3,2,1,0:T(8,128)(2,1)S(1)}, bf16[8,2,2,80,128]{4,3,2,1,0:T(8,128)(2,1)S(1)}, u32[]{:S(2)}, u32[]{:S(2)}) collective-permute-start(bf16[8,2,2,80,128]{4,3,2,1,0:T(8,128)(2,1)S(1)} %constant_dynamic-update-slice_fusion.8.refs_1_), channel_id=1, source_target_pairs={{0,1},{1,0},{2,3},{3,2},{4,5},{5,4},{6,7},{7,6},{8,9},{9,8},{10,11... | collective-permute-start | bytes 1966088 | tf_op jit(solution)/shard_map/ppermute | solution.py:491
  201.4 10.8 %collective-permute-start.36 = (bf16[4,2,2,80,128]{4,3,2,1,0:T(8,128)(2,1)S(1)}, bf16[4,2,2,80,128]{4,3,2,1,0:T(8,128)(2,1)S(1)}, u32[]{:S(2)}, u32[]{:S(2)}) collective-permute-start(bf16[4,2,2,80,128]{4,3,2,1,0:T(8,128)(2,1)S(1)} %pad_maximum_fusion.10), channel_id=1, source_target_pairs={{0,8},{4,12},{8,0},{12,4},{16,24},{20,28},{24,16},{28,20},{1,9},{5... | collective-permute-start | bytes 983048 | tf_op jit(solution)/shard_map/ppermute | solution.py:491
  206.1 8.5 %collective-permute-start.41 = (bf16[8,2,2,80,128]{4,3,2,1,0:T(8,128)(2,1)S(1)}, bf16[8,2,2,80,128]{4,3,2,1,0:T(8,128)(2,1)S(1)}, u32[]{:S(2)}, u32[]{:S(2)}) collective-permute-start(bf16[8,2,2,80,128]{4,3,2,1,0:T(8,128)(2,1)S(1)} %collective-permute-done.40.refs_3_), channel_id=1, source_target_pairs={{0,1},{1,0},{2,3},{3,2},{4,5},{5,4},{6,7},{7,6},{8,9},{9,8},{10,11... | collective-permute-start | bytes 1966088 | tf_op jit(solution)/shard_map/ppermute | solution.py:491
  210.9 20.5 %collective-permute-start.49 = (bf16[8,2,80,128]{3,2,1,0:T(8,128)(2,1)S(1)}, bf16[8,2,80,128]{3,2,1,0:T(8,128)(2,1)S(1)}, u32[]{:S(2)}, u32[]{:S(2)}) collective-permute-start(bf16[8,2,80,128]{3,2,1,0:T(8,128)(2,1)S(1)} %constant_dynamic-update-slice_fusion.9.refs_1_), channel_id=1, source_target_pairs={{0,2},{1,3},{2,0},{3,1},{4,6},{5,7},{6,4},{7,5},{8,10},{9,11},{10,... | collective-permute-start | bytes 983048 | tf_op jit(solution)/shard_map/ppermute | solution.py:491
  212.3 17.9 %collective-permute-start.38 = (bf16[4,2,2,80,128]{4,3,2,1,0:T(8,128)(2,1)S(1)}, bf16[4,2,2,80,128]{4,3,2,1,0:T(8,128)(2,1)S(1)}, u32[]{:S(2)}, u32[]{:S(2)}) collective-permute-start(bf16[4,2,2,80,128]{4,3,2,1,0:T(8,128)(2,1)S(1)} %pad_maximum_fusion.11), channel_id=1, source_target_pairs={{0,16},{4,20},{8,24},{12,28},{16,0},{20,4},{24,8},{28,12},{1,17},{... | collective-permute-start | bytes 983048 | tf_op jit(solution)/shard_map/ppermute | solution.py:491
  230.3 15.8 %collective-permute-start.46 = (bf16[8,2,2,80,128]{4,3,2,1,0:T(8,128)(2,1)S(1)}, bf16[8,2,2,80,128]{4,3,2,1,0:T(8,128)(2,1)S(1)}, u32[]{:S(2)}, u32[]{:S(2)}) collective-permute-start(bf16[8,2,2,80,128]{4,3,2,1,0:T(8,128)(2,1)S(1)} %constant_dynamic-update-slice_fusion.14.refs_1_), channel_id=1, source_target_pairs={{0,2},{1,3},{2,0},{3,1},{4,6},{5,7},{6,4},{7,5},{8,10},{9,11},{10,... | collective-permute-start | bytes 1966088 | tf_op jit(solution)/shard_map/ppermute | solution.py:491
  230.6 3.2 %collective-permute-start.48 = (bf16[8,2,80,128]{3,2,1,0:T(8,128)(2,1)S(1)}, bf16[8,2,80,128]{3,2,1,0:T(8,128)(2,1)S(1)}, u32[]{:S(2)}, u32[]{:S(2)}) collective-permute-start(bf16[8,2,80,128]{3,2,1,0:T(8,128)(2,1)S(1)} %constant_dynamic-update-slice_fusion.9.refs_1_), channel_id=1, source_target_pairs={{0,1},{1,0},{2,3},{3,2},{4,5},{5,4},{6,7},{7,6},{8,9},{9,8},{10,11... | collective-permute-start | bytes 983048 | tf_op jit(solution)/shard_map/ppermute | solution.py:491
  231.4 2.4 collective-permute-start.50
  231.4 28.7 %collective-permute-start.43 = (bf16[2,128,1280]{2,1,0:T(8,128)(2,1)S(1)}, bf16[2,128,1280]{2,1,0:T(8,128)(2,1)S(1)}, u32[]{:S(2)}, u32[]{:S(2)}) collective-permute-start(bf16[2,128,1280]{2,1,0:T(8,128)(2,1)S(1)} %copy-done.37), channel_id=1, source_target_pairs={{0,2},{1,3},{2,0},{3,1},{4,6},{5,7},{6,4},{7,5},{8,10},{9,11},{10,... | collective-permute-start | bytes 1966088 | tf_op jit(solution)/shard_map/ppermute | solution.py:491
  233.0 28.6 %collective-permute-start.45 = (bf16[8,2,2,80,128]{4,3,2,1,0:T(8,128)(2,1)S(1)}, bf16[8,2,2,80,128]{4,3,2,1,0:T(8,128)(2,1)S(1)}, u32[]{:S(2)}, u32[]{:S(2)}) collective-permute-start(bf16[8,2,2,80,128]{4,3,2,1,0:T(8,128)(2,1)S(1)} %constant_dynamic-update-slice_fusion.14.refs_1_), channel_id=1, source_target_pairs={{0,1},{1,0},{2,3},{3,2},{4,5},{5,4},{6,7},{7,6},{8,9},{9,8},{10,11... | collective-permute-start | bytes 1966088 | tf_op jit(solution)/shard_map/ppermute | solution.py:491
  233.8 43.9 %collective-permute-start.42 = (bf16[128,1280]{1,0:T(8,128)(2,1)S(1)}, bf16[128,1280]{1,0:T(8,128)(2,1)S(1)}, u32[]{:S(2)}, u32[]{:S(2)}) collective-permute-start(bf16[128,1280]{1,0:T(8,128)(2,1)S(1)} %get-tuple-element.268), channel_id=1, source_target_pairs={{0,1},{1,0},{2,3},{3,2},{4,5},{5,4},{6,7},{7,6},{8,9},{9,8},{10,11... | collective-permute-start | bytes 983048 | tf_op jit(solution)/shard_map/ppermute | solution.py:491
  246.1 15.6 %collective-permute-start.47 = (bf16[8,2,2,80,128]{4,3,2,1,0:T(8,128)(2,1)S(1)}, bf16[8,2,2,80,128]{4,3,2,1,0:T(8,128)(2,1)S(1)}, u32[]{:S(2)}, u32[]{:S(2)}) collective-permute-start(bf16[8,2,2,80,128]{4,3,2,1,0:T(8,128)(2,1)S(1)} %collective-permute-done.46.refs_3_), channel_id=1, source_target_pairs={{0,1},{1,0},{2,3},{3,2},{4,5},{5,4},{6,7},{7,6},{8,9},{9,8},{10,11... | collective-permute-start | bytes 1966088 | tf_op jit(solution)/shard_map/ppermute | solution.py:491
  260.2 17.6 %copy-start.13 = (s32[4]{0:T(128)S(1)}, s32[4]{0:T(128)}, u32[]{:S(2)}) copy-start(s32[4]{0:T(128)} %copy-done.12) | copy-start | bytes 52
  260.2 17.6 %collective-permute-start.44 = (bf16[128,1280]{1,0:T(8,128)(2,1)S(1)}, bf16[128,1280]{1,0:T(8,128)(2,1)S(1)}, u32[]{:S(2)}, u32[]{:S(2)}) collective-permute-start(bf16[128,1280]{1,0:T(8,128)(2,1)S(1)} %get-tuple-element.326), channel_id=1, source_target_pairs={{0,1},{1,0},{2,3},{3,2},{4,5},{5,4},{6,7},{7,6},{8,9},{9,8},{10,11... | collective-permute-start | bytes 983048 | tf_op jit(solution)/shard_map/ppermute | solution.py:491
  (25 other events, 64.0 us)
